TPU v7x, 32 devices: a whole 2x2x4 slice. The times are simulated.
32 devices in a mesh: blk: 16 (over z, y, core), head: 2 (over x).
Axes of the slice: x: 2, y: 2, z: 4, core: 2. Of those that a mesh axis runs over, the one named last changes fastest.
Arguments:
- layer_input: bfloat16 [2, 2048, 2048], P(None, ('blk', 'head')), may hold values from -6 to 6
- attn_gain: bfloat16 [2048], P(('blk', 'head')), may hold values from 0.5 to 1.5
- query_weight: bfloat16 [2048, 2048], P(('blk', 'head')), may hold values from -0.125 to 0.125
- key_matrix: bfloat16 [2048, 512], P(('blk', 'head')), may hold values from -0.125 to 0.125
- value_matrix: bfloat16 [2048, 512], P(('blk', 'head')), may hold values from -0.125 to 0.125
- output_weight: bfloat16 [2048, 2048], P(('blk', 'head')), may hold values from -3 to 3
- ffn_gain: bfloat16 [2048], P(('blk', 'head')), may hold values from 0.5 to 1.5
- gate_weight: bfloat16 [2048, 8192], P(('blk', 'head')), may hold values from -0.125 to 0.125
- up_weight: bfloat16 [2048, 8192], P(('blk', 'head')), may hold values from -0.125 to 0.125
- down_weight: bfloat16 [2048, 8192], P(('blk', 'head')), may hold values from -0.0625 to 0.0625
- block_ids: int32 [2, 2048], replicated, may hold values from 0 to 15, never falling along the last dimension, each value on 1 to 256 neighbouring positions
- cotangent: bfloat16 [2, 2048, 2048], P(None, ('blk', 'head')), may hold values from -6 to 6
Outputs:
- layer_output: float32 [2, 2048, 2048], P(None, ('blk', 'head'))
- input_grad: float32 [2, 2048, 2048], P(None, ('blk', 'head'))
- grad_attn_gain: float32 [2048], P(('blk', 'head'))
- grad_query: float32 [2048, 2048], P(('blk', 'head'))
- grad_key: float32 [2048, 512], P(('blk', 'head'))
- grad_value: float32 [2048, 512], P(('blk', 'head'))
- grad_output: float32 [2048, 2048], P(('blk', 'head'))
- grad_ffn_gain: float32 [2048], P(('blk', 'head'))
- grad_gate: float32 [2048, 8192], P(('blk', 'head'))
- grad_up: float32 [2048, 8192], P(('blk', 'head'))
- grad_down: float32 [2048, 8192], P(('blk', 'head'))
Inputs may be any that keep to these rules, and one draw needn't show every extreme that they name: `block_ids`: along each sequence the ids start at 0 and never fall, every id of 0 to 15 is used, a block holds 1 to 256 tokens, and some block holds exactly 256.
All inputs are finite; a program needn't handle non-finite values.
Results may differ from a plain program's by a relative error of at most 0.023.
Values may be sent and summed in bfloat16 or wider, within the bound.
A program may use at most 576 MiB of HBM per device.

v0:
```python
import math

import jax
import jax.numpy as jnp
from jax import lax
from jax.sharding import PartitionSpec as P

QUERY_HEADS = 32
KEY_HEADS = 8
HEAD_DIM = 64


epsilon = 1e-05
rope_base = 500000.0


def rotation_tables(positions, head_size):
    half = head_size // 2
    freqs = rope_base ** (-jnp.arange(half, dtype=jnp.float32) * 2.0 / head_size)
    angles = positions.astype(jnp.float32)[:, None] * freqs[None, :]
    return (jnp.cos(angles), jnp.sin(angles))


def rotate(value_rows, cosine_table, sine_table, direction):
    count_of_rows = value_rows.shape[0]
    half = cosine_table.shape[1]
    shaped = value_rows.reshape(count_of_rows, -1, 2 * half)
    first = shaped[..., :half]
    second = shaped[..., half:]
    cos_wide = cosine_table[:, None, :]
    sin_wide = direction * sine_table[:, None, :]
    turned = jnp.concatenate(
        [first * cos_wide - second * sin_wide, second * cos_wide + first * sin_wide], axis=-1
    )
    return turned.reshape(count_of_rows, -1)


def in_blocks(advance, state_now, pieces):
    sequence_length = pieces[0].shape[1]
    span_rows = math.gcd(sequence_length, 512)
    block_count = sequence_length // span_rows

    def to_blocks(piece):
        shaped = piece.reshape(piece.shape[:1] + (block_count, span_rows) + piece.shape[2:])
        return jnp.moveaxis(shaped, 1, 0)

    stacked = tuple((to_blocks(piece) for piece in pieces))

    def one_step(state_in, element):
        counter, blocks_here = element
        return (advance(state_in, blocks_here, counter * span_rows), None)

    result, unused = lax.scan(
        one_step, state_now, (jnp.arange(block_count, dtype=jnp.int32), stacked)
    )
    return result


def norm_back(grad_normed, normed, norm_scale):
    return norm_scale * (
        grad_normed - normed * jnp.mean(grad_normed * normed, axis=-1, keepdims=True)
    )


def local(
    layer_input,
    attn_gain,
    query_weight,
    key_matrix,
    value_matrix,
    output_weight,
    ffn_gain,
    gate_weight,
    up_weight,
    down_weight,
    block_ids,
    cotangent,
):
    count_of_heads = lax.axis_size("head")
    shard_index = lax.axis_index("blk") * count_of_heads + lax.axis_index("head")
    sequence_batch, token_rows, model_width = layer_input.shape
    count_of_rows = sequence_batch * token_rows
    query_group_width = QUERY_HEADS // KEY_HEADS
    local_heads = QUERY_HEADS // count_of_heads
    resident_key_value = KEY_HEADS // count_of_heads
    pair_tokens = token_rows * count_of_heads
    score_scale = HEAD_DIM ** (-0.5)
    contract_last = (((1,), (1,)), ((), ()))
    contract_first = (((0,), (0,)), ((), ()))
    positions = jnp.tile(
        shard_index * token_rows + jnp.arange(token_rows, dtype=jnp.int32), sequence_batch
    )
    cosine_table, sine_table = rotation_tables(positions, HEAD_DIM)
    head_positions = jnp.tile(
        lax.axis_index("blk") * pair_tokens + jnp.arange(pair_tokens, dtype=jnp.int32),
        sequence_batch,
    )
    head_cosine, head_sine = rotation_tables(head_positions, HEAD_DIM)
    inputs_flat = layer_input.reshape(count_of_rows, model_width).astype(jnp.float32)
    norm_one = lax.rsqrt(jnp.mean(inputs_flat * inputs_flat, axis=-1, keepdims=True) + epsilon)
    normed_one = inputs_flat * norm_one
    gain_piece = lax.all_gather(attn_gain, ("blk", "head"), axis=0, tiled=True)
    query_piece = lax.all_gather(query_weight, ("blk", "head"), axis=0, tiled=True)
    key_piece = lax.all_gather(key_matrix, ("blk", "head"), axis=0, tiled=True)
    value_piece = lax.all_gather(value_matrix, ("blk", "head"), axis=0, tiled=True)
    span_rows = gain_piece.shape[0]
    gain_wide = gain_piece.astype(jnp.float32)
    columns = normed_one
    scaled = (columns * gain_wide).astype(jnp.bfloat16)
    gain_one = gain_wide
    normed_low_one = scaled
    query_raw = jnp.dot(scaled, query_piece, preferred_element_type=jnp.float32)
    key_raw = jnp.dot(scaled, key_piece, preferred_element_type=jnp.float32)
    value_unrotated = jnp.dot(scaled, value_piece, preferred_element_type=jnp.float32)
    queries_tok = (
        rotate(query_raw, cosine_table, sine_table, 1.0)
        .astype(jnp.bfloat16)
        .reshape(sequence_batch, token_rows, QUERY_HEADS * HEAD_DIM)
    )
    keys_tok = (
        rotate(key_raw, cosine_table, sine_table, 1.0)
        .astype(jnp.bfloat16)
        .reshape(sequence_batch, token_rows, KEY_HEADS * HEAD_DIM)
    )
    value_token_rows = value_unrotated.astype(jnp.bfloat16).reshape(
        sequence_batch, token_rows, KEY_HEADS * HEAD_DIM
    )
    queries_head, keys_head, values_head = (
        lax.all_to_all(queries_tok, "head", split_axis=2, concat_axis=1, tiled=True),
        lax.all_to_all(keys_tok, "head", split_axis=2, concat_axis=1, tiled=True),
        lax.all_to_all(value_token_rows, "head", split_axis=2, concat_axis=1, tiled=True),
    )
    query_ids = lax.dynamic_slice_in_dim(
        block_ids, lax.axis_index("blk") * pair_tokens, pair_tokens, 1
    )
    query_split = queries_head.reshape(
        sequence_batch, pair_tokens, resident_key_value, query_group_width, HEAD_DIM
    )
    key_own = keys_head.reshape(sequence_batch, pair_tokens, resident_key_value, HEAD_DIM)
    value_own = values_head.reshape(sequence_batch, pair_tokens, resident_key_value, HEAD_DIM)

    def attend(state_now, pieces, offset):
        running_max, running_sum, running_acc = state_now
        key_piece, value_piece = pieces
        span_rows = key_piece.shape[1]
        key_split = key_piece.reshape(sequence_batch, span_rows, resident_key_value, HEAD_DIM)
        value_split = value_piece.reshape(sequence_batch, span_rows, resident_key_value, HEAD_DIM)
        piece_ids = lax.dynamic_slice_in_dim(block_ids, offset, span_rows, 1)
        allowed = (piece_ids[:, None, :] <= query_ids[:, :, None])[:, :, None, None, :]
        scores = (
            jnp.einsum(
                "sqkgd,snkd->sqkgn", query_split, key_split, preferred_element_type=jnp.float32
            )
            * score_scale
        )
        masked = jnp.where(allowed, scores, -1e30)
        new_max = jnp.maximum(running_max, jnp.max(masked, axis=-1))
        weights = jnp.where(allowed, jnp.exp(masked - new_max[..., None]), 0.0)
        factor = jnp.exp(running_max - new_max)
        new_sum = running_sum * factor + jnp.sum(weights, axis=-1)
        new_acc = running_acc * factor[..., None] + jnp.einsum(
            "sqkgn,snkd->sqkgd",
            weights.astype(jnp.bfloat16),
            value_split,
            preferred_element_type=jnp.float32,
        )
        return (new_max, new_sum, new_acc)

    stat_shape = (sequence_batch, pair_tokens, resident_key_value, query_group_width)
    start_attend = (
        jnp.full(stat_shape, -1e30, jnp.float32),
        jnp.zeros(stat_shape, jnp.float32),
        jnp.zeros(stat_shape + (HEAD_DIM,), jnp.float32),
    )
    final_max, final_sum, final_acc = in_blocks(
        attend,
        start_attend,
        (
            lax.all_gather(keys_head, "blk", axis=1, tiled=True),
            lax.all_gather(values_head, "blk", axis=1, tiled=True),
        ),
    )
    log_total = final_max + jnp.log(final_sum)
    attended_split = (final_acc / final_sum[..., None]).astype(jnp.bfloat16)
    attended_head = attended_split.reshape(sequence_batch, pair_tokens, local_heads * HEAD_DIM)
    attended_tok = lax.all_to_all(attended_head, "head", split_axis=1, concat_axis=2, tiled=True)
    attended_flat = attended_tok.reshape(count_of_rows, QUERY_HEADS * HEAD_DIM)
    columns = attended_flat
    branch_attn = jnp.dot(
        columns,
        lax.all_gather(output_weight, ("blk", "head"), axis=0, tiled=True),
        preferred_element_type=jnp.float32,
    )
    middle = inputs_flat + branch_attn
    norm_two = lax.rsqrt(jnp.mean(middle * middle, axis=-1, keepdims=True) + epsilon)
    normed_two = middle * norm_two
    gain_piece = lax.all_gather(ffn_gain, ("blk", "head"), axis=0, tiled=True)
    gate_piece = lax.all_gather(gate_weight, ("blk", "head"), axis=0, tiled=True)
    up_piece = lax.all_gather(up_weight, ("blk", "head"), axis=0, tiled=True)
    span_rows = gain_piece.shape[0]
    gain_wide = gain_piece.astype(jnp.float32)
    columns = normed_two
    scaled = (columns * gain_wide).astype(jnp.bfloat16)
    gate = jnp.dot(scaled, gate_piece, preferred_element_type=jnp.float32)
    upper = jnp.dot(scaled, up_piece, preferred_element_type=jnp.float32)
    sigmoid_gate = jax.nn.sigmoid(gate)
    silu_gate = gate * sigmoid_gate
    active = (silu_gate * upper).astype(jnp.bfloat16)
    cotangent_flat = cotangent.reshape(count_of_rows, model_width)
    piece = lax.all_gather(down_weight, ("blk", "head"), axis=0, tiled=True)
    span_rows = piece.shape[0]
    produced = lax.dot_general(active, piece, contract_last, preferred_element_type=jnp.float32)
    active_grad = jnp.dot(cotangent_flat, piece, preferred_element_type=jnp.float32)
    layer_output = (middle + produced).reshape(sequence_batch, token_rows, model_width)
    gate_grad = (active_grad * upper * sigmoid_gate * (1.0 + gate * (1.0 - sigmoid_gate))).astype(
        jnp.bfloat16
    )
    up_grad = (active_grad * silu_gate).astype(jnp.bfloat16)
    gate_piece, up_piece = lax.all_gather(
        (gate_weight, up_weight), ("blk", "head"), axis=0, tiled=True
    )
    normed_two_grad = lax.dot_general(
        gate_grad, gate_piece, contract_last, preferred_element_type=jnp.float32
    ) + lax.dot_general(up_grad, up_piece, contract_last, preferred_element_type=jnp.float32)
    middle_grad = cotangent_flat.astype(jnp.float32) + norm_back(
        normed_two_grad * gain_wide, normed_two, norm_two
    )
    middle_low = middle_grad.astype(jnp.bfloat16)
    attended_grad = lax.dot_general(
        middle_low,
        lax.all_gather(output_weight, ("blk", "head"), axis=0, tiled=True),
        contract_last,
        preferred_element_type=jnp.float32,
    )
    attended_grad_tok = attended_grad.astype(jnp.bfloat16).reshape(
        sequence_batch, token_rows, QUERY_HEADS * HEAD_DIM
    )
    attended_grad_head = lax.all_to_all(
        attended_grad_tok, "head", split_axis=2, concat_axis=1, tiled=True
    )
    grad_split = attended_grad_head.reshape(
        sequence_batch, pair_tokens, resident_key_value, query_group_width, HEAD_DIM
    )
    delta_rows = jnp.sum(
        grad_split.astype(jnp.float32) * attended_split.astype(jnp.float32), axis=-1
    )

    def attend_back(state_now, pieces, offset):
        query_total, key_total, value_total = state_now
        key_piece, value_piece, query_piece, grad_piece, total_piece, delta_piece = pieces
        span_rows = key_piece.shape[1]
        key_split = key_piece.astype(jnp.bfloat16).reshape(
            sequence_batch, span_rows, resident_key_value, HEAD_DIM
        )
        value_split = value_piece.astype(jnp.bfloat16).reshape(
            sequence_batch, span_rows, resident_key_value, HEAD_DIM
        )
        query_remote = query_piece.astype(jnp.bfloat16).reshape(
            sequence_batch, span_rows, resident_key_value, query_group_width, HEAD_DIM
        )
        grad_remote = grad_piece.astype(jnp.bfloat16).reshape(
            sequence_batch, span_rows, resident_key_value, query_group_width, HEAD_DIM
        )
        piece_ids = lax.dynamic_slice_in_dim(block_ids, offset, span_rows, 1)
        allowed = (piece_ids[:, None, :] <= query_ids[:, :, None])[:, :, None, None, :]
        scores = (
            jnp.einsum(
                "sqkgd,snkd->sqkgn", query_split, key_split, preferred_element_type=jnp.float32
            )
            * score_scale
        )
        probs = jnp.where(allowed, jnp.exp(scores - log_total[..., None]), 0.0)
        prob_grad = jnp.einsum(
            "sqkgd,snkd->sqkgn", grad_split, value_split, preferred_element_type=jnp.float32
        )
        score_grad = (probs * (prob_grad - delta_rows[..., None])).astype(jnp.bfloat16)
        query_total = (
            query_total
            + jnp.einsum(
                "sqkgn,snkd->sqkgd", score_grad, key_split, preferred_element_type=jnp.float32
            )
            * score_scale
        )
        allowed_back = (query_ids[:, None, :] <= piece_ids[:, :, None])[:, :, None, None, :]
        scores_back = (
            jnp.einsum(
                "sqkgd,snkd->sqkgn", query_remote, key_own, preferred_element_type=jnp.float32
            )
            * score_scale
        )
        probs_back = jnp.where(allowed_back, jnp.exp(scores_back - total_piece[..., None]), 0.0)
        value_total = value_total + jnp.einsum(
            "sqkgn,sqkgd->snkd",
            probs_back.astype(jnp.bfloat16),
            grad_remote,
            preferred_element_type=jnp.float32,
        )
        prob_grad_back = jnp.einsum(
            "sqkgd,snkd->sqkgn", grad_remote, value_own, preferred_element_type=jnp.float32
        )
        score_grad_back = (probs_back * (prob_grad_back - delta_piece[..., None])).astype(
            jnp.bfloat16
        )
        key_total = (
            key_total
            + jnp.einsum(
                "sqkgn,sqkgd->snkd",
                score_grad_back,
                query_remote,
                preferred_element_type=jnp.float32,
            )
            * score_scale
        )
        return (query_total, key_total, value_total)

    start_back = (
        jnp.zeros(stat_shape + (HEAD_DIM,), jnp.float32),
        jnp.zeros((sequence_batch, pair_tokens, resident_key_value, HEAD_DIM), jnp.float32),
        jnp.zeros((sequence_batch, pair_tokens, resident_key_value, HEAD_DIM), jnp.float32),
    )
    query_total, key_total, value_total = in_blocks(
        attend_back,
        start_back,
        (
            lax.all_gather(keys_head.astype(jnp.float32), "blk", axis=1, tiled=True),
            lax.all_gather(values_head.astype(jnp.float32), "blk", axis=1, tiled=True),
            lax.all_gather(queries_head.astype(jnp.float32), "blk", axis=1, tiled=True),
            lax.all_gather(attended_grad_head.astype(jnp.float32), "blk", axis=1, tiled=True),
            lax.all_gather(log_total, "blk", axis=1, tiled=True),
            lax.all_gather(delta_rows, "blk", axis=1, tiled=True),
        ),
    )
    head_rows = sequence_batch * pair_tokens
    query_grad_head = (
        rotate(query_total.reshape(head_rows, local_heads * HEAD_DIM), head_cosine, head_sine, -1.0)
        .astype(jnp.bfloat16)
        .reshape(sequence_batch, pair_tokens, local_heads * HEAD_DIM)
    )
    key_grad_head = (
        rotate(
            key_total.reshape(head_rows, resident_key_value * HEAD_DIM),
            head_cosine,
            head_sine,
            -1.0,
        )
        .astype(jnp.bfloat16)
        .reshape(sequence_batch, pair_tokens, resident_key_value * HEAD_DIM)
    )
    value_grad_head = value_total.astype(jnp.bfloat16).reshape(
        sequence_batch, pair_tokens, resident_key_value * HEAD_DIM
    )
    query_grad_tok, key_grad_tokens, value_grad_tokens = (
        lax.all_to_all(query_grad_head, "head", split_axis=1, concat_axis=2, tiled=True),
        lax.all_to_all(key_grad_head, "head", split_axis=1, concat_axis=2, tiled=True),
        lax.all_to_all(value_grad_head, "head", split_axis=1, concat_axis=2, tiled=True),
    )
    query_grad = query_grad_tok.reshape(count_of_rows, QUERY_HEADS * HEAD_DIM)
    key_grad = key_grad_tokens.reshape(count_of_rows, KEY_HEADS * HEAD_DIM)
    value_gradient = value_grad_tokens.reshape(count_of_rows, KEY_HEADS * HEAD_DIM)
    query_piece, key_piece, value_piece = lax.all_gather(
        (query_weight, key_matrix, value_matrix), ("blk", "head"), axis=0, tiled=True
    )
    normed_one_grad = (
        lax.dot_general(query_grad, query_piece, contract_last, preferred_element_type=jnp.float32)
        + lax.dot_general(key_grad, key_piece, contract_last, preferred_element_type=jnp.float32)
        + lax.dot_general(
            value_gradient, value_piece, contract_last, preferred_element_type=jnp.float32
        )
    )
    input_grad = (
        middle_grad + norm_back(normed_one_grad * gain_one, normed_one, norm_one)
    ).reshape(sequence_batch, token_rows, model_width)
    chosen = tuple(
        (
            matrix
            for matrix in (
                normed_one,
                normed_one_grad,
                normed_low_one,
                query_grad,
                key_grad,
                value_gradient,
                attended_flat,
                middle_low,
                normed_two,
                normed_two_grad,
                scaled,
                gate_grad,
                up_grad,
                cotangent_flat,
                active,
            )
        )
    )
    (
        part_normed_one,
        part_grad_one,
        part_low_one,
        part_query,
        part_key,
        part_value,
        part_attended,
        part_middle,
        part_normed_two,
        part_grad_two,
        part_low_two,
        part_gate,
        part_up,
        part_cotangent,
        part_active,
    ) = chosen

    def columns(matrix):
        return matrix

    def outer(left, right):
        return lax.dot_general(
            columns(left), right, contract_first, preferred_element_type=jnp.float32
        )

    grads = lax.psum_scatter(
        (
            jnp.sum(columns(part_normed_one) * columns(part_grad_one), axis=0),
            outer(part_low_one, part_query),
            outer(part_low_one, part_key),
            outer(part_low_one, part_value),
            outer(part_attended, part_middle),
            jnp.sum(columns(part_normed_two) * columns(part_grad_two), axis=0),
            outer(part_low_two, part_gate),
            outer(part_low_two, part_up),
            outer(part_cotangent, part_active),
        ),
        ("blk", "head"),
        scatter_dimension=0,
        tiled=True,
    )
    return (
        layer_output,
        input_grad,
        grads[0],
        grads[1],
        grads[2],
        grads[3],
        grads[4],
        grads[5],
        grads[6],
        grads[7],
        grads[8],
    )


def solution(mesh):
    in_specs = (
        P(None, ("blk", "head"), None),
        P(("blk", "head")),
        P(("blk", "head"), None),
        P(("blk", "head"), None),
        P(("blk", "head"), None),
        P(("blk", "head"), None),
        P(("blk", "head")),
        P(("blk", "head"), None),
        P(("blk", "head"), None),
        P(("blk", "head"), None),
        P(),
        P(None, ("blk", "head"), None),
    )
    out_specs = (
        P(None, ("blk", "head"), None),
        P(None, ("blk", "head"), None),
        P(("blk", "head")),
        P(("blk", "head"), None),
        P(("blk", "head"), None),
        P(("blk", "head"), None),
        P(("blk", "head"), None),
        P(("blk", "head")),
        P(("blk", "head"), None),
        P(("blk", "head"), None),
        P(("blk", "head"), None),
    )
    return jax.shard_map(local, mesh=mesh, in_specs=in_specs, out_specs=out_specs, check_vma=False)
```

profile of v0, /device:TPU:0, one launch (start us, length us, event | category | flops | bytes accessed | tf_op | source)
XLA Modules:
  0.0 6646.4 jit_solution(15365461400769342164)
XLA Ops:
  11.2 42.1 all-reduce.5
  56.0 14.2 all-gather.14.cloned.1.call-done
  74.4 7.0 all_to_all.126
  83.0 45.6 all-gather.20.cloned.1.call-done
  131.2 7.0 all_to_all.127
  143.3 64.7 all-gather.18.cloned.1.call-done
  208.0 12.3 copy.283
  220.3 5.8 fusion.82
  233.0 7.4 all-to-all-done.1
  243.6 7.1 all-gather.16.cloned.1.call-done
  250.6 42.8 all-gather.22.cloned.1.call-done
  293.5 80.0 %while.30 = (s32[]{:T(128)}, f32[2,128,4,4]{1,3,2,0:T(4,128)S(1)}, f32[2,128,4,4]{1,3,2,0:T(4,128)S(1)}, f32[2,128,4,4,64]{1,4,3,2,0:T(8,128)}, s32[4]{0:T(128)S...) while((s32[]{:T(128)}, f32[2,128,4,4]{1,3,2,0:T(4,128)S(1)}, ...), condition=%wide.region_4.5_spmd.clone, body=%wide.region_1.4_spmd.clone.sunk | while | flops 565071872 | bytes 33830104 | solution.py:53
  306.7 6.4 fusion.179
  326.1 6.7 fusion.179
  341.0 5.6 fusion.177
  346.9 6.7 fusion.179
  366.6 6.9 fusion.179
  379.7 11.5 all-to-all-done.3
  392.0 5.0 multiply_reduce_fusion.5
  397.2 171.6 %all-gather.26.cloned.1.call-done = bf16[2048,8192]{1,0:T(8,128)(2,1)} async-done(((bf16[64,8192]{1,0:T(8,128)(2,1)}), bf16[2048,8192]{1,0:T(8,128)(2,1)}) %all-gather.26.cloned.1.call-update) | async-done | bytes 33554448 | tf_op jit(solution)/shard_map/all_gather | solution.py:198
  568.8 17.9 fusion.83
  586.7 178.1 %all-gather.28.cloned.1.call-done = bf16[2048,8192]{1,0:T(8,128)(2,1)} async-done(((bf16[64,8192]{1,0:T(8,128)(2,1)}), bf16[2048,8192]{1,0:T(8,128)(2,1)}) %all-gather.28.cloned.1.call-update) | async-done | bytes 33554448 | tf_op jit(solution)/shard_map/all_gather | solution.py:199
  764.8 17.8 fusion.84
  782.6 178.2 %all-gather.30.cloned.1.call-done = bf16[2048,8192]{1,0:T(8,128)(2,1)} async-done(((bf16[64,8192]{1,0:T(8,128)(2,1)}), bf16[2048,8192]{1,0:T(8,128)(2,1)}) %all-gather.30.cloned.1.call-update) | async-done | bytes 33554448 | tf_op jit(solution)/shard_map/all_gather | solution.py:210
  960.9 19.8 multiply_convert_fusion
  980.6 16.3 fusion.85
  997.0 17.3 multiply_reduce_fusion
  1014.6 7.5 convolution_convert_fusion
  1026.0 13.0 all_to_all.128
  1045.6 21.3 all_gather.71
  1073.6 19.1 all_gather.73
  1093.7 29.4 all-gather.36.cloned.1.call-done
  1123.1 76.0 %all-gather.38.cloned.1.call-done = bf16[2,2048,1024]{2,1,0:T(8,128)(2,1)} async-done(((bf16[2,128,1024]{2,1,0:T(8,128)(2,1)}), bf16[2,2048,1024]{2,1,0:T(8,128)(2,1)}) %all-gather.38.cloned.1.call-update) | async-done | bytes 8388624 | tf_op jit(solution)/shard_map/all_gather | solution.py:328
  1199.2 203.1 %while.31 = (s32[]{:T(128)}, f32[2,128,4,4,64]{1,4,3,2,0:T(8,128)}, f32[2,128,4,64]{1,3,2,0:T(8,128)}, f32[2,128,4,64]{1,3,2,0:T(8,128)}, bf16[4,2,512,256]{3,2,...) while((s32[]{:T(128)}, f32[2,128,4,4,64]{1,4,3,2,0:T(8,128)}, ...), condition=%wide.region_9.10_spmd.clone, body=%wide.region_8.9_spmd.clone.sunk | while | flops 1913978880 | bytes 78760232 | solution.py:53
  1207.7 7.7 fusion.195
  1233.0 10.6 fusion.197
  1243.6 6.1 fusion.198
  1258.1 8.1 fusion.195
  1283.7 10.6 fusion.197
  1294.3 6.1 fusion.198
  1308.8 8.1 fusion.195
  1334.4 10.6 fusion.197
  1345.0 6.1 fusion.198
  1359.6 8.1 fusion.195
  1385.2 10.6 fusion.197
  1395.8 6.1 fusion.198
  1404.3 7.0 all_to_all.129
  1415.3 8.1 all_to_all.130
  1426.4 8.2 fusion.76
  1439.3 13.4 all_to_all.131
  1454.3 8.1 fusion.87
  1464.2 23.5 fusion.90
  1489.3 23.4 fusion.91
  1514.4 23.3 convolution_bitcast_fusion
  1537.7 61.3 copy.346
  1600.2 17.1 convolution_add_fusion.3
  1617.3 6.4 fusion.86
  1625.7 41.6 all-reduce.4
  1669.8 27.6 reduce-scatter.14.cloned.1.call-done
  1697.4 357.6 %reduce-scatter.16.cloned.1.call-done = f32[64,2048]{1,0:T(8,128)} async-done(((f32[2048,2048]{1,0:T(8,128)}), f32[64,2048]{1,0:T(8,128)}) %reduce-scatter.16.cloned.1.call-update) | async-done | bytes 524304 | tf_op jit(solution)/shard_map/reduce_scatter | solution.py:421
  2055.0 361.3 %reduce-scatter.10.cloned.1.call-done = f32[64,2048]{1,0:T(8,128)} async-done(((f32[2048,2048]{1,0:T(8,128)}), f32[64,2048]{1,0:T(8,128)}) %reduce-scatter.10.cloned.1.call-update) | async-done | bytes 524304 | tf_op jit(solution)/shard_map/reduce_scatter | solution.py:421
  2416.3 1406.6 %reduce-scatter.18.cloned.1.call-done = f32[64,8192]{1,0:T(8,128)} async-done(((f32[2048,8192]{1,0:T(8,128)}), f32[64,8192]{1,0:T(8,128)}) %reduce-scatter.18.cloned.1.call-update) | async-done | bytes 2097168 | tf_op jit(solution)/shard_map/reduce_scatter | solution.py:421
  3822.9 1408.3 %reduce-scatter.20.cloned.1.call-done = f32[64,8192]{1,0:T(8,128)} async-done(((f32[2048,8192]{1,0:T(8,128)}), f32[64,8192]{1,0:T(8,128)}) %reduce-scatter.20.cloned.1.call-update) | async-done | bytes 2097168 | tf_op jit(solution)/shard_map/reduce_scatter | solution.py:421
  5231.2 1408.2 %reduce-scatter.22.cloned.1.call-done = f32[64,8192]{1,0:T(8,128)} async-done(((f32[2048,8192]{1,0:T(8,128)}), f32[64,8192]{1,0:T(8,128)}) %reduce-scatter.22.cloned.1.call-update) | async-done | bytes 2097168
  (329 shorter events, 226.9 us)
Async XLA Ops:
  7.2 75.4 %copy-start.4 = (bf16[2,64,2048]{2,1,0:T(8,128)(2,1)S(1)}, bf16[2,64,2048]{2,1,0:T(8,128)(2,1)}, u32[]{:S(2)}) copy-start(bf16[2,64,2048]{2,1,0:T(8,128)(2,1)} %param.16) | copy-start | bytes 1572868
  7.2 63.1 all-gather.14.cloned.1.call-start
  7.9 120.8 %all-gather.20.cloned.1.call-start = ((), (), s32[]{:S(2)}) async-start(), calls=%async_computation.18 | async-start | bytes 2162688 | tf_op jit(solution)/shard_map/all_gather | solution.py:105
  8.7 199.3 %all-gather.18.cloned.1.call-start = ((), (), s32[]{:S(2)}) async-start(), calls=%async_computation.17 | async-start | bytes 8650752 | tf_op jit(solution)/shard_map/all_gather | solution.py:103
  9.4 241.2 %all-gather.16.cloned.1.call-start = ((), (), s32[]{:S(2)}) async-start(), calls=%async_computation.16 | async-start | bytes 2228224 | tf_op jit(solution)/shard_map/all_gather | solution.py:179
  53.3 85.9 %copy-start.34 = (f32[2048]{0:T(1024)}, f32[2048]{0:T(1024)S(1)}, u32[]{:S(2)}) copy-start(f32[2048]{0:T(1024)S(1)} %convert_element_type.171) | copy-start | bytes 24580
  56.0 164.3 %copy-start.2 = (bf16[2,64,2048]{2,1,0:T(8,128)(2,1)}, bf16[2,64,2048]{2,1,0:T(8,128)(2,1)S(1)}, u32[]{:S(2)}) copy-start(bf16[2,64,2048]{2,1,0:T(8,128)(2,1)S(1)} %multiply_convert_fusion.5) | copy-start | bytes 1572868
  82.4 211.1 %all-gather.22.cloned.1.call-start = ((), (), s32[]{:S(2)}) async-start(), calls=%async_computation.19 | async-start | bytes 2228224 | tf_op jit(solution)/shard_map/all_gather | solution.py:180
  82.5 0.5 copy-start.37
  138.3 82.0 %copy-start.21 = (bf16[512,2,64]{2,1,0:T(2,128)(2,1)}, bf16[512,2,64]{2,1,0:T(2,128)(2,1)S(1)}, u32[]{:S(2)}) copy-start(bf16[512,2,64]{2,1,0:T(2,128)(2,1)S(1)} %reshape.428) | copy-start | bytes 393220
  139.2 252.8 %all-gather.24.cloned.1.call-start = ((), (), s32[]{:S(2)}) async-start(), calls=%async_computation.20 | async-start | bytes 8650752 | tf_op jit(solution)/shard_map/all_gather | solution.py:191
  139.8 429.1 %all-gather.26.cloned.1.call-start = ((), (), s32[]{:S(2)}) async-start(), calls=%async_computation.21 | async-start | bytes 34603008 | tf_op jit(solution)/shard_map/all_gather | solution.py:198
  140.5 624.3 %all-gather.28.cloned.1.call-start = ((), (), s32[]{:S(2)}) async-start(), calls=%async_computation.22 | async-start | bytes 34603008 | tf_op jit(solution)/shard_map/all_gather | solution.py:199
  141.3 819.6 %all-gather.30.cloned.1.call-start = ((), (), s32[]{:S(2)}) async-start(), calls=%async_computation.23 | async-start | bytes 34603008 | tf_op jit(solution)/shard_map/all_gather | solution.py:210
  142.0 951.7 %all-gather.32.cloned.1.call-start = ((), (), s32[]{:S(2)}) async-start(), calls=%async_computation.24 | async-start | bytes 2228224 | tf_op jit(solution)/shard_map/all_gather | solution.py:325
  142.6 951.1 %all-gather.34.cloned.1.call-start = ((), (), s32[]{:S(2)}) async-start(), calls=%async_computation.25 | async-start | bytes 2228224 | tf_op jit(solution)/shard_map/all_gather | solution.py:326
  228.3 12.2 all-to-all-start.1
  231.8 891.3 %all-gather.36.cloned.1.call-start = ((), (), s32[]{:S(2)}) async-start(), calls=%async_computation.26 | async-start | bytes 8912896 | tf_op jit(solution)/shard_map/all_gather | solution.py:327
  241.9 1.6 copy-start.18
  376.0 15.2 all-to-all-start.3
  379.5 819.7 %all-gather.38.cloned.1.call-start = ((), (), s32[]{:S(2)}) async-start(), calls=%async_computation.27 | async-start | bytes 8912896 | tf_op jit(solution)/shard_map/all_gather | solution.py:328
  392.0 5.1 copy-start.16
  397.0 617.2 %copy-start = (f32[128,2048]{1,0:T(8,128)}, f32[128,2048]{1,0:T(8,128)S(1)}, u32[]{:S(2)}) copy-start(f32[128,2048]{1,0:T(8,128)S(1)} %get-tuple-element.658) | copy-start | bytes 3145732
  397.2 367.6 %copy-start.9 = (bf16[128,2048]{1,0:T(8,128)(2,1)}, bf16[128,2048]{1,0:T(8,128)(2,1)S(1)}, u32[]{:S(2)}) copy-start(bf16[128,2048]{1,0:T(8,128)(2,1)S(1)} %multiply_convert_fusion.3) | copy-start | bytes 1572868
  586.7 374.2 %copy-start.23 = (bf16[2,64,2048]{2,1,0:T(8,128)(2,1)S(1)}, bf16[2,64,2048]{2,1,0:T(8,128)(2,1)}, u32[]{:S(2)}) copy-start(bf16[2,64,2048]{2,1,0:T(8,128)(2,1)} %param.27) | copy-start | bytes 1572868
  1014.6 28.0 copy-start.6
  1014.6 29.2 copy-start.22
  1042.6 627.2 %reduce-scatter.12.cloned.1.call-start = ((), (), s32[]{:S(2)}) async-start(), calls=%async_computation.29 | async-start | bytes 4325376 | tf_op jit(solution)/shard_map/reduce_scatter | solution.py:421
  1071.4 127.8 %copy-start.25 = (bf16[2,128,4,4,64]{1,4,3,2,0:T(8,128)(2,1)}, bf16[2,128,4,4,64]{1,4,3,2,0:T(8,128)(2,1)S(1)}, u32[]{:S(2)}) copy-start(bf16[2,128,4,4,64]{1,4,3,2,0:T(8,128)(2,1)S(1)} %copy.305) | copy-start | bytes 1572868
  1199.1 213.0 %copy-start.3 = (bf16[2,64,2048]{2,1,0:T(8,128)(2,1)S(1)}, bf16[2,64,2048]{2,1,0:T(8,128)(2,1)}, u32[]{:S(2)}) copy-start(bf16[2,64,2048]{2,1,0:T(8,128)(2,1)} %copy-done.2) | copy-start | bytes 1572868
  1402.3 12.8 copy-start.33
  1411.5 0.6 copy-start.26
  1415.0 11.3 copy-start.7
  1415.0 11.3 copy-start.17
  1415.1 282.3 %reduce-scatter.14.cloned.1.call-start = ((), (), s32[]{:S(2)}) async-start(), calls=%async_computation.30 | async-start | bytes 4325376 | tf_op jit(solution)/shard_map/reduce_scatter | solution.py:421
  1423.6 11.0 copy-start.28
  1426.3 628.7 %reduce-scatter.16.cloned.1.call-start = ((), (), s32[]{:S(2)}) async-start(), calls=%async_computation.31 | async-start | bytes 17301504 | tf_op jit(solution)/shard_map/reduce_scatter | solution.py:421
  1434.5 1.2 copy-start.30
  1434.5 2.9 copy-start.31
  1434.5 2.9 copy-start.32
  1434.6 981.7 %reduce-scatter.10.cloned.1.call-start = ((), (), s32[]{:S(2)}) async-start(), calls=%async_computation.28 | async-start | bytes 17301504 | tf_op jit(solution)/shard_map/reduce_scatter | solution.py:421
  1453.5 0.8 copy-start.19
  1462.5 1.0 copy-start.10
  1462.5 1.8 copy-start.13
  1462.5 2360.4 %reduce-scatter.18.cloned.1.call-start = ((), (), s32[]{:S(2)}) async-start(), calls=%async_computation.32 | async-start | bytes 69206016 | tf_op jit(solution)/shard_map/reduce_scatter | solution.py:421
  1487.7 1.6 copy-start.12
  1487.8 3743.5 %reduce-scatter.20.cloned.1.call-start = ((), (), s32[]{:S(2)}) async-start(), calls=%async_computation.33 | async-start | bytes 69206016 | tf_op jit(solution)/shard_map/reduce_scatter | solution.py:421
  1512.7 1.6 copy-start.11
  1512.7 1.7 copy-start.24
  1512.7 5126.7 %reduce-scatter.22.cloned.1.call-start = ((), (), s32[]{:S(2)}) async-start(), calls=%async_computation.34 | async-start | bytes 69206016
  1598.9 1.2 copy-start.1
  1600.2 17.1 copy-start.20
  1617.3 6.5 copy-start.14
  1617.3 6.5 copy-start.27
  1617.3 7.4 copy-start.5
  1617.3 7.4 copy-start.15
  1617.3 7.4 copy-start.29
  1617.3 7.4 copy-start.35
  1617.3 7.4 copy-start.38
  1617.3 8.4 copy-start.36
  1617.3 51.2 copy-start.8
Sparse Core Ops, SparseCore 0:
  11.0 59.2 all-gather.13
  73.2 55.4 all-gather.19
  131.7 76.2 all-gather.17
  210.6 40.0 all-gather.15
  253.3 40.1 all-gather.21
  296.3 76.0 all-gather.23
  375.4 193.3 all-gather.25
  571.8 192.9 all-gather.27
  767.8 192.9 all-gather.29
  963.5 39.5 all-gather.31
  1005.8 40.2 all-gather.33
  1048.1 74.9 all-gather.35
  1125.9 73.2 all-gather.37
  1415.2 139.5 reduce-scatter.11
  1557.5 139.8 reduce-scatter.13
  1700.1 354.7 reduce-scatter.15
  2057.7 358.5 reduce-scatter.9
  2419.1 1403.7 reduce-scatter.17
  3825.9 1405.3 reduce-scatter.19
  5234.0 1405.3 reduce-scatter.21
where the time goes:
time: 6660 us; the launch traced here: 6650 us
  waiting for transfers between devices  5800 us (87%)
  matrix products  408 us (6%)
  local copies, waits for them, and re-layouts  193 us (3%)
  blocking collectives  180 us (3%)
    reduce_scatter x6, waiting for transfers between devices, local(): lax.psum_scatter((jnp.sum(columns(part_normed_one) * columns(part_grad_on...  3560 us
    unnamed x21, waiting for transfers between devices  1410 us
    all_gather x1, waiting for transfers between devices, local(): piece = lax.all_gather(down_weight, ('blk', 'head'), axis=0, tiled=True)  178 us
    all_gather x1, waiting for transfers between devices, local(): up_piece = lax.all_gather(up_weight, ('blk', 'head'), axis=0, tiled=True)  178 us
    all_gather x1, waiting for transfers between devices, local(): lax.all_gather(gate_weight, ('blk', 'head'), axis=0, tiled=True)  172 us
  transfers between devices with their start and end apart: 22, of which 18 were waited for; matrix products, arithmetic and copies ran while one was open for 6% of the time, Pallas kernels for 0%

commit v1 on v0

v1 whole, which is shorter than its diff:
```python
import itertools

import jax
import jax.numpy as jnp
from jax import lax
from jax.experimental import pallas as pl
from jax.experimental.pallas import tpu as pltpu
from jax.sharding import Mesh
from jax.sharding import PartitionSpec as P

QUERY_HEADS = 32
KEY_HEADS = 8
HEAD_DIM = 64
TEAM = 16
SCALE = HEAD_DIM ** (-0.5)
epsilon = 1e-05
rope_base = 500000.0
NT = (((1,), (1,)), ((), ()))
TN = (((0,), (0,)), ((), ()))
TEAM_AXES = ("z", "y", "c", "x")
ALL = ("dp",) + TEAM_AXES

DIMS = ("z", "y", "c", "x")
WEIGHT = {"z": 8, "y": 4, "c": 2, "x": 1}
LINKS = ("x", "y", "z")
ORDERS = (("x", "y", "z"), ("y", "z", "x"), ("z", "x", "y"))
MESH = pl.DeviceIdType.MESH


def part_rows(rows):
    tiles = rows // 16
    base = [tiles // 3 + (1 if i < tiles % 3 else 0) for i in range(3)]
    out, at = [], 0
    for b in base:
        out.append((at * 16, b * 16))
        at += b
    return out


def coords():
    return {d: lax.axis_index(d) for d in DIMS}


def slot_of(me, flips=()):
    return sum(((1 - me[d]) if d in flips else me[d]) * WEIGHT[d] for d in DIMS)


def greet(me):
    barrier = pltpu.get_barrier_semaphore()
    for d in DIMS:
        pl.semaphore_signal(barrier, inc=1, device_id={d: 1 - me[d]}, device_id_type=MESH)
    pl.semaphore_wait(barrier, len(DIMS))


def ag_kernel(x_ref, g_ref, ssem, rsem, lsem):
    me = coords()
    rows = x_ref.shape[0]
    parts = part_rows(rows)
    greet(me)
    mine = slot_of(me)
    local = pltpu.make_async_copy(x_ref, g_ref.at[mine], lsem)
    local.start()
    counter = itertools.count()
    copies = []

    def send(flips, r0, rn, dim, own):
        i = next(counter)
        s = slot_of(me, flips)
        src = x_ref.at[pl.ds(r0, rn)] if own else g_ref.at[s, pl.ds(r0, rn)]
        cp = pltpu.make_async_remote_copy(
            src_ref=src, dst_ref=g_ref.at[s, pl.ds(r0, rn)],
            send_sem=ssem.at[i], recv_sem=rsem.at[i],
            device_id={dim: 1 - me[dim]}, device_id_type=MESH)
        cp.start()
        copies.append(cp)
        return cp

    step1, step2, step3 = {}, {}, {}
    for p, (r0, rn) in enumerate(parts):
        step1[p] = [send((), r0, rn, ORDERS[p][0], True)]
    for p, (r0, rn) in enumerate(parts):
        step2[p] = [send((), r0, rn, ORDERS[p][1], True)]
    for p, (r0, rn) in enumerate(parts):
        step3[p] = [send((), r0, rn, ORDERS[p][2], True)]
    core = [send((), 0, rows, "c", True)]
    for p, (r0, rn) in enumerate(parts):
        a, b, c = ORDERS[p]
        step1[p][0].wait_recv()
        step2[p].append(send((a,), r0, rn, b, False))
        step3[p].append(send((a,), r0, rn, c, False))
        core.append(send((a,), r0, rn, "c", False))
    for p, (r0, rn) in enumerate(parts):
        a, b, c = ORDERS[p]
        for cp, fl in zip(step2[p], ((b,), (a, b))):
            cp.wait_recv()
            step3[p].append(send(fl, r0, rn, c, False))
            core.append(send(fl, r0, rn, "c", False))
    for p, (r0, rn) in enumerate(parts):
        a, b, c = ORDERS[p]
        for cp, fl in zip(step3[p], ((c,), (a, c), (b, c), (a, b, c))):
            cp.wait_recv()
            core.append(send(fl, r0, rn, "c", False))
    for cp in core:
        cp.wait_recv()
    for cp in copies:
        cp.wait_send()
    local.wait()


def all_gather16(x, cid=1):
    rows, cols = x.shape
    return pl.pallas_call(
        ag_kernel,
        out_shape=jax.ShapeDtypeStruct((16, rows, cols), x.dtype),
        in_specs=[pl.BlockSpec(memory_space=pltpu.VMEM)],
        out_specs=pl.BlockSpec(memory_space=pltpu.VMEM),
        scratch_shapes=[pltpu.SemaphoreType.DMA((64,)), pltpu.SemaphoreType.DMA((64,)), pltpu.SemaphoreType.DMA],
        compiler_params=pltpu.CompilerParams(collective_id=cid, has_side_effects=True, vmem_limit_bytes=50 << 20),
    )(x)


FULL = list(itertools.product((0, 1), repeat=3))


def flips_of(bits, order):
    return tuple(d for b, d in zip(bits, order) if b)


def add_rows(dst, a, b, r0, rn):
    def body(i, _):
        r = pl.multiple_of(r0 + i * 16, 16)
        dst[pl.ds(r, 16)] = (a[pl.ds(r, 16)].astype(jnp.float32) + b[pl.ds(r, 16)].astype(jnp.float32)).astype(dst.dtype)
        return 0
    lax.fori_loop(0, rn // 16, body, 0)


def rs_kernel(p_ref, o_ref, acc, cbuf, b1, b2, b3, ssem, rsem):
    me = coords()
    rows = p_ref.shape[1]
    parts = part_rows(rows)
    greet(me)
    counter = itertools.count()
    copies = []

    def send(src, dst, dim):
        i = next(counter)
        cp = pltpu.make_async_remote_copy(
            src_ref=src, dst_ref=dst, send_sem=ssem.at[i], recv_sem=rsem.at[i],
            device_id={dim: 1 - me[dim]}, device_id_type=MESH)
        cp.start()
        copies.append(cp)
        return cp

    def key(flips):
        return sum((1 << i) for i, d in enumerate(LINKS) if d in flips)

    order0 = [(1, 1, 1), (0, 1, 1), (1, 0, 1), (1, 1, 0), (1, 0, 0), (0, 1, 0), (0, 0, 1), (0, 0, 0)]
    core = {}
    for bits in order0:
        fl = flips_of(bits, LINKS)
        core[fl] = send(p_ref.at[slot_of(me, fl + ("c",))], cbuf.at[key(fl)], "c")
    s1 = {p: {} for p in range(3)}
    for bits in order0:
        fl = flips_of(bits, LINKS)
        core[fl].wait_recv()
        k = key(fl)
        add_rows(acc.at[k], p_ref.at[slot_of(me, fl)], cbuf.at[k], 0, rows)
        for p, (r0, rn) in enumerate(parts):
            a, b, c = ORDERS[p]
            if a in fl:
                rest = tuple(d for d in fl if d != a)
                j = (1 if b in fl else 0) + (2 if c in fl else 0)
                s1[p][rest] = send(acc.at[k, pl.ds(r0, rn)], b1.at[j, pl.ds(r0, rn)], a)
    s2 = {p: {} for p in range(3)}
    for (bb, cc) in ((1, 1), (1, 0), (0, 1), (0, 0)):
        for p, (r0, rn) in enumerate(parts):
            a, b, c = ORDERS[p]
            fl = flips_of((bb, cc), (b, c))
            match = [q for q in s1[p] if set(q) == set(fl)][0]
            s1[p][match].wait_recv()
            k = key(fl)
            add_rows(acc.at[k], acc.at[k], b1.at[bb + 2 * cc], r0, rn)
            if bb:
                s2[p][cc] = send(acc.at[k, pl.ds(r0, rn)], b2.at[cc, pl.ds(r0, rn)], b)
    s3 = {}
    for cc in (1, 0):
        for p, (r0, rn) in enumerate(parts):
            a, b, c = ORDERS[p]
            s2[p][cc].wait_recv()
            k = key((c,) if cc else ())
            add_rows(acc.at[k], acc.at[k], b2.at[cc], r0, rn)
            if cc:
                s3[p] = send(acc.at[k, pl.ds(r0, rn)], b3.at[pl.ds(r0, rn)], c)
    for p, (r0, rn) in enumerate(parts):
        s3[p].wait_recv()
        add_rows(o_ref, acc.at[0], b3, r0, rn)
    for cp in copies:
        cp.wait_send()


def reduce_scatter16(p, cid=2, out_dtype=jnp.float32):
    _, rows, cols = p.shape
    return pl.pallas_call(
        rs_kernel,
        out_shape=jax.ShapeDtypeStruct((rows, cols), out_dtype),
        in_specs=[pl.BlockSpec(memory_space=pltpu.VMEM)],
        out_specs=pl.BlockSpec(memory_space=pltpu.VMEM),
        scratch_shapes=[
            pltpu.VMEM((8, rows, cols), p.dtype), pltpu.VMEM((8, rows, cols), p.dtype),
            pltpu.VMEM((4, rows, cols), p.dtype), pltpu.VMEM((2, rows, cols), p.dtype), pltpu.VMEM((rows, cols), p.dtype),
            pltpu.SemaphoreType.DMA((32,)), pltpu.SemaphoreType.DMA((32,))],
        compiler_params=pltpu.CompilerParams(collective_id=cid, has_side_effects=True, vmem_limit_bytes=56 << 20),
    )(p)
NEG = -1e30
Q_CHUNK = 256
K_CHUNK = 512


def attend_kernel(count_ref, q_ref, k_ref, v_ref, qid_ref, kid_ref, o_ref, lse_ref):
    s, i = pl.program_id(0), pl.program_id(1)
    heads, chunk, width = q_ref.shape[1:]
    rows = heads * chunk
    q = q_ref[0].reshape(rows, width)
    qid = qid_ref[0]
    qids = jnp.concatenate([qid] * heads, axis=0)

    def step(j, state):
        top, total, acc = state
        at = pl.multiple_of(j * K_CHUNK, K_CHUNK)
        k = k_ref[0, pl.ds(at, K_CHUNK), :]
        v = v_ref[0, pl.ds(at, K_CHUNK), :]
        kid = kid_ref[0, :, pl.ds(at, K_CHUNK)]
        scores = lax.dot_general(q, k, NT, preferred_element_type=jnp.float32) * SCALE
        scores = jnp.where(kid <= qids, scores, NEG)
        new_top = jnp.maximum(top, jnp.max(scores, axis=-1, keepdims=True))
        p = jnp.exp(scores - new_top)
        factor = jnp.exp(top - new_top)
        total = total * factor + jnp.sum(p, axis=-1, keepdims=True)
        acc = acc * factor + jnp.dot(p.astype(jnp.bfloat16), v, preferred_element_type=jnp.float32)
        return new_top, total, acc

    start = (
        jnp.full((rows, 1), NEG, jnp.float32),
        jnp.zeros((rows, 1), jnp.float32),
        jnp.zeros((rows, width), jnp.float32),
    )
    top, total, acc = lax.fori_loop(0, count_ref[s, i], step, start)
    o_ref[0] = (acc / total).astype(jnp.bfloat16).reshape(heads, chunk, width)
    lse_ref[0] = (top + jnp.log(total)).reshape(heads, chunk, 1)


def attend(counts, q, k, v, qid, kid):
    seqs, heads, n, width = q.shape
    keys = k.shape[1]
    spec = pltpu.PrefetchScalarGridSpec(
        num_scalar_prefetch=1,
        grid=(seqs, n // Q_CHUNK),
        in_specs=[
            pl.BlockSpec((1, heads, Q_CHUNK, width), lambda s, i, c: (s, 0, i, 0)),
            pl.BlockSpec((1, keys, width), lambda s, i, c: (s, 0, 0)),
            pl.BlockSpec((1, keys, width), lambda s, i, c: (s, 0, 0)),
            pl.BlockSpec((1, Q_CHUNK, 1), lambda s, i, c: (s, i, 0)),
            pl.BlockSpec((1, 1, keys), lambda s, i, c: (s, 0, 0)),
        ],
        out_specs=[
            pl.BlockSpec((1, heads, Q_CHUNK, width), lambda s, i, c: (s, 0, i, 0)),
            pl.BlockSpec((1, heads, Q_CHUNK, 1), lambda s, i, c: (s, 0, i, 0)),
        ],
    )
    return pl.pallas_call(
        attend_kernel,
        grid_spec=spec,
        out_shape=[
            jax.ShapeDtypeStruct(q.shape, jnp.bfloat16),
            jax.ShapeDtypeStruct((seqs, heads, n, 1), jnp.float32),
        ],
        compiler_params=pltpu.CompilerParams(vmem_limit_bytes=48 << 20),
    )(counts, q, k, v, qid, kid)


def attend_back_kernel(count_ref, q_ref, g_ref, lse_ref, delta_ref, k_ref, v_ref, qid_ref, kid_ref, dq_ref, dk_ref, dv_ref):
    s, i = pl.program_id(0), pl.program_id(1)
    heads, chunk, width = q_ref.shape[1:]
    rows = heads * chunk
    q = q_ref[0].reshape(rows, width)
    g = g_ref[0].reshape(rows, width)
    lse = jnp.concatenate([lse_ref[0, h] for h in range(heads)], axis=1)
    delta = jnp.concatenate([delta_ref[0, h] for h in range(heads)], axis=1)
    qids = jnp.concatenate([qid_ref[0]] * heads, axis=1)

    @pl.when(i == 0)
    def _():
        dk_ref[...] = jnp.zeros_like(dk_ref)
        dv_ref[...] = jnp.zeros_like(dv_ref)

    def step(j, dq):
        at = pl.multiple_of(j * K_CHUNK, K_CHUNK)
        here = pl.ds(at, K_CHUNK)
        k = k_ref[0, here, :]
        v = v_ref[0, here, :]
        kid = kid_ref[0, here, :]
        scores = lax.dot_general(k, q, NT, preferred_element_type=jnp.float32) * SCALE
        p = jnp.where(kid <= qids, jnp.exp(scores - lse), 0.0)
        dp = lax.dot_general(v, g, NT, preferred_element_type=jnp.float32)
        ds = (p * (dp - delta)).astype(jnp.bfloat16)
        dv_ref[0, here, :] += jnp.dot(p.astype(jnp.bfloat16), g, preferred_element_type=jnp.float32)
        dk_ref[0, here, :] += jnp.dot(ds, q, preferred_element_type=jnp.float32) * SCALE
        return dq + lax.dot_general(ds, k, TN, preferred_element_type=jnp.float32)

    dq = lax.fori_loop(0, count_ref[s, i], step, jnp.zeros((rows, width), jnp.float32))
    dq_ref[0] = (dq * SCALE).reshape(heads, chunk, width)


def attend_back(counts, q, g, lse, delta, k, v, qid, kid):
    seqs, heads, n, width = q.shape
    keys = k.shape[1]
    wide = pl.BlockSpec((1, heads, Q_CHUNK, width), lambda s, i, c: (s, 0, i, 0))
    row = pl.BlockSpec((1, heads, 1, Q_CHUNK), lambda s, i, c: (s, 0, 0, i))
    whole = pl.BlockSpec((1, keys, width), lambda s, i, c: (s, 0, 0))
    spec = pltpu.PrefetchScalarGridSpec(
        num_scalar_prefetch=1,
        grid=(seqs, n // Q_CHUNK),
        in_specs=[
            wide, wide, row, row, whole, whole,
            pl.BlockSpec((1, 1, Q_CHUNK), lambda s, i, c: (s, 0, i)),
            pl.BlockSpec((1, keys, 1), lambda s, i, c: (s, 0, 0)),
        ],
        out_specs=[wide, whole, whole],
    )
    return pl.pallas_call(
        attend_back_kernel,
        grid_spec=spec,
        out_shape=[
            jax.ShapeDtypeStruct(q.shape, jnp.float32),
            jax.ShapeDtypeStruct(k.shape, jnp.float32),
            jax.ShapeDtypeStruct(k.shape, jnp.float32),
        ],
        compiler_params=pltpu.CompilerParams(vmem_limit_bytes=56 << 20),
    )(counts, q, g, lse, delta, k, v, qid, kid)


def rotation_tables(positions):
    half = HEAD_DIM // 2
    freqs = rope_base ** (-jnp.arange(half, dtype=jnp.float32) * 2.0 / HEAD_DIM)
    angles = positions.astype(jnp.float32)[:, None] * freqs[None, :]
    return jnp.cos(angles), jnp.sin(angles)


def rotate(values, cosine, sine):
    half = HEAD_DIM // 2
    first, second = values[..., :half], values[..., half:]
    return jnp.concatenate([first * cosine - second * sine, second * cosine + first * sine], axis=-1)


def norm_back(grad, normed, scale):
    return scale * (grad - normed * jnp.mean(grad * normed, axis=-1, keepdims=True))


def exchange(x):
    return lax.all_to_all(x, ALL, split_axis=0, concat_axis=0, tiled=True)


def local(
    layer_input, attn_gain, query_weight, key_matrix, value_matrix, output_weight, ffn_gain,
    gate_weight, up_weight, down_weight, block_ids, cotangent,
):
    f32, bf16 = jnp.float32, jnp.bfloat16
    seqs, tokens, model = layer_input.shape
    rows = seqs * tokens
    groups = lax.axis_size("dp")
    group = lax.axis_index("dp")
    devices = groups * TEAM
    share = query_weight.shape[0]
    span = TEAM * tokens
    heads = QUERY_HEADS // TEAM
    ff = gate_weight.shape[1] // TEAM
    twin = TEAM // KEY_HEADS

    gain_one = attn_gain.astype(f32)[:, None]
    gain_two = ffn_gain.astype(f32)[:, None]

    def scaled(weight, gain):
        return (weight.astype(f32) * gain).astype(bf16)

    def send_out(piece):
        piece = jnp.moveaxis(piece, 1, 0)
        return exchange(jnp.broadcast_to(piece[None], (groups,) + piece.shape).reshape((devices,) + piece.shape[1:]))

    def doubled(weight):
        split = weight.reshape(share, KEY_HEADS, 1, HEAD_DIM)
        return jnp.broadcast_to(split, (share, KEY_HEADS, twin, HEAD_DIM)).reshape(share, TEAM, HEAD_DIM)

    w_in = send_out(
        jnp.concatenate(
            [
                scaled(query_weight, gain_one).reshape(share, TEAM, heads * HEAD_DIM),
                doubled(scaled(key_matrix, gain_one)),
                doubled(scaled(value_matrix, gain_one)),
            ],
            axis=-1,
        )
    ).reshape(model, -1)
    w_ffn = send_out(
        jnp.concatenate(
            [
                scaled(gate_weight, gain_two).reshape(share, TEAM, ff),
                scaled(up_weight, gain_two).reshape(share, TEAM, ff),
                down_weight.reshape(share, TEAM, ff),
            ],
            axis=-1,
        )
    ).reshape(model, -1)
    w_gate_up, w_down = w_ffn[:, : 2 * ff], w_ffn[:, 2 * ff :]
    deal = [(j, (j % groups) * TEAM + j // groups) for j in range(devices)]
    w_out = lax.all_gather(lax.ppermute(output_weight, ALL, deal), "dp", axis=0, tiled=True)

    x = layer_input.reshape(rows, model).astype(f32)
    norm_one = lax.rsqrt(jnp.mean(x * x, axis=-1, keepdims=True) + epsilon)
    normed_one = x * norm_one
    c_own = cotangent.reshape(rows, model)
    h_one = all_gather16(normed_one.astype(bf16)).reshape(-1, model)
    c_all = all_gather16(c_own).reshape(-1, model)

    def by_sequence(piece, count):
        piece = piece.reshape(TEAM, seqs, tokens, count, HEAD_DIM)
        return piece.transpose(1, 3, 0, 2, 4).reshape(seqs, count, span, HEAD_DIM)

    def by_device(piece):
        count = piece.shape[1]
        piece = piece.reshape(seqs, count, TEAM, tokens, HEAD_DIM)
        return piece.transpose(2, 0, 3, 1, 4).reshape(TEAM * rows, count * HEAD_DIM)

    cosine, sine = rotation_tables(group * span + jnp.arange(span, dtype=jnp.int32))
    raw = jnp.dot(h_one, w_in, preferred_element_type=f32)
    qk = by_sequence(raw[:, : (heads + 1) * HEAD_DIM], heads + 1)
    qk = rotate(qk, cosine, sine).astype(bf16)
    q, k_own = qk[:, :heads], qk[:, heads]
    v_own = by_sequence(raw[:, (heads + 1) * HEAD_DIM :].astype(bf16), 1)[:, 0]
    kv = lax.all_gather(jnp.concatenate([k_own, v_own], axis=-1), "dp", axis=1, tiled=True)
    k, v = kv[..., :HEAD_DIM], kv[..., HEAD_DIM:]
    ids = lax.dynamic_slice_in_dim(block_ids, group * span, span, 1)
    counts = jnp.sum(
        block_ids[:, None, ::K_CHUNK] <= ids[:, Q_CHUNK - 1 :: Q_CHUNK, None], axis=-1
    ).astype(jnp.int32)
    o, lse = attend(counts, q, k, v, ids[:, :, None], block_ids[:, None, :])
    o_all = by_device(o)
    branch = reduce_scatter16(jnp.dot(o_all, w_out, preferred_element_type=f32).astype(bf16).reshape(TEAM, rows, model))
    middle = x + branch
    norm_two = lax.rsqrt(jnp.mean(middle * middle, axis=-1, keepdims=True) + epsilon)
    normed_two = middle * norm_two
    h_two = all_gather16(normed_two.astype(bf16)).reshape(-1, model)
    gate_up = jnp.dot(h_two, w_gate_up, preferred_element_type=f32)
    gate, up = gate_up[:, :ff], gate_up[:, ff:]
    sig = jax.nn.sigmoid(gate)
    silu = gate * sig
    active = (silu * up).astype(bf16)
    da = jnp.dot(c_all, w_down, preferred_element_type=f32)
    d_gate_up = jnp.concatenate(
        [(da * up * sig * (1.0 + gate * (1.0 - sig))).astype(bf16), (da * silu).astype(bf16)], axis=-1
    )
    produced = reduce_scatter16(
        lax.dot_general(active, w_down, NT, preferred_element_type=f32).astype(bf16).reshape(TEAM, rows, model)
    )
    layer_output = (middle + produced).reshape(seqs, tokens, model)
    dn_two = reduce_scatter16(
        lax.dot_general(d_gate_up, w_gate_up, NT, preferred_element_type=f32).astype(bf16).reshape(TEAM, rows, model)
    )
    middle_grad = c_own.astype(f32) + norm_back(dn_two, normed_two, norm_two)
    middle_low = all_gather16(middle_grad.astype(bf16)).reshape(-1, model)
    do = lax.dot_general(middle_low, w_out, NT, preferred_element_type=f32).astype(bf16)
    g = by_sequence(do, heads)
    delta = jnp.sum(g.astype(f32) * o.astype(f32), axis=-1)
    dq, dk, dv = attend_back(
        counts, q, g, lse.reshape(seqs, heads, 1, span), delta.reshape(seqs, heads, 1, span), k, v,
        ids[:, None, :], block_ids[:, :, None],
    )
    dkv = jnp.concatenate([dk, dv], axis=-1).astype(bf16).reshape(seqs, groups, span, 2 * HEAD_DIM)
    dkv = lax.all_to_all(dkv, "dp", split_axis=1, concat_axis=1, tiled=True)
    dkv = jnp.sum(dkv.astype(f32), axis=1)
    dqk = rotate(jnp.concatenate([dq, dkv[:, None, :, :HEAD_DIM]], axis=1), cosine, -sine)
    d_in = by_device(jnp.concatenate([dqk, dkv[:, None, :, HEAD_DIM:]], axis=1).astype(bf16))
    dn_one = reduce_scatter16(
        lax.dot_general(d_in, w_in, NT, preferred_element_type=f32).astype(bf16).reshape(TEAM, rows, model)
    )
    input_grad = (middle_grad + norm_back(dn_one, normed_one, norm_one)).reshape(seqs, tokens, model)

    def outer(left, right):
        return lax.dot_general(left, right, TN, preferred_element_type=f32)

    def gather_sum(piece):
        piece = exchange(piece.astype(bf16).reshape(devices, share, piece.shape[-1]))
        piece = jnp.sum(piece.reshape(groups, TEAM, share, -1).astype(f32), axis=0)
        return jnp.moveaxis(piece, 0, 1)

    ffn = gather_sum(jnp.concatenate([outer(h_two, d_gate_up), outer(c_all, active)], axis=-1))
    grad_gate = ffn[..., :ff].reshape(share, -1) * gain_two
    grad_up = ffn[..., ff : 2 * ff].reshape(share, -1) * gain_two
    grad_down = ffn[..., 2 * ff :].reshape(share, -1)
    attn = gather_sum(outer(h_one, d_in))
    cut = heads * HEAD_DIM
    grad_query = attn[..., :cut].reshape(share, -1) * gain_one
    pair = attn[..., cut:].reshape(share, KEY_HEADS, twin, 2, HEAD_DIM).sum(axis=2)
    grad_key = pair[:, :, 0].reshape(share, -1) * gain_one
    grad_value = pair[:, :, 1].reshape(share, -1) * gain_one
    w_out_part = outer(o_all, middle_low).astype(bf16).reshape(groups, -1, model)
    w_out_part = lax.all_to_all(w_out_part, "dp", split_axis=0, concat_axis=0, tiled=True)
    grad_output = lax.ppermute(
        jnp.sum(w_out_part.astype(f32), axis=0), ALL, [(b, a) for a, b in deal]
    )
    gains = jnp.stack(
        [jnp.sum(normed_one * dn_one, axis=0), jnp.sum(normed_two * dn_two, axis=0)], axis=0
    )
    gains = exchange(gains.reshape(2, devices, share).transpose(1, 0, 2)).sum(axis=0)
    return (
        layer_output, input_grad, gains[0] / gain_one[:, 0], grad_query, grad_key, grad_value, grad_output,
        gains[1] / gain_two[:, 0], grad_gate, grad_up, grad_down,
    )


def solution(mesh):
    fine = Mesh(mesh.devices.reshape(-1, 2, 2, 2, 2), ALL)
    token = P(None, ALL, None)
    row = P(ALL, None)
    vec = P(ALL)
    in_specs = (token, vec, row, row, row, row, vec, row, row, row, P(), token)
    out_specs = (token, token, vec, row, row, row, row, vec, row, row, row)
    return jax.shard_map(local, mesh=fine, in_specs=in_specs, out_specs=out_specs, check_vma=False)
```

time: 6660 us -> 932 us (0.14)
  the two profiles are of different devices: /device:TPU:0 before, /device:TPU:25 now
where the time goes in v1:
time: 932 us; the launch traced here: 926 us
  Pallas kernels  572 us (61%)
  matrix products  109 us (12%)
  local copies, waits for them, and re-layouts  71.4 us (8%)
  other arithmetic  52.7 us (6%)
  starting transfers between devices  51.8 us (6%)
  waiting for transfers between devices  39 us (4%)
  blocking collectives  15.3 us (2%)
  between operations  15.3 us (2%)
    pallas_call x4, Pallas kernels, all_gather16(): pl.pallas_call(ag_kernel, out_shape=jax.ShapeDtypeStruct((16, rows, cols)...  262 us
    pallas_call x4, Pallas kernels, reduce_scatter16(): pl.pallas_call(rs_kernel, out_shape=jax.ShapeDtypeStruct((rows, cols), ou...  245 us
    pallas_call x1, Pallas kernels, attend_back(): pl.pallas_call(attend_back_kernel, grid_spec=spec, out_shape=[jax.ShapeDt...  37.5 us
    dot_general x4, matrix products, outer(): return lax.dot_general(left, right, TN, preferred_element_type=f32)  34.9 us
    all_to_all x5, starting transfers between devices, exchange(): return lax.all_to_all(x, ALL, split_axis=0, concat_axis=0, tiled=True)  29.7 us
    all_to_all x5, waiting for transfers between devices, exchange(): return lax.all_to_all(x, ALL, split_axis=0, concat_axis=0, tiled=True)  27.4 us
    pallas_call x1, Pallas kernels, attend(): pl.pallas_call(attend_kernel, grid_spec=spec, out_shape=[jax.ShapeDtypeSt...  27.1 us
  transfers between devices with their start and end apart: 10, of which 4 were waited for; matrix products, arithmetic and copies ran while one was open for 16% of the time, Pallas kernels for 49%

profile of v1, /device:TPU:25, one launch (start us, length us, event | category | flops | bytes accessed | tf_op | source)
XLA Modules:
  0.0 925.8 jit_solution(3753967919826084728)
XLA Ops:
  12.0 6.2 all-to-all-start
  20.6 1.7 copy.101
  22.4 19.6 %all-to-all-done = bf16[32,64,256]{2,1,0:T(8,128)(2,1)} async-done(((bf16[32,64,256]{2,1,0:T(8,128)(2,1)}), bf16[32,64,256]{2,1,0:T(8,128)(2,1)}, u32[]{:S(2)}, u32[]{:S(2)}) %all-to-all-start) | async-done | bytes 1048608 | tf_op jit(solution)/shard_map/all_to_all | solution.py:360
  42.0 3.3 broadcast_in_dim.29
  45.3 6.2 all-to-all-start.1
  52.3 134.3 %shard_map.203 = bf16[16,128,2048]{2,1,0:T(8,128)(2,1)} custom-call(bf16[128,2048]{1,0:T(8,128)(2,1)S(1)} %fusion.20.x_ref), custom_call_target="tpu_custom_call" | custom-call | tf_op jit(solution)/shard_map/pallas_call | solution.py:112
  186.6 3.2 fusion.29
  189.8 6.0 fusion.38
  195.9 3.5 reshape.308
  199.4 4.2 copy.96
  205.0 2.2 copy.97
  207.1 2.3 add_convert_fusion.1
  212.2 8.9 collective-permute-start
  223.3 49.9 %shard_map.208 = bf16[16,128,2048]{2,1,0:T(8,128)(2,1)} custom-call(bf16[128,2048]{1,0:T(8,128)(2,1)S(1)} %bitcast.157), custom_call_target="tpu_custom_call" | custom-call | tf_op jit(solution)/shard_map/pallas_call | solution.py:112
  273.3 2.0 copy.105.kid_ref
  275.5 15.3 %all_gather.7 = bf16[128,2048]{1,0:T(8,128)(2,1)S(1)} all-gather(bf16[64,2048]{1,0:T(8,128)(2,1)S(1)} %collective-permute-done), channel_id=1, replica_groups=mesh['dp'=2,'z'=2,'y'=2,'c'=2,'x'=2] {'dp'}, dimensions={0}, use_global_device_ids=true | all-gather | bytes 786432 | tf_op jit(solution)/shard_map/all_gather | solution.py:415
  290.8 2.0 fusion.17
  292.9 2.3 fusion.36
  295.2 2.0 copy-done.5
  297.2 27.1 %shard_map.204 = (bf16[2,2,1024,64]{3,2,1,0:T(8,128)(2,1)S(1)}, f32[2,2,1024,1]{3,2,1,0:T(8,128)}) custom-call(s32[2,4]{1,0:T(2,128)S(1)} %convert_reduce_fusion.4.count_ref, bf16[2,2,1024,64]{3,2,1,0:T(8,128)(2,1)S(1)} %copy.98.q_ref, bf16[2,2048,64]{2,1,0:T(8,128)(2,1)S(1)} %get-tuple-element.42.k_ref, bf16[2,2048,64]{2,1,0:T(8,128)(2,1)S(1)} %get-tuple-element.41.v_ref, ...), custom_call_target="tpu_custom_call" | custom-call | tf_op jit(solution)/shard_map/pallas_call | solution.py:270
  326.9 5.6 convolution_convert_fusion.3
  332.5 37.8 %shard_map.205 = f32[128,2048]{1,0:T(8,128)} custom-call(bf16[16,128,2048]{2,1,0:T(8,128)(2,1)} %bitcast.161), custom_call_target="tpu_custom_call" | custom-call | tf_op jit(solution)/shard_map/pallas_call | solution.py:203
  372.0 38.5 %shard_map.206 = bf16[16,128,2048]{2,1,0:T(8,128)(2,1)} custom-call(bf16[128,2048]{1,0:T(8,128)(2,1)S(1)} %multiply_convert_fusion.3.x_ref), custom_call_target="tpu_custom_call" | custom-call | tf_op jit(solution)/shard_map/pallas_call | solution.py:112
  410.5 12.3 %copy.113 = bf16[2048,2048]{1,0:T(8,128)(2,1)} copy(bf16[2048,2048]{0,1:T(8,128)(2,1)} %bitcast.163) | data formatting | bytes 16777216 | tf_op jit(solution)/shard_map/dot_general | solution.py:488
  422.9 2.2 reduce.1
  425.7 13.6 %fusion.8 = f32[2048,1024]{0,1:T(8,128)S(1)} fusion(bf16[2048,2048]{1,0:T(8,128)(2,1)} %bitcast.164, bf16[2048,1536]{1,0:T(8,128)(2,1)} %bitcast.20), kind=kOutput, calls=%fused_computation.19 | convolution fusion | flops 8589934592 | bytes 20971520 | tf_op jit(solution)/shard_map/dot_general | solution.py:452
  439.3 10.3 %fusion.4 = (bf16[2048,512]{0,1:T(8,128)(2,1)S(1)}, bf16[2048,512]{0,1:T(8,128)(2,1)S(1)}, bf16[2048,512]{0,1:T(8,128)(2,1)}) fusion(f32[2048,1024]{0,1:T(8,128)S(1)} %fusion.8, bf16[2048,2048]{1,0:T(8,128)(2,1)} %bitcast.174, bf16[2048,1536]{1,0:T(8,128)(2,1)} %bitcast.20), kind=kOutput, calls=%fused_computation.13 | convolution fusion | flops 4310695936 | bytes 25165824 | tf_op jit(solution)/shard_map/dot_general | solution.py:457
  449.6 14.8 %convolution_convert_fusion.1 = bf16[2048,2048]{1,0:T(8,128)(2,1)} fusion(bf16[2048,1536]{1,0:T(8,128)(2,1)} %bitcast.20, bf16[2048,512]{0,1:T(8,128)(2,1)S(1)} %get-tuple-element.28, bf16[2048,512]{0,1:T(8,128)(2,1)S(1)} %get-tuple-element.27), kind=kOutput, calls=%fused_computation.2 | convolution fusion | flops 8602517504 | bytes 16777216 | tf_op jit(solution)/shard_map/dot_general | solution.py:466
  464.4 37.5 %shard_map.209 = f32[128,2048]{1,0:T(8,128)} custom-call(bf16[16,128,2048]{2,1,0:T(8,128)(2,1)} %bitcast.170), custom_call_target="tpu_custom_call" | custom-call | tf_op jit(solution)/shard_map/pallas_call | solution.py:203
  503.4 1.5 fusion.34.x_ref
  504.9 38.8 %shard_map.210 = bf16[16,128,2048]{2,1,0:T(8,128)(2,1)} custom-call(bf16[128,2048]{1,0:T(8,128)(2,1)S(1)} %fusion.34.x_ref), custom_call_target="tpu_custom_call" | custom-call | tf_op jit(solution)/shard_map/pallas_call | solution.py:112
  543.8 6.5 convolution_convert_fusion.7
  550.3 3.3 reshape.326
  556.3 37.5 %shard_map.211 = (f32[2,2,1024,64]{3,2,1,0:T(8,128)}, f32[2,2048,64]{2,1,0:T(8,128)}, f32[2,2048,64]{2,1,0:T(8,128)}) custom-call(s32[2,4]{1,0:T(2,128)} %copy-done.8, bf16[2,2,1024,64]{3,2,1,0:T(8,128)(2,1)} %copy-done, bf16[2,2,1024,64]{3,2,1,0:T(8,128)(2,1)} %bitcast.168, f32[2,2,1,1024]{3,2,1,0:T(1,128)} %reshape.344.lse_ref, ...), custom_call_target="tpu_custom_call" | custom-call | tf_op jit(solution)/shard_map/pallas_call | solution.py:330
  593.8 1.9 convert.44
  597.8 4.4 all-to-all-start.2
  602.2 9.8 %fusion.10 = bf16[2048,512]{0,1:T(8,128)(2,1)} fusion(bf16[2048,512]{0,1:T(8,128)(2,1)} %get-tuple-element.29, bf16[2048,2048]{1,0:T(8,128)(2,1)} %bitcast.175), kind=kOutput, calls=%fused_computation.29 | convolution fusion | flops 4296015872 | bytes 12582912 | tf_op jit(solution)/shard_map/dot_general | solution.py:488
  612.1 4.0 copy.115
  616.1 5.5 convolution_convert_fusion.6
  621.6 3.4 all-to-all-done.2
  625.0 4.2 all-to-all-start.5
  629.3 1.6 convert_reduce_fusion.2
  631.5 1.8 subtract_convert_fusion
  636.7 3.7 maximum_bitcast_fusion.1
  640.5 3.5 reshape.330
  643.9 6.8 convolution_convert_fusion
  650.8 41.1 %shard_map.212 = f32[128,2048]{1,0:T(8,128)} custom-call(bf16[16,128,2048]{2,1,0:T(8,128)(2,1)} %bitcast.162), custom_call_target="tpu_custom_call" | custom-call | tf_op jit(solution)/shard_map/pallas_call | solution.py:203
  691.9 1.5 fusion.25
  694.2 5.2 all-to-all-start.3
  699.5 6.9 convolution_convert_fusion.5
  706.4 5.8 all-to-all-start.4
  712.2 12.7 %fusion.11 = bf16[32,64,1024]{2,1,0:T(8,128)(2,1)S(1)} fusion(bf16[32,64,2048]{2,1,0:T(8,128)(2,1)} %bitcast.173, bf16[2048,512]{0,1:T(8,128)(2,1)} %copy-done.41, bf16[2048,512]{0,1:T(8,128)(2,1)} %copy-done.40), kind=kOutput, calls=%fused_computation.30 | convolution fusion | flops 8600420352 | bytes 16777216 | tf_op jit(solution)/shard_map/dot_general | solution.py:488
  724.9 3.2 pad_maximum_fusion
  728.1 7.8 all-to-all-done.4
  736.9 6.2 all-to-all-start.6
  744.3 4.2 collective-permute-start.1
  748.5 10.1 %convolution_convert_fusion.2 = bf16[2048,2048]{1,0:T(8,128)(2,1)} fusion(bf16[2048,512]{0,1:T(8,128)(2,1)} %get-tuple-element.29, bf16[2048,1536]{1,0:T(8,128)(2,1)} %bitcast.20), kind=kOutput, calls=%fused_computation.3 | convolution fusion | flops 4299161600 | bytes 12582912 | tf_op jit(solution)/shard_map/dot_general | solution.py:462
  758.6 129.1 %shard_map.207 = f32[128,2048]{1,0:T(8,128)} custom-call(bf16[16,128,2048]{2,1,0:T(8,128)(2,1)} %bitcast.169), custom_call_target="tpu_custom_call" | custom-call | tf_op jit(solution)/shard_map/pallas_call | solution.py:203
  887.7 8.1 collective-permute-done.1
  895.8 3.0 fusion.23
  900.7 1.5 convert_reduce_fusion.1
  906.7 4.7 convert_reduce_fusion
  914.3 2.6 broadcast_multiply_fusion
  916.8 1.9 copy.141
  (172 shorter events, 41.7 us)
Async XLA Ops:
  7.8 2.5 copy-start.32
  10.4 7.9 copy-start.37
  10.4 7.9 copy-start.28
  10.4 7.9 copy-start.29
  12.0 30.0 %all-to-all-start = ((bf16[32,64,256]{2,1,0:T(8,128)(2,1)}), bf16[32,64,256]{2,1,0:T(8,128)(2,1)}, u32[]{:S(2)}, u32[]{:S(2)}) async-start(bf16[32,64,256]{2,1,0:T(8,128)(2,1)} %bitcast.5), calls=%async_computation | async-start | bytes 2097152 | tf_op jit(solution)/shard_map/all_to_all | solution.py:360
  18.3 0.5 copy-start.34
  18.8 1.2 copy-start.30
  45.3 6.5 copy-start.13
  45.3 380.4 %all-to-all-start.1 = ((bf16[32,64,1536]{2,1,0:T(8,128)(2,1)}), bf16[32,64,1536]{2,1,0:T(8,128)(2,1)}, u32[]{:S(2)}, u32[]{:S(2)}) async-start(bf16[32,64,1536]{2,1,0:T(8,128)(2,1)} %bitcast.166), calls=%async_computation.1 | async-start | bytes 12582912 | tf_op jit(solution)/shard_map/all_to_all | solution.py:360
  51.5 241.4 %all-gather.2.cloned.1.call-start = ((), (), s32[]{:S(2)}) async-start(), calls=%async_computation.7 | async-start | bytes 1572864 | tf_op jit(solution)/shard_map/all_gather | solution.py:439
  209.4 1.1 copy-start.10
  209.4 1.7 copy-start.12
  209.4 1.6 copy-start.24
  209.5 2.7 copy-start.39
  209.5 11.7 %copy-start.31 = (s32[2,2048]{1,0:T(2,128)S(1)}, s32[2,2048]{1,0:T(2,128)}, u32[]{:S(2)}) copy-start(s32[2,2048]{1,0:T(2,128)} %param.22) | copy-start | bytes 49156
  210.6 12.8 %copy-start.3 = (bf16[2,64,2048]{2,1,0:T(8,128)(2,1)S(1)}, bf16[2,64,2048]{2,1,0:T(8,128)(2,1)}, u32[]{:S(2)}) copy-start(bf16[2,64,2048]{2,1,0:T(8,128)(2,1)} %param.23) | copy-start | bytes 1572868
  212.2 63.3 %collective-permute-start = (bf16[64,2048]{1,0:T(8,128)(2,1)S(1)}, bf16[64,2048]{1,0:T(8,128)(2,1)S(1)}, u32[]{:S(2)}, u32[]{:S(2)}) collective-permute-start(bf16[64,2048]{1,0:T(8,128)(2,1)S(1)} %copy-done.39), channel_id=1, source_target_pairs={{0,0},{1,16},{2,1},{3,17},{4,2},{5,18},{6,3},{7,19},{8,4},{9,20},{... | collective-permute-start | bytes 786440 | tf_op jit(solution)/shard_map/ppermute | solution.py:415
  273.3 17.5 %copy-start.11 = (bf16[2,3,1024,32]{3,2,0,1:T(8,128)(2,1)S(1)}, bf16[2,3,1024,32]{3,2,0,1:T(8,128)(2,1)}, u32[]{:S(2)}) copy-start(bf16[2,3,1024,32]{3,2,0,1:T(8,128)(2,1)} %copy-done.10) | copy-start | bytes 1179652
  275.5 19.8 %copy-start.8 = (s32[2,4]{1,0:T(2,128)}, s32[2,4]{1,0:T(2,128)S(1)}, u32[]{:S(2)}) copy-start(s32[2,4]{1,0:T(2,128)S(1)} %convert_reduce_fusion.4.count_ref) | copy-start | bytes 100
  290.8 36.1 %copy-start.26 = (bf16[128,2048]{1,0:T(8,128)(2,1)}, bf16[128,2048]{1,0:T(8,128)(2,1)S(1)}, u32[]{:S(2)}) copy-start(bf16[128,2048]{1,0:T(8,128)(2,1)S(1)} %all_gather.7) | copy-start | bytes 1572868
  292.9 31.5 %copy-start = (bf16[2,2,1024,64]{3,2,1,0:T(8,128)(2,1)}, bf16[2,2,1024,64]{3,2,1,0:T(8,128)(2,1)S(1)}, u32[]{:S(2)}) copy-start(bf16[2,2,1024,64]{3,2,1,0:T(8,128)(2,1)S(1)} %copy.98.q_ref) | copy-start | bytes 1572868
  295.2 31.2 %copy-start.1 = (bf16[2,2048,64]{2,1,0:T(8,128)(2,1)}, bf16[2,2048,64]{2,1,0:T(8,128)(2,1)S(1)}, u32[]{:S(2)}) copy-start(bf16[2,2048,64]{2,1,0:T(8,128)(2,1)S(1)} %get-tuple-element.41.v_ref) | copy-start | bytes 1572868
  295.2 31.2 %copy-start.2 = (bf16[2,2048,64]{2,1,0:T(8,128)(2,1)}, bf16[2,2048,64]{2,1,0:T(8,128)(2,1)S(1)}, u32[]{:S(2)}) copy-start(bf16[2,2048,64]{2,1,0:T(8,128)(2,1)S(1)} %get-tuple-element.42.k_ref) | copy-start | bytes 1572868
  295.2 2.0 copy-start.5
  324.3 1.0 copy-start.6
  326.9 5.6 copy-start.15
  332.5 37.9 %copy-start.14 = (bf16[2,64,2048]{2,1,0:T(8,128)(2,1)S(1)}, bf16[2,64,2048]{2,1,0:T(8,128)(2,1)}, u32[]{:S(2)}) copy-start(bf16[2,64,2048]{2,1,0:T(8,128)(2,1)} %param.12) | copy-start | bytes 1572868
  449.6 14.8 %copy-start.40 = (bf16[2048,512]{0,1:T(8,128)(2,1)}, bf16[2048,512]{0,1:T(8,128)(2,1)S(1)}, u32[]{:S(2)}) copy-start(bf16[2048,512]{0,1:T(8,128)(2,1)S(1)} %get-tuple-element.27) | copy-start | bytes 6291460
  449.6 14.8 %copy-start.41 = (bf16[2048,512]{0,1:T(8,128)(2,1)}, bf16[2048,512]{0,1:T(8,128)(2,1)S(1)}, u32[]{:S(2)}) copy-start(bf16[2048,512]{0,1:T(8,128)(2,1)S(1)} %get-tuple-element.28) | copy-start | bytes 6291460
  464.4 39.0 %copy-start.4 = (bf16[2,64,2048]{2,1,0:T(8,128)(2,1)S(1)}, bf16[2,64,2048]{2,1,0:T(8,128)(2,1)}, u32[]{:S(2)}) copy-start(bf16[2,64,2048]{2,1,0:T(8,128)(2,1)} %param.23) | copy-start | bytes 1572868
  504.9 38.8 %copy-start.27 = (bf16[128,2048]{1,0:T(8,128)(2,1)S(1)}, bf16[128,2048]{1,0:T(8,128)(2,1)}, u32[]{:S(2)}) copy-start(bf16[128,2048]{1,0:T(8,128)(2,1)} %copy-done.26) | copy-start | bytes 1572868
  550.3 4.7 copy-start.7
  555.0 1.3 copy-start.18
  593.8 2.2 copy-start.25
  597.8 27.2 %all-to-all-start.2 = ((bf16[2,2,1024,128]{3,2,0,1:T(8,128)(2,1)}), bf16[2,2,1024,128]{3,2,0,1:T(8,128)(2,1)}, u32[]{:S(2)}, u32[]{:S(2)}) async-start(bf16[2,2,1024,128]{3,2,0,1:T(8,128)(2,1)} %copy.120), calls=%async_computation.2 | async-start | bytes 2097152 | tf_op jit(solution)/shard_map/all_to_all | solution.py:478
  612.1 4.1 copy-start.16
  625.0 69.2 %all-to-all-start.5 = ((bf16[2,64,2048]{2,1,0:T(8,128)(2,1)}), bf16[2,64,2048]{2,1,0:T(8,128)(2,1)}, u32[]{:S(2)}, u32[]{:S(2)}) async-start(bf16[2,64,2048]{2,1,0:T(8,128)(2,1)} %bitcast.45), calls=%async_computation.5 | async-start | bytes 1048576 | tf_op jit(solution)/shard_map/all_to_all | solution.py:506
  629.3 2.0 copy-start.20
  629.3 2.0 copy-start.22
  629.3 2.2 copy-start.23
  694.2 12.1 %all-to-all-start.3 = ((f32[32,1,128]{2,1,0:T(1,128)}), f32[32,1,128]{2,1,0:T(1,128)S(1)}, u32[]{:S(2)}, u32[]{:S(2)}) async-start(f32[32,1,128]{2,1,0:T(1,128)} %reshape.355), calls=%async_computation.3 | async-start | bytes 32768 | tf_op jit(solution)/shard_map/all_to_all | solution.py:360
  706.4 29.5 %all-to-all-start.4 = ((bf16[32,64,256]{2,1,0:T(8,128)(2,1)}), bf16[32,64,256]{2,1,0:T(8,128)(2,1)S(1)}, u32[]{:S(2)}, u32[]{:S(2)}) async-start(bf16[32,64,256]{2,1,0:T(8,128)(2,1)} %bitcast.197), calls=%async_computation.4 | async-start | bytes 2097152 | tf_op jit(solution)/shard_map/all_to_all | solution.py:360
  712.2 12.7 %copy-start.19 = (bf16[2048,512]{1,0:T(8,128)(2,1)S(1)}, bf16[2048,512]{1,0:T(8,128)(2,1)}, u32[]{:S(2)}) copy-start(bf16[2048,512]{1,0:T(8,128)(2,1)} %copy.115) | copy-start | bytes 6291460
  735.9 1.0 copy-start.21
  736.9 169.8 %all-to-all-start.6 = ((bf16[32,64,1536]{2,1,0:T(8,128)(2,1)}), bf16[32,64,1536]{2,1,0:T(8,128)(2,1)}, u32[]{:S(2)}, u32[]{:S(2)}) async-start(bf16[32,64,1536]{2,1,0:T(8,128)(2,1)} %pad_maximum_fusion), calls=%async_computation.6 | async-start | bytes 12582912 | tf_op jit(solution)/shard_map/all_to_all | solution.py:360
  744.3 151.5 %collective-permute-start.1 = (f32[64,2048]{1,0:T(8,128)S(1)}, f32[64,2048]{1,0:T(8,128)}, u32[]{:S(2)}, u32[]{:S(2)}) collective-permute-start(f32[64,2048]{1,0:T(8,128)S(1)} %convert_reduce_fusion.3), channel_id=1, source_target_pairs={{0,0},{16,1},{1,2},{17,3},{2,4},{18,5},{3,6},{19,7},{4,8},{20,9},{... | collective-permute-start | bytes 1572872 | tf_op jit(solution)/shard_map/ppermute | solution.py:507
  758.6 137.2 %copy-start.9 = (f32[128,2048]{1,0:T(8,128)S(1)}, f32[128,2048]{1,0:T(8,128)}, u32[]{:S(2)}) copy-start(f32[128,2048]{1,0:T(8,128)} %shard_map.209) | copy-start | bytes 3145732
  758.6 137.2 %copy-start.17 = (f32[128,2048]{1,0:T(8,128)S(1)}, f32[128,2048]{1,0:T(8,128)}, u32[]{:S(2)}) copy-start(f32[128,2048]{1,0:T(8,128)} %shard_map.212) | copy-start | bytes 3145732
  895.8 4.3 copy-start.36
  895.8 4.3 copy-start.38
  902.3 2.7 copy-start.33
  912.8 1.5 copy-start.35
Sparse Core Ops, SparseCore 0:
  212.3 35.7 all-gather.1

commit v2 on v1

v2 whole, which is shorter than its diff:
```python
import functools
import itertools

import jax
import jax.numpy as jnp
from jax import lax
from jax.experimental import pallas as pl
from jax.experimental.pallas import tpu as pltpu
from jax.sharding import Mesh
from jax.sharding import PartitionSpec as P

QUERY_HEADS = 32
KEY_HEADS = 8
HEAD_DIM = 64
TEAM = 16
SCALE = HEAD_DIM ** (-0.5)
epsilon = 1e-05
rope_base = 500000.0
NT = (((1,), (1,)), ((), ()))
TN = (((0,), (0,)), ((), ()))
TEAM_AXES = ("z", "y", "c", "x")
ALL = ("dp",) + TEAM_AXES

DIMS = ("z", "y", "c", "x")
WEIGHT = {"z": 8, "y": 4, "c": 2, "x": 1}
LINKS = ("x", "y", "z")
ORDERS = (("x", "y", "z"), ("y", "z", "x"), ("z", "x", "y"))
MESH = pl.DeviceIdType.MESH


def part_rows(rows):
    tiles = rows // 16
    base = [tiles // 3 + (1 if i < tiles % 3 else 0) for i in range(3)]
    out, at = [], 0
    for b in base:
        out.append((at * 16, b * 16))
        at += b
    return out


def coords():
    return {d: lax.axis_index(d) for d in DIMS}


def slot_of(me, flips=()):
    return sum(((1 - me[d]) if d in flips else me[d]) * WEIGHT[d] for d in DIMS)


def greet(groups, team=True):
    barrier = pltpu.get_barrier_semaphore()
    me = coords()
    group = lax.axis_index("dp")
    if team:
        for d in DIMS:
            pl.semaphore_signal(barrier, inc=1, device_id={d: 1 - me[d]}, device_id_type=MESH)
    for k in range(1, groups):
        pl.semaphore_signal(barrier, inc=1, device_id={"dp": lax.rem(group + k, groups)}, device_id_type=MESH)
    pl.semaphore_wait(barrier, groups - 1 + (len(DIMS) if team else 0))


COST = pl.CostEstimate(flops=30_000_000_000, bytes_accessed=1 << 20, transcendentals=0)


class Errand:
    def __init__(self, array, first, count, own_block):
        self.arrays, self.first, self.count, self.own_block = [array], first, count, own_block
        self.steps = 0

    def outputs(self, groups):
        a = self.arrays[0]
        return [jax.ShapeDtypeStruct((max(groups - 1, 1), self.count, a.shape[-1]), a.dtype)]

    def in_specs(self):
        return [anywhere()]

    def out_specs(self, groups):
        return [anywhere()]

    def scratch(self, groups):
        n = max(1, groups - 1)
        return [pltpu.SemaphoreType.DMA((n,)), pltpu.SemaphoreType.DMA((n,))]

    def bind(self, groups, src, dst, scratch):
        me = lax.axis_index("dp")
        here = pl.ds(self.first, self.count)
        self.copies = []
        for k in range(1, groups):
            peer = lax.rem(me + k, groups)
            self.copies.append(
                pltpu.make_async_remote_copy(
                    src_ref=src[0].at[peer, here] if self.own_block else src[0].at[here],
                    dst_ref=dst[0].at[k - 1], send_sem=scratch[0].at[k - 1], recv_sem=scratch[1].at[k - 1],
                    device_id={"dp": peer}, device_id_type=MESH,
                )
            )

    def step(self, k):
        if k == 0:
            for cp in self.copies:
                cp.start()

    def finish(self):
        for cp in self.copies:
            cp.wait()


class Swap:
    def __init__(self, array, order, far=False):
        self.shape = array.shape[1:]
        self.arrays, self.order, self.far = [array.reshape((2, 2, 2, 2) + self.shape)], order, far
        self.steps = 5

    def outputs(self, groups):
        a = self.arrays[0]
        out = [jax.ShapeDtypeStruct(a.shape, a.dtype)]
        return out + [jax.ShapeDtypeStruct((max(groups - 1, 1),) + a.shape, a.dtype)] * self.far

    def in_specs(self):
        return [vmem()]

    def out_specs(self, groups):
        return [vmem()] + [anywhere()] * self.far

    def scratch(self, groups):
        a = self.arrays[0]
        n = max(1, groups - 1)
        sem = pltpu.SemaphoreType.DMA
        return [pltpu.VMEM(a.shape, a.dtype)] * 3 + [sem((4,)), sem((4,)), sem((4,)), sem((n,)), sem((n,))]

    def bind(self, groups, src, dst, scratch):
        me = coords()
        chain = [src[0], scratch[0], scratch[1], scratch[2], dst[0]]
        ssem, rsem, lsem, fs, fr = scratch[3:]
        self.moves, self.tail = [], []
        for k, d in enumerate(self.order):
            lead = (slice(None),) * DIMS.index(d)
            a, z = chain[k], chain[k + 1]
            self.moves.append(
                (
                    pltpu.make_async_remote_copy(
                        src_ref=a.at[lead + (1 - me[d],)], dst_ref=z.at[lead + (me[d],)], send_sem=ssem.at[k],
                        recv_sem=rsem.at[k], device_id={d: 1 - me[d]}, device_id_type=MESH,
                    ),
                    pltpu.make_async_copy(a.at[lead + (me[d],)], z.at[lead + (me[d],)], lsem.at[k]),
                )
            )
        if self.far:
            group = lax.axis_index("dp")
            for k in range(1, groups):
                self.tail.append(
                    pltpu.make_async_remote_copy(
                        src_ref=dst[0], dst_ref=dst[1].at[k - 1], send_sem=fs.at[k - 1], recv_sem=fr.at[k - 1],
                        device_id={"dp": lax.rem(group + k, groups)}, device_id_type=MESH,
                    )
                )

    def step(self, k):
        if 0 < k <= 4:
            self.moves[k - 1][0].wait_recv()
            self.moves[k - 1][1].wait()
        if k < 4:
            self.moves[k][0].start()
            self.moves[k][1].start()
        if k == 4:
            for cp in self.tail:
                cp.start()

    def finish(self):
        for cp, _ in self.moves:
            cp.wait_send()
        for cp in self.tail:
            cp.wait()


class Runner:
    def __init__(self, jobs):
        self.jobs, self.k = jobs, 0

    def tick(self):
        for job in self.jobs:
            if self.k == 0 or self.k < job.steps:
                job.step(self.k)
        self.k += 1

    def finish(self):
        while self.k < max([1] + [job.steps for job in self.jobs]):
            self.tick()
        for job in self.jobs:
            job.finish()


def anywhere():
    return pl.BlockSpec(memory_space=pl.ANY)


def vmem():
    return pl.BlockSpec(memory_space=pltpu.VMEM)


def call(body, inputs, outputs, scratch, jobs, cid, limit=58):
    groups = lax.axis_size("dp")
    jobs = list(jobs)
    n_in, n_out, n_scratch = len(inputs), len(outputs), len(scratch)
    job_in = [a for job in jobs for a in job.arrays]
    job_out = [job.outputs(groups) for job in jobs]
    job_scratch = [job.scratch(groups) for job in jobs]

    def kernel(*refs):
        def take(n):
            nonlocal refs
            head, refs = refs[:n], refs[n:]
            return head

        ins = take(n_in)
        src = [take(len(job.arrays)) for job in jobs]
        outs = take(n_out)
        dst = [take(len(o)) for o in job_out]
        scr = take(n_scratch)
        own = [take(len(o)) for o in job_scratch]
        greet(groups)
        for job, a, z, m in zip(jobs, src, dst, own):
            job.bind(groups, a, z, m)
        run = Runner(jobs)
        run.tick()
        body(groups, run.tick, *ins, *outs, *scr)
        run.finish()

    out = pl.pallas_call(
        kernel,
        out_shape=list(outputs) + [o for each in job_out for o in each],
        in_specs=[vmem()] * n_in + [p for job in jobs for p in job.in_specs()],
        out_specs=[vmem()] * n_out + [p for job in jobs for p in job.out_specs(groups)],
        scratch_shapes=list(scratch) + [o for each in job_scratch for o in each],
        cost_estimate=COST,
        compiler_params=pltpu.CompilerParams(collective_id=cid, has_side_effects=True, vmem_limit_bytes=limit << 20),
    )(*inputs, *job_in)
    main, rest = out[:n_out], list(out[n_out:])
    got = []
    for o in job_out:
        got.append(tuple(rest[: len(o)]))
        rest = rest[len(o) :]
    return main, got


def ag_kernel(groups, tick, x_ref, g_ref, ssem, rsem, lsem):
    me = coords()
    rows = x_ref.shape[0]
    parts = part_rows(rows)
    mine = slot_of(me)
    local = pltpu.make_async_copy(x_ref, g_ref.at[mine], lsem)
    local.start()
    counter = itertools.count()
    copies = []

    def send(flips, r0, rn, dim, own):
        i = next(counter)
        s = slot_of(me, flips)
        src = x_ref.at[pl.ds(r0, rn)] if own else g_ref.at[s, pl.ds(r0, rn)]
        cp = pltpu.make_async_remote_copy(
            src_ref=src, dst_ref=g_ref.at[s, pl.ds(r0, rn)],
            send_sem=ssem.at[i], recv_sem=rsem.at[i],
            device_id={dim: 1 - me[dim]}, device_id_type=MESH)
        cp.start()
        copies.append(cp)
        return cp

    step1, step2, step3 = {}, {}, {}
    for p, (r0, rn) in enumerate(parts):
        step1[p] = [send((), r0, rn, ORDERS[p][0], True)]
    for p, (r0, rn) in enumerate(parts):
        step2[p] = [send((), r0, rn, ORDERS[p][1], True)]
    for p, (r0, rn) in enumerate(parts):
        step3[p] = [send((), r0, rn, ORDERS[p][2], True)]
    core = [send((), 0, rows, "c", True)]
    tick()
    for p, (r0, rn) in enumerate(parts):
        a, b, c = ORDERS[p]
        step1[p][0].wait_recv()
        step2[p].append(send((a,), r0, rn, b, False))
        step3[p].append(send((a,), r0, rn, c, False))
        core.append(send((a,), r0, rn, "c", False))
    for p, (r0, rn) in enumerate(parts):
        a, b, c = ORDERS[p]
        for cp, fl in zip(step2[p], ((b,), (a, b))):
            cp.wait_recv()
            step3[p].append(send(fl, r0, rn, c, False))
            core.append(send(fl, r0, rn, "c", False))
    tick()
    for p, (r0, rn) in enumerate(parts):
        a, b, c = ORDERS[p]
        for cp, fl in zip(step3[p], ((c,), (a, c), (b, c), (a, b, c))):
            cp.wait_recv()
            core.append(send(fl, r0, rn, "c", False))
    tick()
    for cp in core:
        cp.wait_recv()
    for cp in copies:
        cp.wait_send()
    local.wait()


def all_gather16(x, cid, jobs=()):
    rows, cols = x.shape
    out = call(
        ag_kernel, [x], [jax.ShapeDtypeStruct((TEAM, rows, cols), x.dtype)],
        [pltpu.SemaphoreType.DMA((64,)), pltpu.SemaphoreType.DMA((64,)), pltpu.SemaphoreType.DMA], jobs, cid,
    )
    return out[0][0], out[1]


FULL = list(itertools.product((0, 1), repeat=3))


def flips_of(bits, order):
    return tuple(d for b, d in zip(bits, order) if b)


def add_rows(dst, a, b, r0, rn):
    def body(i, _):
        r = pl.multiple_of(r0 + i * 16, 16)
        dst[pl.ds(r, 16)] = (a[pl.ds(r, 16)].astype(jnp.float32) + b[pl.ds(r, 16)].astype(jnp.float32)).astype(dst.dtype)
        return 0
    lax.fori_loop(0, rn // 16, body, 0)


def matmul_scatter_kernel(flip, groups, tick, a_ref, w_ref, o_ref, part, acc, cbuf, b1, b2, b3, ssem, rsem):
    me = coords()
    rows, cols = o_ref.shape
    parts = part_rows(rows)
    counter = itertools.count()
    copies = []

    def send(src, dst, dim):
        i = next(counter)
        cp = pltpu.make_async_remote_copy(
            src_ref=src, dst_ref=dst, send_sem=ssem.at[i], recv_sem=rsem.at[i],
            device_id={dim: 1 - me[dim]}, device_id_type=MESH)
        cp.start()
        copies.append(cp)
        return cp

    def product(slot, dst):
        def column(j, _):
            here = pl.ds(pl.multiple_of(j * 512, 512), 512)
            if flip:
                out = lax.dot_general(a_ref[slot], w_ref[here, :], NT, preferred_element_type=jnp.float32)
            else:
                out = jnp.dot(a_ref[slot], w_ref[:, here], preferred_element_type=jnp.float32)
            dst[:, here] = out.astype(dst.dtype)
            return 0
        lax.fori_loop(0, cols // 512, column, 0)

    def key(flips):
        return sum((1 << i) for i, d in enumerate(LINKS) if d in flips)

    order0 = [(1, 1, 1), (0, 1, 1), (1, 0, 1), (1, 1, 0), (1, 0, 0), (0, 1, 0), (0, 0, 1), (0, 0, 0)]
    core = {}
    for bits in order0:
        fl = flips_of(bits, LINKS)
        product(slot_of(me, fl + ("c",)), part.at[key(fl)])
        core[fl] = send(part.at[key(fl)], cbuf.at[key(fl)], "c")
    s1 = {p: {} for p in range(3)}
    tick()
    for bits in order0:
        fl = flips_of(bits, LINKS)
        k = key(fl)
        product(slot_of(me, fl), acc.at[k])
        core[fl].wait_recv()
        add_rows(acc.at[k], acc.at[k], cbuf.at[k], 0, rows)
        for p, (r0, rn) in enumerate(parts):
            a, b, c = ORDERS[p]
            if a in fl:
                rest = tuple(d for d in fl if d != a)
                j = (1 if b in fl else 0) + (2 if c in fl else 0)
                s1[p][rest] = send(acc.at[k, pl.ds(r0, rn)], b1.at[j, pl.ds(r0, rn)], a)
    tick()
    s2 = {p: {} for p in range(3)}
    for (bb, cc) in ((1, 1), (1, 0), (0, 1), (0, 0)):
        for p, (r0, rn) in enumerate(parts):
            a, b, c = ORDERS[p]
            fl = flips_of((bb, cc), (b, c))
            match = [q for q in s1[p] if set(q) == set(fl)][0]
            s1[p][match].wait_recv()
            k = key(fl)
            add_rows(acc.at[k], acc.at[k], b1.at[bb + 2 * cc], r0, rn)
            if bb:
                s2[p][cc] = send(acc.at[k, pl.ds(r0, rn)], b2.at[cc, pl.ds(r0, rn)], b)
    tick()
    s3 = {}
    for cc in (1, 0):
        for p, (r0, rn) in enumerate(parts):
            a, b, c = ORDERS[p]
            s2[p][cc].wait_recv()
            k = key((c,) if cc else ())
            add_rows(acc.at[k], acc.at[k], b2.at[cc], r0, rn)
            if cc:
                s3[p] = send(acc.at[k, pl.ds(r0, rn)], b3.at[pl.ds(r0, rn)], c)
    for p, (r0, rn) in enumerate(parts):
        s3[p].wait_recv()
        add_rows(o_ref, acc.at[0], b3, r0, rn)
    for cp in copies:
        cp.wait_send()


def matmul_scatter16(a, w, flip, cid, jobs=()):
    _, rows, _ = a.shape
    cols = w.shape[0] if flip else w.shape[1]
    bf16 = jnp.bfloat16
    out = call(
        functools.partial(matmul_scatter_kernel, flip), [a, w], [jax.ShapeDtypeStruct((rows, cols), jnp.float32)],
        [
            pltpu.VMEM((8, rows, cols), bf16), pltpu.VMEM((8, rows, cols), bf16), pltpu.VMEM((8, rows, cols), bf16),
            pltpu.VMEM((4, rows, cols), bf16), pltpu.VMEM((2, rows, cols), bf16), pltpu.VMEM((rows, cols), bf16),
            pltpu.SemaphoreType.DMA((32,)), pltpu.SemaphoreType.DMA((32,)),
        ],
        jobs, cid,
    )
    return out[0][0], out[1]


NEG = -1e30
CHUNK = 256
SLOTS = 4
CUTS = (5, 5, 6)
BACK_CUTS = (5, 4, 7)
SWAP_ORDERS = (("x", "y", "z", "c"), ("y", "z", "x", "c"), ("z", "x", "y", "c"))


def swapped(v):
    lane = lax.broadcasted_iota(jnp.int32, v.shape, 1)
    low = lax.rem(lane, HEAD_DIM) < HEAD_DIM // 2
    return jnp.where(low, pltpu.roll(v, 128 - HEAD_DIM // 2, 1), pltpu.roll(v, HEAD_DIM // 2, 1))


def low_lanes(shape):
    return lax.broadcasted_iota(jnp.int32, shape, 1) < HEAD_DIM


def as_row(column):
    return jnp.transpose(jnp.broadcast_to(column, (column.shape[0], 128)))[0:1]


def attend_kernel(groups, tick, h_ref, w_ref, cos_ref, sin_ref, idc_ref, idr_ref, q_ref, kv_ref, o_ref, lse_ref, top, total, acc, ssem, rsem):
    me = lax.axis_index("dp")
    tokens = cos_ref.shape[1]
    span = TEAM * tokens
    steps = span // CHUNK
    heads = q_ref.shape[0]

    def project(g, _):
        raw = jnp.dot(h_ref[g], w_ref[...], preferred_element_type=jnp.float32)
        cos = jnp.concatenate([cos_ref[g]] * 2, axis=0)
        sin = jnp.concatenate([sin_ref[g]] * 2, axis=0)
        qp, kvp = raw[:, :128], raw[:, 128:]
        qp = qp * cos[:, :128] + swapped(qp) * sin[:, :128]
        kvp = kvp * cos[:, 128:] + swapped(kvp) * sin[:, 128:]
        low = low_lanes(qp.shape)
        q_ref[0, g] = jnp.where(low, qp, 0.0).astype(jnp.bfloat16)
        q_ref[1, g] = jnp.where(low, pltpu.roll(qp, HEAD_DIM, 1), 0.0).astype(jnp.bfloat16)
        kv_ref[me, g] = kvp.astype(jnp.bfloat16)
        return 0

    lax.fori_loop(0, TEAM, project, 0)
    copies = []
    for k in range(1, groups):
        copies.append(
            pltpu.make_async_remote_copy(
                src_ref=kv_ref.at[me], dst_ref=kv_ref.at[me], send_sem=ssem.at[k - 1], recv_sem=rsem.at[k - 1],
                device_id={"dp": lax.rem(me + k, groups)}, device_id_type=MESH,
            )
        )
        copies[-1].start()
    for k in range(groups):
        p = lax.rem(me + groups - k, groups)
        if k > 0:
            copies[k - 1].wait_recv()
        for s in range(2):
            kv = kv_ref[p, :, s * tokens : (s + 1) * tokens, :].reshape(span, 128)
            kid = idr_ref[s, :, pl.ds(pl.multiple_of(p * span, 128), span)]

            def block(i, _, s=s, kv=kv, kid=kid, k=k):
                at = s * steps + i
                q = q_ref[:, pl.ds(i * SLOTS, SLOTS), s * tokens : (s + 1) * tokens, :].reshape(heads * CHUNK, 128)
                qid = idc_ref[s, pl.ds(pl.multiple_of(i * CHUNK, CHUNK), CHUNK), :]
                qid = jnp.concatenate([qid] * heads, axis=0)
                scores = lax.dot_general(q, kv, NT, preferred_element_type=jnp.float32)
                scores = jnp.where(kid <= qid, scores, NEG)
                peak = jnp.max(scores, axis=-1, keepdims=True)
                if k > 0:
                    old = top[at]
                    peak = jnp.maximum(old, peak)
                weight = jnp.exp(scores - peak)
                summed = jnp.sum(weight, axis=-1, keepdims=True)
                mixed = jnp.dot(weight.astype(jnp.bfloat16), kv, preferred_element_type=jnp.float32)
                if k > 0:
                    factor = jnp.exp(old - peak)
                    summed = summed + total[at] * factor
                    mixed = mixed + acc[at] * factor
                if k < groups - 1:
                    top[at] = peak
                    total[at] = summed
                    acc[at] = mixed
                else:
                    mixed = mixed / summed
                    first, second = mixed[:CHUNK], mixed[CHUNK:]
                    out = jnp.where(low_lanes(first.shape), pltpu.roll(first, HEAD_DIM, 1), second)
                    o_ref[pl.ds(i * SLOTS, SLOTS), s * tokens : (s + 1) * tokens, :] = out.astype(jnp.bfloat16).reshape(SLOTS, tokens, 128)
                    lse_ref[at] = as_row(peak + jnp.log(summed))
                return 0

            lax.fori_loop(0, steps, block, 0)
            tick()
    for cp in copies:
        cp.wait_send()


def attend(groups, h, w, cos, sin, idc, idr, cid, jobs=()):
    tokens = cos.shape[1]
    rows = 2 * tokens
    blocks = 2 * TEAM * tokens // CHUNK
    peers = max(groups - 1, 1)
    f32, bf16 = jnp.float32, jnp.bfloat16
    out = call(
        attend_kernel, [h, w, cos, sin, idc, idr],
        [
            jax.ShapeDtypeStruct((2, TEAM, rows, 128), bf16),
            jax.ShapeDtypeStruct((groups, TEAM, rows, 128), bf16),
            jax.ShapeDtypeStruct((TEAM, rows, 128), bf16),
            jax.ShapeDtypeStruct((blocks, 1, 2 * CHUNK), f32),
        ],
        [
            pltpu.VMEM((blocks, 2 * CHUNK, 1), f32), pltpu.VMEM((blocks, 2 * CHUNK, 1), f32),
            pltpu.VMEM((blocks, 2 * CHUNK, 128), f32),
            pltpu.SemaphoreType.DMA((peers,)), pltpu.SemaphoreType.DMA((peers,)),
        ],
        jobs, cid,
    )
    return out


def attend_back_kernel(groups, tick, dm_ref, wo_ref, q_ref, kv_ref, o_ref, lse_ref, cos_ref, sin_ref, idc_ref, idr_ref, d_ref, do, gz, delta, dq, dkv, out_buf, in_buf, ssem, rsem):
    me = lax.axis_index("dp")
    tokens = cos_ref.shape[1]
    span = TEAM * tokens
    steps = span // CHUNK
    f32, bf16 = jnp.float32, jnp.bfloat16

    def project(g, _):
        part = lax.dot_general(dm_ref[g], wo_ref[...], NT, preferred_element_type=f32).astype(bf16)
        do[g] = part
        part = part.astype(f32)
        low = low_lanes(part.shape)
        gz[0, g] = jnp.where(low, 0.0, pltpu.roll(part, HEAD_DIM, 1)).astype(bf16)
        gz[1, g] = jnp.where(low, 0.0, part).astype(bf16)
        return 0

    lax.fori_loop(0, TEAM, project, 0)
    for s in range(2):

        def deltas(i, _, s=s):
            here = (pl.ds(i * SLOTS, SLOTS), slice(s * tokens, (s + 1) * tokens), slice(None))
            both = do[here].reshape(CHUNK, 128).astype(f32) * o_ref[here].reshape(CHUNK, 128).astype(f32)
            low = low_lanes(both.shape)
            first = jnp.sum(jnp.where(low, both, 0.0), axis=-1, keepdims=True)
            second = jnp.sum(jnp.where(low, 0.0, both), axis=-1, keepdims=True)
            delta[s * steps + i] = as_row(jnp.concatenate([first, second], axis=0))
            return 0

        lax.fori_loop(0, steps, deltas, 0)
    copies = []
    order = list(range(1, groups)) + [0]
    for turn, k in enumerate(order):
        p = lax.rem(me + k, groups)
        for s in range(2):
            kv = kv_ref[p, :, s * tokens : (s + 1) * tokens, :].reshape(span, 128)
            kid = idc_ref[s, pl.ds(pl.multiple_of(p * span, span), span), :]

            def block(i, _, s=s, kv=kv, kid=kid, turn=turn):
                at = s * steps + i
                here = (slice(None), pl.ds(i * SLOTS, SLOTS), slice(s * tokens, (s + 1) * tokens), slice(None))
                q = q_ref[here].reshape(2 * CHUNK, 128)
                g = gz[here].reshape(2 * CHUNK, 128)
                qid = idr_ref[s, :, pl.ds(pl.multiple_of(i * CHUNK, CHUNK), CHUNK)]
                qid = jnp.concatenate([qid] * 2, axis=1)
                scores = lax.dot_general(kv, q, NT, preferred_element_type=f32)
                prob = jnp.where(kid <= qid, jnp.exp(scores - lse_ref[at]), 0.0)
                dp = lax.dot_general(kv, g, NT, preferred_element_type=f32)
                ds = (prob * (dp - delta[at])).astype(bf16)
                part = jnp.dot(ds, q, preferred_element_type=f32)
                part = part + jnp.dot(prob.astype(bf16), g, preferred_element_type=f32)
                dkv[s] = dkv[s] + part
                mine = lax.dot_general(ds, kv, TN, preferred_element_type=f32)
                if turn == 0:
                    dq[at] = mine
                else:
                    dq[at] = dq[at] + mine
                return 0

            dkv[s] = jnp.zeros((span, 128), f32)
            lax.fori_loop(0, steps, block, 0)
            tick()
            if k > 0:
                out_buf[k - 1, :, s * tokens : (s + 1) * tokens, :] = dkv[s].astype(bf16).reshape(TEAM, tokens, 128)
        if k > 0:
            copies.append(
                pltpu.make_async_remote_copy(
                    src_ref=out_buf.at[k - 1], dst_ref=in_buf.at[k - 1], send_sem=ssem.at[k - 1], recv_sem=rsem.at[k - 1],
                    device_id={"dp": p}, device_id_type=MESH,
                )
            )
            copies[-1].start()
    for cp in copies:
        cp.wait_recv()
    for s in range(2):

        def finish(i, _, s=s):
            here = (pl.ds(i * SLOTS, SLOTS), slice(s * tokens, (s + 1) * tokens), slice(None))
            cos = cos_ref[pl.ds(i * SLOTS, SLOTS)].reshape(CHUNK, 256)
            sin = sin_ref[pl.ds(i * SLOTS, SLOTS)].reshape(CHUNK, 256)
            both = dq[s * steps + i]
            first, second = both[:CHUNK], both[CHUNK:]
            qp = jnp.where(low_lanes(first.shape), first, pltpu.roll(second, HEAD_DIM, 1))
            kvp = dkv[s, pl.ds(pl.multiple_of(i * CHUNK, CHUNK), CHUNK), :]
            for k in range(1, groups):
                kvp = kvp + in_buf[(k - 1,) + here].reshape(CHUNK, 128).astype(f32)
            qp = qp * cos[:, :128] - swapped(qp) * sin[:, :128]
            kvp = kvp * cos[:, 128:] - swapped(kvp) * sin[:, 128:]
            both = jnp.concatenate([qp, kvp], axis=1).astype(bf16)
            d_ref[here] = both.reshape(SLOTS, tokens, 256)
            return 0

        lax.fori_loop(0, steps, finish, 0)
    for cp in copies:
        cp.wait_send()


def attend_back(groups, dm, wo, q, kv, o, lse, cos, sin, idc, idr, cid, jobs=()):
    tokens = cos.shape[1]
    rows = 2 * tokens
    span = TEAM * tokens
    blocks = 2 * span // CHUNK
    peers = max(groups - 1, 1)
    f32, bf16 = jnp.float32, jnp.bfloat16
    out = call(
        attend_back_kernel, [dm, wo, q, kv, o, lse, cos, sin, idc, idr], [jax.ShapeDtypeStruct((TEAM, rows, 256), bf16)],
        [
            pltpu.VMEM((TEAM, rows, 128), bf16), pltpu.VMEM((2, TEAM, rows, 128), bf16),
            pltpu.VMEM((blocks, 1, 2 * CHUNK), f32), pltpu.VMEM((blocks, 2 * CHUNK, 128), f32),
            pltpu.VMEM((2, span, 128), f32),
            pltpu.VMEM((peers, TEAM, rows, 128), bf16), pltpu.VMEM((peers, TEAM, rows, 128), bf16),
            pltpu.SemaphoreType.DMA((peers,)), pltpu.SemaphoreType.DMA((peers,)),
        ],
        jobs, cid,
    )
    return out[0][0], out[1]


def rotation_tables(positions):
    half = HEAD_DIM // 2
    freqs = rope_base ** (-jnp.arange(half, dtype=jnp.float32) * 2.0 / HEAD_DIM)
    angles = positions.astype(jnp.float32)[:, None] * freqs[None, :]
    cos, sin = jnp.cos(angles), jnp.sin(angles)
    one, none = jnp.ones_like(cos), jnp.zeros_like(cos)
    c = jnp.concatenate([cos * SCALE] * 4 + [cos, cos, one, one], axis=-1)
    s = jnp.concatenate([-sin * SCALE, sin * SCALE] * 2 + [-sin, sin, none, none], axis=-1)
    return c.reshape(TEAM, -1, 256), s.reshape(TEAM, -1, 256)


def norm_back(grad, normed, scale):
    return scale * (grad - normed * jnp.mean(grad * normed, axis=-1, keepdims=True))


def after(x, *others):
    return lax.optimization_barrier((x,) + others)[0]


def local(
    layer_input, attn_gain, query_weight, key_matrix, value_matrix, output_weight, ffn_gain,
    gate_weight, up_weight, down_weight, block_ids, cotangent,
):
    f32, bf16 = jnp.float32, jnp.bfloat16
    seqs, tokens, model = layer_input.shape
    rows = seqs * tokens
    groups = lax.axis_size("dp")
    group = lax.axis_index("dp")
    devices = groups * TEAM
    share = query_weight.shape[0]
    span = TEAM * tokens
    heads = QUERY_HEADS // TEAM
    ff = gate_weight.shape[1] // TEAM
    twin = TEAM // KEY_HEADS

    gain_one = attn_gain.astype(f32)[:, None]
    gain_two = ffn_gain.astype(f32)[:, None]

    def scaled(weight, gain):
        return (weight.astype(f32) * gain).astype(bf16)

    def doubled(weight):
        split = weight.reshape(share, KEY_HEADS, 1, HEAD_DIM)
        return jnp.broadcast_to(split, (share, KEY_HEADS, twin, HEAD_DIM)).reshape(share, TEAM, HEAD_DIM)

    def deal(k):
        return [(j, ((j + k) % groups) * TEAM + j // groups) for j in range(devices)]

    pack_q = jnp.moveaxis(scaled(query_weight, gain_one).reshape(share, TEAM, heads * HEAD_DIM), 1, 0)
    pack_kv = jnp.concatenate(
        [doubled(scaled(key_matrix, gain_one)), doubled(scaled(value_matrix, gain_one))], axis=-1
    )
    pack_kv = jnp.moveaxis(pack_kv, 1, 0)

    def in_order(mine, far):
        mine = mine.reshape(TEAM * share, -1)
        far = far.reshape((-1,) + mine.shape)
        if groups == 1:
            return mine
        if groups == 2:
            first = group == 0
            return jnp.concatenate([jnp.where(first, mine, far[0]), jnp.where(first, far[0], mine)])
        blocks = jnp.concatenate([mine[None], far])
        return jnp.take(blocks, lax.rem(group - jnp.arange(groups) + groups, groups), axis=0).reshape(model, -1)

    x = layer_input.reshape(rows, model).astype(f32)
    norm_one = lax.rsqrt(jnp.mean(x * x, axis=-1, keepdims=True) + epsilon)
    normed_one = x * norm_one
    c_own = cotangent.reshape(rows, model)
    h_one, (w_q, w_kv) = all_gather16(
        normed_one.astype(bf16), 1, [Swap(pack_q, ("x", "y", "z", "c"), True), Swap(pack_kv, ("y", "z", "x", "c"), True)]
    )
    w_in = jnp.concatenate([in_order(*w_q), in_order(*w_kv)], axis=-1)

    dealt = jnp.stack([lax.ppermute(output_weight, ALL, deal(k)) for k in range(groups)])
    if groups > 1:
        dealt = jnp.take(dealt, lax.rem(group - jnp.arange(groups) + groups, groups), axis=0)
    w_out = dealt.reshape(-1, model)

    pack_gate = jnp.moveaxis(scaled(gate_weight, gain_two).reshape(share, TEAM, ff), 1, 0)
    pack_up = jnp.moveaxis(scaled(up_weight, gain_two).reshape(share, TEAM, ff), 1, 0)
    pack_down = jnp.moveaxis(down_weight.reshape(share, TEAM, ff), 1, 0)
    packs = list(zip((pack_gate, pack_up, pack_down), SWAP_ORDERS))

    def errands(pair, first, count, own_block):
        return [Errand(a, first * share, count * share, own_block) for a in pair]

    cos, sin = rotation_tables(group * span + jnp.arange(span, dtype=jnp.int32))
    ids = lax.dynamic_slice_in_dim(block_ids, group * span, span, 1)
    (q, kv, o, lse), own = attend(
        groups, h_one, w_in, cos, sin, ids[:, :, None], block_ids[:, None, :], 3, [Swap(a, order) for a, order in packs]
    )
    own = [a[0].reshape(TEAM * share, ff) for a in own]
    branch, far_a = matmul_scatter16(o, w_out, False, 4, errands(own, 0, CUTS[0], False))
    middle = x + branch
    norm_two = lax.rsqrt(jnp.mean(middle * middle, axis=-1, keepdims=True) + epsilon)
    normed_two = middle * norm_two
    h_two, far_b = all_gather16(normed_two.astype(bf16), 9, errands(own, CUTS[0], CUTS[1], False))
    c_all, far_c = all_gather16(after(c_own, h_two), 10, errands(own, CUTS[0] + CUTS[1], CUTS[2], False))

    w_gate, w_up, w_down = [
        in_order(own[i], jnp.concatenate([far_a[i][0], far_b[i][0], far_c[i][0]], axis=1)) for i in range(3)
    ]
    w_gate_up = jnp.concatenate([w_gate, w_up], axis=-1)
    c_flat, h_flat = c_all.reshape(-1, model), h_two.reshape(-1, model)
    gate_up = jnp.dot(h_flat, w_gate_up, preferred_element_type=f32)
    gate, up = gate_up[:, :ff], gate_up[:, ff:]
    sig = jax.nn.sigmoid(gate)
    silu = gate * sig
    active = (silu * up).astype(bf16)
    da = jnp.dot(c_flat, w_down, preferred_element_type=f32)
    d_gate_up = jnp.concatenate(
        [(da * up * sig * (1.0 + gate * (1.0 - sig))).astype(bf16), (da * silu).astype(bf16)], axis=-1
    )

    def outer(left, right):
        return lax.dot_general(left, right, TN, preferred_element_type=f32)

    def by_group(piece):
        return piece.astype(bf16).reshape(groups, TEAM * share, -1)

    g_all = [by_group(outer(h_flat, d_gate_up[:, :ff])), by_group(outer(h_flat, d_gate_up[:, ff:])), by_group(outer(c_flat, active))]
    dn_two, sum_a = matmul_scatter16(
        d_gate_up.reshape(TEAM, rows, 2 * ff), w_gate_up, True, 5, errands(g_all, 0, BACK_CUTS[0], True)
    )
    middle_grad = c_own.astype(f32) + norm_back(dn_two, normed_two, norm_two)
    middle_low, sum_b = all_gather16(middle_grad.astype(bf16), 11, errands(g_all, BACK_CUTS[0], BACK_CUTS[1], True))
    w_part = outer(o.reshape(-1, heads * HEAD_DIM), middle_low.reshape(-1, model)).astype(bf16).reshape(groups, -1, model)
    d_in, sum_c = attend_back(
        groups, middle_low, w_out, q, kv, o, lse, cos, sin, block_ids[:, :, None], ids[:, None, :], 6,
        errands(g_all, BACK_CUTS[0] + BACK_CUTS[1], BACK_CUTS[2], True),
    )

    def summed(mine, *far):
        total = lax.dynamic_index_in_dim(mine, group, 0, keepdims=False).astype(f32)
        far = jnp.concatenate([a[0] for a in far], axis=1)
        for k in range(groups - 1):
            total = total + far[k].astype(f32)
        return total.astype(bf16).reshape(TEAM, share, -1)

    def home(piece):
        return jnp.moveaxis(piece[0].reshape(TEAM, share, -1).astype(f32), 0, 1)

    parts = [summed(g_all[i], sum_a[i], sum_b[i], sum_c[i]) for i in range(3)]
    d_flat = d_in.reshape(-1, d_in.shape[-1])
    attn = by_group(outer(h_one.reshape(-1, model), d_flat))
    dn_one, got = matmul_scatter16(
        d_in, w_in, True, 7,
        [Swap(a, order) for a, order in zip(parts, SWAP_ORDERS)] + errands([attn], 0, TEAM, True),
    )
    input_grad = (middle_grad + norm_back(dn_one, normed_one, norm_one)).reshape(seqs, tokens, model)
    gate_home, up_home, down_home = got[:3]
    attn = summed(attn, got[3])
    pieces = []
    for k in range(groups):
        pick = lax.rem(group + groups - k, groups) if groups > 1 else 0
        mine = lax.dynamic_index_in_dim(w_part, pick, 0, keepdims=False)
        pieces.append(lax.ppermute(mine, ALL, [(b, a) for a, b in deal(k)]).astype(f32))
    grad_output = sum(pieces)
    gains = jnp.stack(
        [jnp.sum(normed_one * dn_one, axis=0), jnp.sum(normed_two * dn_two, axis=0)], axis=0
    )
    gains = gains.reshape(2, groups, TEAM, share).transpose(2, 1, 0, 3).reshape(TEAM, 2 * groups, share)
    gains = jnp.pad(gains, ((0, 0), (0, -2 * groups % 8), (0, -share % 128)))
    cut = heads * HEAD_DIM
    produced, got = matmul_scatter16(
        active.reshape(TEAM, rows, ff), w_down, True, 8,
        [
            Swap(attn[..., :cut], ("x", "y", "z", "c")), Swap(attn[..., cut:], ("y", "z", "x", "c")),
            Swap(gains, ("z", "x", "y", "c"), True),
        ],
    )
    layer_output = (middle + produced).reshape(seqs, tokens, model)
    total = jnp.sum(got[2][0].reshape((TEAM,) + gains.shape[1:]), axis=0)
    if groups > 1:
        total = total + jnp.sum(got[2][1].reshape((-1,) + gains.shape[1:]), axis=0)
    gains = lax.dynamic_slice_in_dim(total, 2 * group, 2, 0)[:, :share]

    grad_gate = home(gate_home).reshape(share, -1) * gain_two
    grad_up = home(up_home).reshape(share, -1) * gain_two
    grad_down = home(down_home).reshape(share, -1)
    grad_query = home(got[0]).reshape(share, -1) * gain_one
    pair = home(got[1]).reshape(share, KEY_HEADS, twin, 2, HEAD_DIM).sum(axis=2)
    grad_key = pair[:, :, 0].reshape(share, -1) * gain_one
    grad_value = pair[:, :, 1].reshape(share, -1) * gain_one
    return (
        layer_output, input_grad, gains[0] / gain_one[:, 0], grad_query, grad_key, grad_value, grad_output,
        gains[1] / gain_two[:, 0], grad_gate, grad_up, grad_down,
    )


def solution(mesh):
    fine = Mesh(mesh.devices.reshape(-1, 2, 2, 2, 2), ALL)
    token = P(None, ALL, None)
    row = P(ALL, None)
    vec = P(ALL)
    in_specs = (token, vec, row, row, row, row, vec, row, row, row, P(), token)
    out_specs = (token, token, vec, row, row, row, row, vec, row, row, row)
    return jax.shard_map(local, mesh=fine, in_specs=in_specs, out_specs=out_specs, check_vma=False)
```

time: 932 us -> 874 us (0.938)
  the two profiles are of different devices: /device:TPU:25 before, /device:TPU:0 now
where the time goes in v2:
time: 874 us; the launch traced here: 863 us
  Pallas kernels  686 us (78%)
  other arithmetic  68.7 us (8%)
  matrix products  62.7 us (7%)
  local copies, waits for them, and re-layouts  32.9 us (4%)
  starting transfers between devices  10.2 us (1%)
    pallas_call x10, Pallas kernels, call(): pl.pallas_call(kernel, out_shape=list(outputs) + [o for each in job_out f...  686 us
    dot_general x5, matrix products, outer(): return lax.dot_general(left, right, TN, preferred_element_type=f32)  29 us
    dot_general x1, matrix products, local(): gate_up = jnp.dot(h_flat, w_gate_up, preferred_element_type=f32)  24.5 us
    concatenate x1, other arithmetic, local(): w_gate_up = jnp.concatenate([w_gate, w_up], axis=-1)  17.9 us
  transfers between devices with their start and end apart: 4, of which 0 were waited for; matrix products, arithmetic and copies ran while one was open for 6% of the time, Pallas kernels for 22%

profile of v2, /device:TPU:0, one launch (start us, length us, event | category | flops | bytes accessed | tf_op | source)
XLA Modules:
  0.0 862.6 jit_solution(1803207078827032941)
XLA Ops:
  0.7 3.7 collective-permute-start
  4.4 2.9 collective-permute-start.1
  7.3 1.3 broadcast_in_dim.53.refs_5_
  10.7 1.0 multiply_convert_fusion.8
  12.0 2.0 copy_bitcast_fusion.3
  14.2 1.0 fusion.5.refs_0_
  15.2 1.3 copy.95.refs_4_
  17.1 1.1 copy.128
  18.2 1.1 copy.127
  19.2 1.1 copy.126
  20.4 0.9 pad_maximum_fusion.3
  21.3 3.1 multiply_sine_fusion
  24.4 70.6 %shard_map.203 = (bf16[16,128,2048]{2,1,0:T(8,128)(2,1)}, bf16[2,2,2,2,64,128]{5,4,3,2,1,0:T(8,128)(2,1)}, bf16[1,2,2,2,2,64,128]{6,5,4,3,2,1,0:T(8,128)(2,1)}, ...) custom-call(bf16[128,2048]{1,0:T(8,128)(2,1)} %fusion.5.refs_0_, ...), custom_call_target="tpu_custom_call" | custom-call | flops 30000001024 | bytes 1048576 | tf_op jit(solution)/shard_map/pallas_call | solution.py:228
  95.1 3.7 concatenate.65.refs_2_.refs_6_
  98.8 1.3 bitcast_select_fusion.2
  100.1 1.1 maximum_maximum_fusion.1.refs_1_
  101.3 3.7 concatenate.67.refs_3_.refs_7_
  105.0 67.1 %shard_map.204 = (bf16[2,16,128,128]{3,2,1,0:T(8,128)(2,1)}, bf16[2,16,128,128]{3,2,1,0:T(8,128)(2,1)}, bf16[16,128,128]{2,1,0:T(8,128)(2,1)}, f32[8,1,512]{2,1,...) custom-call(bf16[16,128,2048]{2,1,0:T(8,128)(2,1)} %get-tuple-elemen, ...), custom_call_target="tpu_custom_call" | custom-call | flops 30000001024 | bytes 1048576 | tf_op jit(solution)/shard_map/pallas_call | solution.py:228
  172.9 2.0 copy.98.refs_8_
  174.9 1.1 pad_maximum_fusion.2
  176.6 0.9 bitcast_select_fusion.refs_1_
  177.5 56.3 %shard_map.205 = (f32[128,2048]{1,0:T(8,128)}, bf16[1,320,512]{2,1,0:T(8,128)(2,1)}, bf16[1,320,512]{2,1,0:T(8,128)(2,1)}, bf16[1,320,512]{2,1,0:T(8,128)(2,1)}) custom-call(bf16[16,128,128]{2,1,0:T(8,128)(2,1)} %get-tuple-element.63.refs_0_.refs_4_, bf16[128,2048]{1,0:T(8,128)(2,1)} %bitcast_select_fusion.refs_1_, bf16[1024,512]{1,0:T(8,128)(2,1)} %bitcast.218, ...), custom_call_target="tpu_custom_call" | custom-call | flops 30000001024 | bytes 1048576 | tf_op jit(solution)/shard_map/pallas_call | solution.py:228
  233.7 1.4 multiply_reduce_fusion
  235.2 0.9 copy-done
  236.2 0.9 multiply_convert_fusion.5.refs_0_
  237.1 62.7 %shard_map.206 = (bf16[16,128,2048]{2,1,0:T(8,128)(2,1)}, bf16[1,320,512]{2,1,0:T(8,128)(2,1)}, bf16[1,320,512]{2,1,0:T(8,128)(2,1)}, bf16[1,320,512]{2,1,0:T(8,128)(2,1)}) custom-call(bf16[128,2048]{1,0:T(8,128)(2,1)} %multiply_convert_fusion.5.refs_0_, bf16[1024,512]{1,0:T(8,128)(2,1)} %bitcast.219, bf16[1024,512]{1,0:T(8,128)(2,1)} %bitcast.216, ...), custom_call_target="tpu_custom_call" | custom-call | flops 30000001024 | bytes 1048576 | tf_op jit(solution)/shard_map/pallas_call | solution.py:228
  299.9 71.8 %shard_map.207 = (bf16[16,128,2048]{2,1,0:T(8,128)(2,1)}, bf16[1,384,512]{2,1,0:T(8,128)(2,1)}, bf16[1,384,512]{2,1,0:T(8,128)(2,1)}, bf16[1,384,512]{2,1,0:T(8,128)(2,1)}) custom-call(bf16[128,2048]{1,0:T(8,128)(2,1)} %bitcast.211, bf16[1024,512]{1,0:T(8,128)(2,1)} %bitcast.220, bf16[1024,512]{1,0:T(8,128)(2,1)} %bitcast.217, bf16[1024,512]{1,0:T(8,128)(2,1)} %bitcast.214), custom_call_target="tpu_custom_call" | custom-call | flops 30000001024 | bytes 1048576 | tf_op jit(solution)/shard_map/pallas_call | solution.py:228
  371.7 1.5 broadcast_select_fusion.5
  373.8 17.9 %maximum_maximum_fusion.refs_1_ = bf16[2048,1024]{1,0:T(8,128)(2,1)} fusion(bf16[1024,512]{1,0:T(8,128)(2,1)S(1)} %get-tuple-element.119, bf16[1024,512]{1,0:T(8,128)(2,1)S(1)} %get-tuple-element.118, bf16[1024,512]{1,0:T(8,128)(2,1)S(1)} %get-tuple-element.117, bf16[1024,512]{1,0:T(8,128)(2,1)S(1)} %get-tuple-element.116), kind=kLoop, calls=%fused_computation.1 | loop fusion | flops 16777216 | bytes 8388608 | tf_op jit(solution)/shard_map/concatenate | solution.py:761
  391.7 24.5 %fusion.22 = f32[2048,1024]{1,0:T(8,128)} fusion(bf16[2048,2048]{1,0:T(8,128)(2,1)S(1)} %bitcast.257, bf16[1024,512]{1,0:T(8,128)(2,1)S(1)} %get-tuple-element.119, bf16[1024,512]{1,0:T(8,128)(2,1)S(1)} %get-tuple-element.118, bf16[1024,512]{1,0:T(8,128)(2,1)S(1)} %get-tuple-element.117, bf16[1024,512]{1,0:T(8,128)(2,1)S(1)} %get-tuple-element.116), kind=kOutput, calls=%fused_computation.108 | convolution fusion | flops 8606711808 | bytes 20971520 | tf_op jit(solution)/shard_map/dot_general | solution.py:763
  416.8 9.1 %multiply_convert_fusion.1 = (bf16[2048,512]{1,0:T(8,128)(2,1)S(1)}, bf16[2048,512]{1,0:T(8,128)(2,1)S(1)}, bf16[2048,512]{1,0:T(8,128)(2,1)S(1)}) fusion(f32[2048,1024]{1,0:T(8,128)} %fusion.22, bf16[2048,2048]{1,0:T(8,128)(2,1)S(1)} %bitcast.255, bf16[1024,512]{1,0:T(8,128)(2,1)S(1)} %get-tuple-element.115, bf16[1024,512]{1,0:T(8,128)(2,1)S(1)} %get-tuple-element.114), kind=kOutput, calls=%fused_computation.4 | convolution fusion | flops 4314890240 | bytes 25165824 | tf_op jit(solution)/shard_map/dot_general | solution.py:768
  425.9 5.7 convolution_convert_fusion.1
  431.7 5.7 convolution_convert_fusion.2
  437.4 2.7 pad_maximum_fusion
  440.1 1.5 pad_maximum_fusion.1.refs_1_
  441.6 5.7 convolution_convert_fusion
  447.3 71.0 %shard_map.208 = (f32[128,2048]{1,0:T(8,128)}, bf16[1,320,512]{2,1,0:T(8,128)(2,1)}, bf16[1,320,512]{2,1,0:T(8,128)(2,1)}, bf16[1,320,512]{2,1,0:T(8,128)(2,1)}) custom-call(bf16[16,128,1024]{2,1,0:T(8,128)(2,1)} %bitcast.207, bf16[2048,1024]{1,0:T(8,128)(2,1)} %maximum_maximum_fusion.refs_1_, bf16[2,1024,512]{2,1,0:T(8,128)(2,1)} %bitcast.232, ...), custom_call_target="tpu_custom_call" | custom-call | flops 30000001024 | bytes 1048576 | tf_op jit(solution)/shard_map/pallas_call | solution.py:228
  518.4 1.6 fusion.15
  520.0 1.1 fusion.20.refs_0_
  521.1 56.6 %shard_map.209 = (bf16[16,128,2048]{2,1,0:T(8,128)(2,1)}, bf16[1,256,512]{2,1,0:T(8,128)(2,1)}, bf16[1,256,512]{2,1,0:T(8,128)(2,1)}, bf16[1,256,512]{2,1,0:T(8,128)(2,1)}) custom-call(bf16[128,2048]{1,0:T(8,128)(2,1)} %fusion.20.refs_0_, bf16[2,1024,512]{2,1,0:T(8,128)(2,1)} %bitcast.233, bf16[2,1024,512]{2,1,0:T(8,128)(2,1)} %bitcast.237, ...), custom_call_target="tpu_custom_call" | custom-call | flops 30000001024 | bytes 1048576 | tf_op jit(solution)/shard_map/pallas_call | solution.py:228
  577.8 4.7 fusion.2
  582.4 94.5 %shard_map.210 = (bf16[16,128,256]{2,1,0:T(8,128)(2,1)}, bf16[1,448,512]{2,1,0:T(8,128)(2,1)}, bf16[1,448,512]{2,1,0:T(8,128)(2,1)}, bf16[1,448,512]{2,1,0:T(8,128)(2,1)}) custom-call(bf16[16,128,2048]{2,1,0:T(8,128)(2,1)} %get-tuple-element.81.refs_0_, bf16[128,2048]{1,0:T(8,128)(2,1)} %bitcast_select_fusion.refs_1_, ...), custom_call_target="tpu_custom_call" | custom-call | flops 30000001024 | bytes 1048576 | tf_op jit(solution)/shard_map/pallas_call | solution.py:228
  677.0 7.2 fusion.1
  684.3 1.3 add_convert_fusion
  686.4 1.3 add_convert_fusion.1
  687.7 1.3 add_convert_fusion.2
  689.0 81.7 %shard_map.211 = (f32[128,2048]{1,0:T(8,128)}, bf16[2,2,2,2,64,512]{5,4,3,2,1,0:T(8,128)(2,1)}, bf16[2,2,2,2,64,512]{5,4,3,2,1,0:T(8,128)(2,1)}, bf16[2,2,2,2,64...) custom-call(bf16[16,128,256]{2,1,0:T(8,128)(2,1)} %get-tuple-element.85.refs_0_, ...), custom_call_target="tpu_custom_call" | custom-call | flops 30000001024 | bytes 1048576 | tf_op jit(solution)/shard_map/pallas_call | solution.py:228
  770.7 1.5 convert_bitcast_fusion.2
  772.2 1.5 copy.118
  774.2 1.5 copy.119
  776.5 3.6 collective-permute-start.2
  781.8 1.2 add_convert_fusion.3
  783.0 0.9 fusion.24
  783.9 53.9 %shard_map.212 = (f32[128,2048]{1,0:T(8,128)}, bf16[2,2,2,2,64,128]{5,4,3,2,1,0:T(8,128)(2,1)}, bf16[2,2,2,2,64,128]{5,4,3,2,1,0:T(8,128)(2,1)}, f32[2,2,2,2,8,1...) custom-call(bf16[16,128,512]{2,1,0:T(8,128)(2,1)} %bitcast.260, bf16[2048,512]{1,0:T(8,128)(2,1)} %pad_maximum_fusion.1.refs_1_, ...), custom_call_target="tpu_custom_call" | custom-call | flops 30000001024 | bytes 1048576 | tf_op jit(solution)/shard_map/pallas_call | solution.py:228
  837.9 1.0 convert_bitcast_fusion.3
  838.9 1.6 reshape.479
  840.5 2.1 reduce_sum.89
  842.6 1.2 fusion.23
  844.7 1.8 bitcast_multiply_fusion.1
  846.6 2.8 convert_bitcast_fusion
  849.4 4.2 broadcast_multiply_fusion
  853.8 1.7 fusion.8
  856.5 3.1 copy.120
  860.5 1.9 convert_add_fusion
  (178 shorter events, 12.3 us)
Async XLA Ops:
  0.6 13.3 %copy-start.2 = (bf16[2,64,2048]{2,1,0:T(8,128)(2,1)S(1)}, bf16[2,64,2048]{2,1,0:T(8,128)(2,1)}, u32[]{:S(2)}) copy-start(bf16[2,64,2048]{2,1,0:T(8,128)(2,1)} %param.12) | copy-start | bytes 1572868
  0.7 174.2 %collective-permute-start = (bf16[64,2048]{1,0:T(8,128)(2,1)}, bf16[64,2048]{1,0:T(8,128)(2,1)}, u32[]{:S(2)}, u32[]{:S(2)}) collective-permute-start(bf16[64,2048]{1,0:T(8,128)(2,1)} %param.17), channel_id=1, source_target_pairs={{0,0},{1,16},{2,1},{3,17},{4,2},{5,18},{6,3},{7,19},{8,4},{9,20},{... | collective-permute-start | bytes 786440 | tf_op jit(solution)/shard_map/ppermute | solution.py:732
  4.4 170.5 %collective-permute-start.1 = (bf16[64,2048]{1,0:T(8,128)(2,1)}, bf16[64,2048]{1,0:T(8,128)(2,1)}, u32[]{:S(2)}, u32[]{:S(2)}) collective-permute-start(bf16[64,2048]{1,0:T(8,128)(2,1)} %param.17), channel_id=1, source_target_pairs={{0,16},{1,0},{2,17},{3,1},{4,18},{5,2},{6,19},{7,3},{8,20},{9,4},{... | collective-permute-start | bytes 786440 | tf_op jit(solution)/shard_map/ppermute | solution.py:732
  10.7 5.9 copy-start.47
  11.6 4.9 copy-start.56
  11.6 4.9 copy-start.13
  11.6 4.9 copy-start.14
  14.2 2.8 copy-start.51
  17.1 2.2 copy-start.19
  95.0 3.8 copy-start.40
  98.8 2.4 copy-start.8
  98.8 2.4 copy-start.9
  105.0 67.9 %copy-start.44 = (s32[2,2048]{1,0:T(2,128)S(1)}, s32[2,2048]{1,0:T(2,128)}, u32[]{:S(2)}) copy-start(s32[2,2048]{1,0:T(2,128)} %param.22) | copy-start | bytes 49156
  235.2 1.0 copy-start
  299.8 71.8 %copy-start.17 = (bf16[2,2,2,2,64,512]{5,4,3,2,1,0:T(8,128)(2,1)S(1)}, bf16[2,2,2,2,64,512]{5,4,3,2,1,0:T(8,128)(2,1)}, u32[]{:S(2)}) copy-start(bf16[2,2,2,2,64,512]{5,4,3,2,1,0:T(8,128)(2,1)} %get-tuple-element.64) | copy-start | bytes 3145732
  299.9 71.8 %copy-start.34 = (bf16[1,320,512]{2,1,0:T(8,128)(2,1)S(1)}, bf16[1,320,512]{2,1,0:T(8,128)(2,1)}, u32[]{:S(2)}) copy-start(bf16[1,320,512]{2,1,0:T(8,128)(2,1)} %get-tuple-element.69) | copy-start | bytes 983044
  299.9 71.8 %copy-start.36 = (bf16[1,320,512]{2,1,0:T(8,128)(2,1)S(1)}, bf16[1,320,512]{2,1,0:T(8,128)(2,1)}, u32[]{:S(2)}) copy-start(bf16[1,320,512]{2,1,0:T(8,128)(2,1)} %get-tuple-element.70) | copy-start | bytes 983044
  371.7 1.6 copy-start.16
  371.7 1.6 copy-start.30
  371.7 1.6 copy-start.33
  371.7 1.6 copy-start.35
  373.3 18.4 %copy-start.58 = (bf16[16,128,2048]{2,1,0:T(8,128)(2,1)S(1)}, bf16[16,128,2048]{2,1,0:T(8,128)(2,1)}, u32[]{:S(2)}) copy-start(bf16[16,128,2048]{2,1,0:T(8,128)(2,1)} %get-tuple-element.68) | copy-start | bytes 25165828
  373.8 43.0 %slice-start = ((s8[8388608]{0:T(1024)(128)(4,1)}), s8[4194304]{0:T(1024)(128)(4,1)S(1)}, s32[]{:S(2)}) async-start(s8[8388608]{0:T(1024)(128)(4,1)} %bitcast.253), calls=%async_computation | async-start | bytes 8388608
  391.7 24.6 %copy-start.15 = (bf16[2,2,2,2,64,512]{5,4,3,2,1,0:T(8,128)(2,1)S(1)}, bf16[2,2,2,2,64,512]{5,4,3,2,1,0:T(8,128)(2,1)}, u32[]{:S(2)}) copy-start(bf16[2,2,2,2,64,512]{5,4,3,2,1,0:T(8,128)(2,1)} %get-tuple-element.66) | copy-start | bytes 3145732
  391.7 24.6 %copy-start.29 = (bf16[1,384,512]{2,1,0:T(8,128)(2,1)S(1)}, bf16[1,384,512]{2,1,0:T(8,128)(2,1)}, u32[]{:S(2)}) copy-start(bf16[1,384,512]{2,1,0:T(8,128)(2,1)} %get-tuple-element.78) | copy-start | bytes 1179652
  391.7 24.6 %copy-start.31 = (bf16[1,320,512]{2,1,0:T(8,128)(2,1)S(1)}, bf16[1,320,512]{2,1,0:T(8,128)(2,1)}, u32[]{:S(2)}) copy-start(bf16[1,320,512]{2,1,0:T(8,128)(2,1)} %get-tuple-element.76) | copy-start | bytes 983044
  391.7 24.6 %copy-start.32 = (bf16[1,320,512]{2,1,0:T(8,128)(2,1)S(1)}, bf16[1,320,512]{2,1,0:T(8,128)(2,1)}, u32[]{:S(2)}) copy-start(bf16[1,320,512]{2,1,0:T(8,128)(2,1)} %get-tuple-element.77) | copy-start | bytes 983044
  391.7 25.0 %slice-start.1 = ((s8[8388608]{0:T(1024)(128)(4,1)}), s8[4194304]{0:T(1024)(128)(4,1)S(1)}, s32[]{:S(2)}) async-start(s8[8388608]{0:T(1024)(128)(4,1)} %bitcast.253), calls=%async_computation.1 | async-start | bytes 8388608
  425.9 15.6 %copy-start.59 = (bf16[2048,512]{1,0:T(8,128)(2,1)}, bf16[2048,512]{1,0:T(8,128)(2,1)S(1)}, u32[]{:S(2)}) copy-start(bf16[2048,512]{1,0:T(8,128)(2,1)S(1)} %get-tuple-element.113) | copy-start | bytes 6291460
  447.3 71.1 %copy-start.1 = (f32[128,2048]{1,0:T(8,128)S(1)}, f32[128,2048]{1,0:T(8,128)}, u32[]{:S(2)}) copy-start(f32[128,2048]{1,0:T(8,128)} %copy-done) | copy-start | bytes 3145732
  447.3 71.1 %copy-start.50 = (f32[128]{0:T(128)S(1)}, f32[128]{0:T(128)}, u32[]{:S(2)}) copy-start(f32[128]{0:T(128)} %copy-done.49) | copy-start | bytes 1540
  518.3 1.7 copy-start.4
  518.3 1.7 copy-start.10
  521.1 56.6 %copy-start.12 = (bf16[16,128,128]{2,1,0:T(8,128)(2,1)S(1)}, bf16[16,128,128]{2,1,0:T(8,128)(2,1)}, u32[]{:S(2)}) copy-start(bf16[16,128,128]{2,1,0:T(8,128)(2,1)} %get-tuple-element.63.refs_0_.refs_4_) | copy-start | bytes 1572868
  677.0 7.3 copy-start.24
  677.0 7.3 copy-start.28
  677.0 7.3 copy-start.39
  677.0 7.3 copy-start.43
  684.2 2.0 copy-start.23
  684.2 2.0 copy-start.27
  684.2 2.1 copy-start.38
  684.2 2.2 copy-start.42
  685.6 2.1 copy-start.22
  685.6 2.1 copy-start.26
  685.6 2.1 copy-start.37
  685.6 2.1 copy-start.41
  772.2 1.5 copy-start.18
  774.1 6.0 copy-start.3
  774.1 6.0 copy-start.6
  774.1 6.0 copy-start.52
  775.7 6.1 copy-start.25
  776.5 83.9 %collective-permute-start.2 = (bf16[64,2048]{1,0:T(8,128)(2,1)}, bf16[64,2048]{1,0:T(8,128)(2,1)}, u32[]{:S(2)}, u32[]{:S(2)}) collective-permute-start(bf16[64,2048]{1,0:T(8,128)(2,1)} %get-tuple-element.122), channel_id=1, source_target_pairs={{0,0},{16,1},{1,2},{17,3},{2,4},{18,5},{3,6},{19,7},{4,8},{20,9},{... | collective-permute-start | bytes 786440 | tf_op jit(solution)/shard_map/ppermute | solution.py:815
  780.1 80.4 %collective-permute-start.3 = (bf16[64,2048]{1,0:T(8,128)(2,1)}, bf16[64,2048]{1,0:T(8,128)(2,1)}, u32[]{:S(2)}, u32[]{:S(2)}) collective-permute-start(bf16[64,2048]{1,0:T(8,128)(2,1)} %get-tuple-element.123), channel_id=1, source_target_pairs={{16,0},{0,1},{17,2},{1,3},{18,4},{2,5},{19,6},{3,7},{20,8},{4,9},{... | collective-permute-start | bytes 786440 | tf_op jit(solution)/shard_map/ppermute | solution.py:815
  838.9 5.0 copy-start.46
  838.9 5.0 copy-start.45
  838.9 5.8 copy-start.48
  843.8 5.6 copy-start.54
  843.9 5.5 copy-start.5
  849.4 4.3 copy-start.7
  849.4 4.3 copy-start.11
  849.4 4.3 copy-start.21
  853.7 1.8 copy-start.55
  853.7 1.7 copy-start.57
  853.7 2.3 copy-start.20
  (2 other events, 1.5 us)

commit v3 on v2

v3 whole, which is shorter than its diff:
```python
import functools
import itertools

import jax
import jax.numpy as jnp
from jax import lax
from jax.experimental import pallas as pl
from jax.experimental.pallas import tpu as pltpu
from jax.sharding import Mesh
from jax.sharding import PartitionSpec as P

QUERY_HEADS = 32
KEY_HEADS = 8
HEAD_DIM = 64
TEAM = 16
SCALE = HEAD_DIM ** (-0.5)
epsilon = 1e-05
rope_base = 500000.0
NT = (((1,), (1,)), ((), ()))
TN = (((0,), (0,)), ((), ()))
TEAM_AXES = ("z", "y", "c", "x")
ALL = ("dp",) + TEAM_AXES
DIMS = ("z", "y", "c", "x")
WEIGHT = {"z": 8, "y": 4, "c": 2, "x": 1}
LINKS = ("x", "y", "z")
MESH = pl.DeviceIdType.MESH
COST = pl.CostEstimate(flops=30_000_000_000, bytes_accessed=1 << 20, transcendentals=0)
EVEN = (("x", "y", "z"), ("y", "z", "x"), ("z", "x", "y"))
PARK = "park"
Z_FIRST = (("z", "x", "y"), ("z", "y", "x"))
Z_LAST = (("x", "y", "z"), ("y", "x", "z"))


def part_rows(rows, count):
    tiles = rows // 16
    base = [tiles // count + (1 if i < tiles % count else 0) for i in range(count)]
    out, at = [], 0
    for b in base:
        out.append((at * 16, b * 16))
        at += b
    return out


def coords():
    return {d: lax.axis_index(d) for d in DIMS}


def slot_of(me, flips=()):
    return sum(((1 - me[d]) if d in flips else me[d]) * WEIGHT[d] for d in DIMS)


def greet(groups):
    barrier = pltpu.get_barrier_semaphore()
    me = coords()
    group = lax.axis_index("dp")
    for d in DIMS:
        pl.semaphore_signal(barrier, inc=1, device_id={d: 1 - me[d]}, device_id_type=MESH)
    for k in range(1, groups):
        pl.semaphore_signal(barrier, inc=1, device_id={"dp": lax.rem(group + k, groups)}, device_id_type=MESH)
    pl.semaphore_wait(barrier, groups - 1 + len(DIMS))


def anywhere():
    return pl.BlockSpec(memory_space=pl.ANY)


def vmem():
    return pl.BlockSpec(memory_space=pltpu.VMEM)


def dma_sems(n):
    return pltpu.SemaphoreType.DMA((max(n, 1),))


def to_groups(groups, make, ssem, rsem):
    me = lax.axis_index("dp")
    copies = []
    for k in range(1, groups):
        peer = lax.rem(me + k, groups)
        src, dst = make(k, peer)
        copies.append(
            pltpu.make_async_remote_copy(
                src_ref=src, dst_ref=dst, send_sem=ssem.at[k - 1], recv_sem=rsem.at[k - 1],
                device_id={"dp": peer}, device_id_type=MESH,
            )
        )
        copies[-1].start()
    return copies


class Errand:
    def __init__(self, array, own_block):
        self.inputs, self.own_block = [(array, anywhere)], own_block

    def outputs(self, groups):
        a = self.inputs[0][0]
        shape = a.shape[1:] if self.own_block else a.shape
        return [(jax.ShapeDtypeStruct((max(groups - 1, 1),) + shape, a.dtype), anywhere)]

    def scratch(self, groups):
        return [dma_sems(groups - 1), dma_sems(groups - 1)]

    def run(self, groups, src, dst, scratch):
        copies = to_groups(
            groups, lambda k, peer: (src[0].at[peer] if self.own_block else src[0], dst[0].at[k - 1]), *scratch
        )
        yield PARK
        for cp in copies:
            cp.wait()


def swap_stages(chain, order, patience, ssem, rsem, lsem):
    me = coords()
    sent = []
    for k, d in enumerate(order):
        lead = (slice(None),) * DIMS.index(d)
        a, z = chain[k], chain[k + 1]
        far = pltpu.make_async_remote_copy(
            src_ref=a.at[lead + (1 - me[d],)], dst_ref=z.at[lead + (me[d],)], send_sem=ssem.at[k],
            recv_sem=rsem.at[k], device_id={d: 1 - me[d]}, device_id_type=MESH,
        )
        near = pltpu.make_async_copy(a.at[lead + (me[d],)], z.at[lead + (me[d],)], lsem.at[k])
        far.start()
        near.start()
        sent.append(far)
        for _ in range(1 if d == "c" else patience):
            yield
        far.wait_recv()
        near.wait()
    return sent


class Swap:
    def __init__(self, array, order, far=False, reduce=0, patience=1):
        lead = array.shape[:1] if reduce else ()
        shape = array.shape[len(lead) + 1 :]
        self.shape, self.dtype = (2, 2, 2, 2) + shape, array.dtype
        self.inputs = [(array.reshape(lead + self.shape), vmem)]
        self.order, self.far, self.reduce, self.patience = order, far, reduce, patience

    def outputs(self, groups):
        out = [(jax.ShapeDtypeStruct(self.shape, self.dtype), vmem)]
        return out + [(jax.ShapeDtypeStruct((max(groups - 1, 1),) + self.shape, self.dtype), anywhere)] * self.far

    def scratch(self, groups):
        extra = [pltpu.VMEM((max(groups - 1, 1),) + self.shape, self.dtype), pltpu.VMEM(self.shape, self.dtype)]
        return (
            [pltpu.VMEM(self.shape, self.dtype)] * 3
            + [dma_sems(4), dma_sems(4), dma_sems(4), dma_sems(groups - 1), dma_sems(groups - 1)]
            + extra * (self.reduce > 0)
        )

    def run(self, groups, src, dst, scratch):
        b1, b2, b3, ssem, rsem, lsem, fs, fr = scratch[:8]
        first = src[0]
        copies = []
        if self.reduce:
            landing, first = scratch[8:]
            copies = to_groups(groups, lambda k, peer: (src[0].at[peer], landing.at[k - 1]), fs, fr)
            for _ in range(self.reduce):
                yield
            for cp in copies:
                cp.wait()
            mine = lax.axis_index("dp")

            def add(i, _):
                at = tuple(lax.rem(i // w, 2) for w in (8, 4, 2, 1))
                total = src[0][(mine,) + at].astype(jnp.float32)
                for k in range(groups - 1):
                    total = total + landing[(k,) + at].astype(jnp.float32)
                first[at] = total.astype(first.dtype)
                return 0

            lax.fori_loop(0, TEAM, add, 0)
        sent = yield from swap_stages([first, b1, b2, b3, dst[0]], self.order, self.patience, ssem, rsem, lsem)
        if self.far:
            copies = to_groups(groups, lambda k, peer: (dst[0], dst[1].at[k - 1]), fs, fr)
            yield PARK
            for cp in copies:
                cp.wait()
        for cp in sent:
            cp.wait_send()


class Gather:
    def __init__(self, x, plan, patience=1):
        self.inputs, self.plan, self.patience = [(x, vmem)], plan, patience

    def outputs(self, groups):
        x = self.inputs[0][0]
        return [(jax.ShapeDtypeStruct((TEAM,) + x.shape, x.dtype), vmem)]

    def scratch(self, groups):
        return [dma_sems(64), dma_sems(64), pltpu.SemaphoreType.DMA]

    def run(self, groups, src, dst, scratch):
        (x_ref,), (g_ref,), (ssem, rsem, lsem) = src, dst, scratch
        me = coords()
        rows = x_ref.shape[0]
        plan = self.plan
        parts = part_rows(rows, len(plan))
        local = pltpu.make_async_copy(x_ref, g_ref.at[slot_of(me)], lsem)
        local.start()
        counter = itertools.count()
        copies = []

        def send(flips, r0, rn, dim):
            i = next(counter)
            s = slot_of(me, flips)
            cp = pltpu.make_async_remote_copy(
                src_ref=g_ref.at[s, pl.ds(r0, rn)] if flips else x_ref.at[pl.ds(r0, rn)],
                dst_ref=g_ref.at[s, pl.ds(r0, rn)], send_sem=ssem.at[i], recv_sem=rsem.at[i],
                device_id={dim: 1 - me[dim]}, device_id_type=MESH,
            )
            cp.start()
            copies.append(cp)
            return cp

        step1 = [send((), r0, rn, plan[p][0]) for p, (r0, rn) in enumerate(parts)]
        step2 = [[send((), r0, rn, plan[p][1])] for p, (r0, rn) in enumerate(parts)]
        step3 = [[send((), r0, rn, plan[p][2])] for p, (r0, rn) in enumerate(parts)]
        core = [send((), 0, rows, "c")]
        for _ in range(self.patience):
            yield
        for p, (r0, rn) in enumerate(parts):
            a, b, c = plan[p]
            step1[p].wait_recv()
            step2[p].append(send((a,), r0, rn, b))
            step3[p].append(send((a,), r0, rn, c))
            core.append(send((a,), r0, rn, "c"))
            yield
        for j in range(2):
            for p, (r0, rn) in enumerate(parts):
                a, b, c = plan[p]
                flips = ((b,), (a, b))[j]
                step2[p][j].wait_recv()
                step3[p].append(send(flips, r0, rn, c))
                core.append(send(flips, r0, rn, "c"))
                yield
        for j in range(4):
            for p, (r0, rn) in enumerate(parts):
                a, b, c = plan[p]
                step3[p][j].wait_recv()
                core.append(send(((c,), (a, c), (b, c), (a, b, c))[j], r0, rn, "c"))
            yield
        for cp in core:
            cp.wait_recv()
        for cp in copies:
            cp.wait_send()
        local.wait()


ROUND = [(1, 1, 1), (0, 1, 1), (1, 0, 1), (1, 1, 0), (1, 0, 0), (0, 1, 0), (0, 0, 1), (0, 0, 0)]


def flips_of(bits, order):
    return tuple(d for b, d in zip(bits, order) if b)


def add_rows(dst, a, b, r0, rn):
    def body(i, _):
        r = pl.multiple_of(r0 + i * 16, 16)
        dst[pl.ds(r, 16)] = (a[pl.ds(r, 16)].astype(jnp.float32) + b[pl.ds(r, 16)].astype(jnp.float32)).astype(dst.dtype)
        return 0

    lax.fori_loop(0, rn // 16, body, 0)


class Scatter:
    def __init__(self, pairs, flip, plan, patience=1):
        self.inputs = [(m, vmem) for pair in pairs for m in pair]
        self.flip, self.plan, self.patience = flip, plan, patience
        w = pairs[0][1]
        self.rows, self.cols = pairs[0][0].shape[1], w.shape[0] if flip else w.shape[1]

    def outputs(self, groups):
        return [(jax.ShapeDtypeStruct((self.rows, self.cols), jnp.float32), vmem)]

    def scratch(self, groups):
        block = [pltpu.VMEM((n, self.rows, self.cols), jnp.bfloat16) for n in (8, 8, 8, 4, 2)]
        return block + [pltpu.VMEM((self.rows, self.cols), jnp.bfloat16), dma_sems(32), dma_sems(32)]

    def run(self, groups, src, dst, scratch):
        part, acc, cbuf, b1, b2, b3, ssem, rsem = scratch
        (o_ref,) = dst
        pairs = list(zip(src[::2], src[1::2]))
        me = coords()
        plan, rows, cols = self.plan, self.rows, self.cols
        parts = part_rows(rows, len(plan))
        counter = itertools.count()
        copies = []

        def send(a, z, dim):
            i = next(counter)
            cp = pltpu.make_async_remote_copy(
                src_ref=a, dst_ref=z, send_sem=ssem.at[i], recv_sem=rsem.at[i],
                device_id={dim: 1 - me[dim]}, device_id_type=MESH,
            )
            cp.start()
            copies.append(cp)
            return cp

        def products(theirs, z, ours, y):
            def column(j, _):
                here = pl.ds(pl.multiple_of(j * 512, 512), 512)
                total = None
                for a, w in pairs:
                    left = jnp.concatenate([a[theirs], a[ours]], axis=0)
                    if self.flip:
                        out = lax.dot_general(left, w[here, :], NT, preferred_element_type=jnp.float32)
                    else:
                        out = jnp.dot(left, w[:, here], preferred_element_type=jnp.float32)
                    total = out if total is None else total + out
                total = total.astype(z.dtype)
                z[:, here] = total[:rows]
                y[:, here] = total[rows:]
                return 0

            lax.fori_loop(0, cols // 512, column, 0)

        def key(flips):
            return sum((1 << i) for i, d in enumerate(LINKS) if d in flips)

        s1 = [{} for _ in plan]
        core = []

        def own(fl):
            k = key(fl)
            core[ROUND.index(tuple(int(d in fl) for d in LINKS))].wait_recv()
            add_rows(acc.at[k], acc.at[k], cbuf.at[k], 0, rows)
            for p, (r0, rn) in enumerate(parts):
                a, b, c = plan[p]
                if a in fl:
                    j = (1 if b in fl else 0) + (2 if c in fl else 0)
                    s1[p][j] = send(acc.at[k, pl.ds(r0, rn)], b1.at[j, pl.ds(r0, rn)], a)

        for n, bits in enumerate(ROUND):
            fl = flips_of(bits, LINKS)
            products(slot_of(me, fl + ("c",)), part.at[key(fl)], slot_of(me, fl), acc.at[key(fl)])
            core.append(send(part.at[key(fl)], cbuf.at[key(fl)], "c"))
            if n > 0:
                own(flips_of(ROUND[n - 1], LINKS))
            if n % 2 == 1:
                yield
        own(())
        for _ in range(self.patience):
            yield
        s2 = [{} for _ in plan]
        for bb, cc in ((1, 1), (1, 0), (0, 1), (0, 0)):
            for p, (r0, rn) in enumerate(parts):
                a, b, c = plan[p]
                s1[p][bb + 2 * cc].wait_recv()
                k = key(flips_of((bb, cc), (b, c)))
                add_rows(acc.at[k], acc.at[k], b1.at[bb + 2 * cc], r0, rn)
                if bb:
                    s2[p][cc] = send(acc.at[k, pl.ds(r0, rn)], b2.at[cc, pl.ds(r0, rn)], b)
            if cc == 0:
                for _ in range(self.patience if bb == 0 else 1):
                    yield
        s3 = []
        for cc in (1, 0):
            for p, (r0, rn) in enumerate(parts):
                a, b, c = plan[p]
                s2[p][cc].wait_recv()
                k = key((c,) if cc else ())
                add_rows(acc.at[k], acc.at[k], b2.at[cc], r0, rn)
                if cc:
                    s3.append(send(acc.at[k, pl.ds(r0, rn)], b3.at[pl.ds(r0, rn)], c))
            yield
        for p, (r0, rn) in enumerate(parts):
            s3[p].wait_recv()
            add_rows(o_ref, acc.at[0], b3, r0, rn)
        for cp in copies:
            cp.wait_send()


def call(jobs, cid, body=None, inputs=(), outputs=(), scratch=()):
    groups = lax.axis_size("dp")
    jobs = list(jobs)
    n_in, n_out, n_scratch = len(inputs), len(outputs), len(scratch)
    job_in = [job.inputs for job in jobs]
    job_out = [job.outputs(groups) for job in jobs]
    job_scratch = [job.scratch(groups) for job in jobs]

    def kernel(*refs):
        def take(n):
            nonlocal refs
            head, refs = refs[:n], refs[n:]
            return head

        ins = take(n_in)
        src = [take(len(o)) for o in job_in]
        outs = take(n_out)
        dst = [take(len(o)) for o in job_out]
        scr = take(n_scratch)
        own = [take(len(o)) for o in job_scratch]
        greet(groups)
        alive = [job.run(groups, a, z, m) for job, a, z, m in zip(jobs, src, dst, own)]

        parked = []

        def tick():
            for job in list(alive):
                state = next(job, alive)
                if state is not None:
                    alive.remove(job)
                if state is PARK:
                    parked.append(job)

        tick()
        if body is not None:
            body(groups, tick, *ins, *outs, *scr)
        while alive:
            tick()
        for job in parked:
            next(job, None)

    out = pl.pallas_call(
        kernel,
        out_shape=list(outputs) + [o for each in job_out for o, _ in each],
        in_specs=[vmem()] * n_in + [place() for each in job_in for _, place in each],
        out_specs=[vmem()] * n_out + [place() for each in job_out for _, place in each],
        scratch_shapes=list(scratch) + [o for each in job_scratch for o in each],
        cost_estimate=COST,
        compiler_params=pltpu.CompilerParams(collective_id=cid, has_side_effects=True, vmem_limit_bytes=60 << 20),
    )(*inputs, *[a for each in job_in for a, _ in each])
    main, rest = list(out[:n_out]), list(out[n_out:])
    got = []
    for each in job_out:
        got.append(rest[: len(each)])
        rest = rest[len(each) :]
    return main, got


NEG = -1e30
CHUNK = 256
SLOTS = 4
FFN_SLOTS = 4
ORDER_A = ("c", "x", "y", "z")
ORDER_B = ("c", "y", "z", "x")
ORDER_C = ("c", "z", "x", "y")


def swapped(v):
    lane = lax.broadcasted_iota(jnp.int32, v.shape, 1)
    low = lax.rem(lane, HEAD_DIM) < HEAD_DIM // 2
    return jnp.where(low, pltpu.roll(v, 128 - HEAD_DIM // 2, 1), pltpu.roll(v, HEAD_DIM // 2, 1))


def low_lanes(shape):
    return lax.broadcasted_iota(jnp.int32, shape, 1) < HEAD_DIM


def as_row(column):
    return jnp.transpose(jnp.broadcast_to(column, (column.shape[0], 128)))[0:1]


def as_column(row):
    return jnp.transpose(jnp.broadcast_to(row, (128, row.shape[1])))[:, 0:1]


def attend_kernel(groups, tick, h_ref, w_ref, cos_ref, sin_ref, own_ref, idr_ref, q_ref, kv_ref, o_ref, lse_ref, top, total, acc, ssem, rsem):
    me = lax.axis_index("dp")
    tokens = cos_ref.shape[1]
    span = TEAM * tokens
    steps = span // CHUNK
    heads = q_ref.shape[0]

    def project(g, _):
        raw = jnp.dot(h_ref[g], w_ref[...], preferred_element_type=jnp.float32)
        cos = jnp.concatenate([cos_ref[g]] * 2, axis=0)
        sin = jnp.concatenate([sin_ref[g]] * 2, axis=0)
        qp, kvp = raw[:, :128], raw[:, 128:]
        low = low_lanes(qp.shape)
        qp = qp * cos + swapped(qp) * sin
        kvp = kvp * jnp.where(low, cos / SCALE, 1.0) + swapped(kvp) * jnp.where(low, sin / SCALE, 0.0)
        q_ref[0, g] = jnp.where(low, qp, 0.0).astype(jnp.bfloat16)
        q_ref[1, g] = jnp.where(low, pltpu.roll(qp, HEAD_DIM, 1), 0.0).astype(jnp.bfloat16)
        kv_ref[me, g] = kvp.astype(jnp.bfloat16)
        return 0

    lax.fori_loop(0, TEAM, project, 0)
    tick()
    copies = []
    for k in range(1, groups):
        copies.append(
            pltpu.make_async_remote_copy(
                src_ref=kv_ref.at[me], dst_ref=kv_ref.at[me], send_sem=ssem.at[k - 1], recv_sem=rsem.at[k - 1],
                device_id={"dp": lax.rem(me + k, groups)}, device_id_type=MESH,
            )
        )
        copies[-1].start()
    for k in range(groups):
        p = lax.rem(me + groups - k, groups)
        if k > 0:
            copies[k - 1].wait_recv()
        for s in range(2):
            kv = kv_ref[p, :, s * tokens : (s + 1) * tokens, :].reshape(span, 128)
            kid = idr_ref[s, :, pl.ds(pl.multiple_of(p * span, 128), span)]

            def block(i, _, s=s, kv=kv, kid=kid, k=k):
                at = s * steps + i
                q = q_ref[:, pl.ds(i * SLOTS, SLOTS), s * tokens : (s + 1) * tokens, :].reshape(heads * CHUNK, 128)
                qid = as_column(own_ref[s, :, pl.ds(pl.multiple_of(i * CHUNK, CHUNK), CHUNK)])
                qid = jnp.concatenate([qid] * heads, axis=0)
                scores = lax.dot_general(q, kv, NT, preferred_element_type=jnp.float32)
                scores = jnp.where(kid <= qid, scores, NEG)
                peak = jnp.max(scores, axis=-1, keepdims=True)
                if k > 0:
                    old = top[at]
                    peak = jnp.maximum(old, peak)
                weight = jnp.exp(scores - peak)
                summed = jnp.sum(weight, axis=-1, keepdims=True)
                mixed = jnp.dot(weight.astype(jnp.bfloat16), kv, preferred_element_type=jnp.float32)
                if k > 0:
                    factor = jnp.exp(old - peak)
                    summed = summed + total[at] * factor
                    mixed = mixed + acc[at] * factor
                if k < groups - 1:
                    top[at] = peak
                    total[at] = summed
                    acc[at] = mixed
                else:
                    mixed = mixed / summed
                    first, second = mixed[:CHUNK], mixed[CHUNK:]
                    out = jnp.where(low_lanes(first.shape), pltpu.roll(first, HEAD_DIM, 1), second)
                    o_ref[pl.ds(i * SLOTS, SLOTS), s * tokens : (s + 1) * tokens, :] = out.astype(jnp.bfloat16).reshape(SLOTS, tokens, 128)
                    lse_ref[at] = as_row(peak + jnp.log(summed))
                return 0

            for first in range(0, steps, 2):
                lax.fori_loop(first, first + 2, block, 0)
                tick()
    for cp in copies:
        cp.wait_send()


def attend(groups, h, w, cos, sin, id_a, id_b, cid, jobs):
    tokens = cos.shape[1]
    rows = 2 * tokens
    blocks = 2 * TEAM * tokens // CHUNK
    f32, bf16 = jnp.float32, jnp.bfloat16
    return call(
        jobs, cid, attend_kernel, [h, w, cos, sin, id_a, id_b],
        [
            jax.ShapeDtypeStruct((2, TEAM, rows, 128), bf16),
            jax.ShapeDtypeStruct((groups, TEAM, rows, 128), bf16),
            jax.ShapeDtypeStruct((TEAM, rows, 128), bf16),
            jax.ShapeDtypeStruct((blocks, 1, 2 * CHUNK), f32),
        ],
        [
            pltpu.VMEM((blocks, 2 * CHUNK, 1), f32), pltpu.VMEM((blocks, 2 * CHUNK, 1), f32),
            pltpu.VMEM((blocks, 2 * CHUNK, 128), f32), dma_sems(groups - 1), dma_sems(groups - 1),
        ],
    )


def attend_back_kernel(groups, tick, dm_ref, wo_ref, q_ref, kv_ref, o_ref, lse_ref, cos_ref, sin_ref, all_ref, own_ref, d_ref, do, gz, delta, dq, dkv, out_buf, in_buf, ssem, rsem):
    me = lax.axis_index("dp")
    tokens = cos_ref.shape[1]
    span = TEAM * tokens
    steps = span // CHUNK
    f32, bf16 = jnp.float32, jnp.bfloat16

    def project(g, _):
        part = lax.dot_general(dm_ref[g], wo_ref[...], NT, preferred_element_type=f32).astype(bf16)
        do[g] = part
        part = part.astype(f32)
        low = low_lanes(part.shape)
        gz[0, g] = jnp.where(low, 0.0, pltpu.roll(part, HEAD_DIM, 1)).astype(bf16)
        gz[1, g] = jnp.where(low, 0.0, part).astype(bf16)
        return 0

    lax.fori_loop(0, TEAM, project, 0)
    tick()
    for s in range(2):

        def deltas(i, _, s=s):
            here = (pl.ds(i * SLOTS, SLOTS), slice(s * tokens, (s + 1) * tokens), slice(None))
            both = do[here].reshape(CHUNK, 128).astype(f32) * o_ref[here].reshape(CHUNK, 128).astype(f32)
            low = low_lanes(both.shape)
            first = jnp.sum(jnp.where(low, both, 0.0), axis=-1, keepdims=True)
            second = jnp.sum(jnp.where(low, 0.0, both), axis=-1, keepdims=True)
            delta[s * steps + i] = as_row(jnp.concatenate([first, second], axis=0))
            return 0

        lax.fori_loop(0, steps, deltas, 0)
    copies = []
    order = list(range(1, groups)) + [0]
    for turn, k in enumerate(order):
        p = lax.rem(me + k, groups)
        for s in range(2):
            kv = kv_ref[p, :, s * tokens : (s + 1) * tokens, :].reshape(span, 128)
            kid = as_column(all_ref[s, :, pl.ds(pl.multiple_of(p * span, span), span)])

            def block(i, _, s=s, kv=kv, kid=kid, turn=turn):
                at = s * steps + i
                here = (slice(None), pl.ds(i * SLOTS, SLOTS), slice(s * tokens, (s + 1) * tokens), slice(None))
                q = q_ref[here].reshape(2 * CHUNK, 128)
                g = gz[here].reshape(2 * CHUNK, 128)
                qid = own_ref[s, :, pl.ds(pl.multiple_of(i * CHUNK, CHUNK), CHUNK)]
                qid = jnp.concatenate([qid] * 2, axis=1)
                scores = lax.dot_general(kv, q, NT, preferred_element_type=f32)
                prob = jnp.where(kid <= qid, jnp.exp(scores - lse_ref[at]), 0.0)
                dp = lax.dot_general(kv, g, NT, preferred_element_type=f32)
                ds = (prob * (dp - delta[at])).astype(bf16)
                part = jnp.dot(ds, q, preferred_element_type=f32)
                part = part + jnp.dot(prob.astype(bf16), g, preferred_element_type=f32)
                dkv[s] = dkv[s] + part
                mine = lax.dot_general(ds, kv, TN, preferred_element_type=f32)
                if turn == 0:
                    dq[at] = mine
                else:
                    dq[at] = dq[at] + mine
                return 0

            dkv[s] = jnp.zeros((span, 128), f32)
            for first in range(0, steps, 2):
                lax.fori_loop(first, first + 2, block, 0)
                tick()
            if k > 0:
                out_buf[k - 1, :, s * tokens : (s + 1) * tokens, :] = dkv[s].astype(bf16).reshape(TEAM, tokens, 128)
        if k > 0:
            copies.append(
                pltpu.make_async_remote_copy(
                    src_ref=out_buf.at[k - 1], dst_ref=in_buf.at[k - 1], send_sem=ssem.at[k - 1], recv_sem=rsem.at[k - 1],
                    device_id={"dp": p}, device_id_type=MESH,
                )
            )
            copies[-1].start()
    for cp in copies:
        cp.wait_recv()
    for s in range(2):

        def finish(i, _, s=s):
            here = (pl.ds(i * SLOTS, SLOTS), slice(s * tokens, (s + 1) * tokens), slice(None))
            cos = cos_ref[pl.ds(i * SLOTS, SLOTS)].reshape(CHUNK, 128)
            sin = sin_ref[pl.ds(i * SLOTS, SLOTS)].reshape(CHUNK, 128)
            both = dq[s * steps + i]
            first, second = both[:CHUNK], both[CHUNK:]
            qp = jnp.where(low_lanes(first.shape), first, pltpu.roll(second, HEAD_DIM, 1))
            kvp = dkv[s, pl.ds(pl.multiple_of(i * CHUNK, CHUNK), CHUNK), :]
            for k in range(1, groups):
                kvp = kvp + in_buf[(k - 1,) + here].reshape(CHUNK, 128).astype(f32)
            low = low_lanes(qp.shape)
            qp = qp * cos - swapped(qp) * sin
            kvp = kvp * jnp.where(low, cos / SCALE, 1.0) - swapped(kvp) * jnp.where(low, sin / SCALE, 0.0)
            both = jnp.concatenate([qp, kvp], axis=1).astype(bf16)
            d_ref[here] = both.reshape(SLOTS, tokens, 256)
            return 0

        lax.fori_loop(0, steps, finish, 0)
    for cp in copies:
        cp.wait_send()


def attend_back(groups, dm, wo, q, kv, o, lse, cos, sin, id_a, id_b, cid, jobs):
    tokens = cos.shape[1]
    rows = 2 * tokens
    span = TEAM * tokens
    blocks = 2 * span // CHUNK
    peers = max(groups - 1, 1)
    f32, bf16 = jnp.float32, jnp.bfloat16
    return call(
        jobs, cid, attend_back_kernel, [dm, wo, q, kv, o, lse, cos, sin, id_a, id_b],
        [jax.ShapeDtypeStruct((TEAM, rows, 256), bf16)],
        [
            pltpu.VMEM((TEAM, rows, 128), bf16), pltpu.VMEM((2, TEAM, rows, 128), bf16),
            pltpu.VMEM((blocks, 1, 2 * CHUNK), f32), pltpu.VMEM((blocks, 2 * CHUNK, 128), f32),
            pltpu.VMEM((2, span, 128), f32),
            pltpu.VMEM((peers, TEAM, rows, 128), bf16), pltpu.VMEM((peers, TEAM, rows, 128), bf16),
            dma_sems(groups - 1), dma_sems(groups - 1),
        ],
    )


def ffn_kernel(h_ref, c_ref, g_ref, u_ref, d_ref, a_ref, dg_ref, du_ref, wg_ref, wu_ref, wd_ref, *sums):
    step = pl.program_id(0)
    slots, rows, model = h_ref.shape
    h = h_ref[...].reshape(slots * rows, model)
    c = c_ref[...].reshape(slots * rows, model)
    f32, bf16 = jnp.float32, jnp.bfloat16
    gate = jnp.dot(h, g_ref[...], preferred_element_type=f32)
    up = jnp.dot(h, u_ref[...], preferred_element_type=f32)
    da = jnp.dot(c, d_ref[...], preferred_element_type=f32)
    sig = 1.0 / (1.0 + jnp.exp(-gate))
    silu = gate * sig
    active = (silu * up).astype(bf16)
    d_gate = (da * up * sig * (1.0 + gate * (1.0 - sig))).astype(bf16)
    d_up = (da * silu).astype(bf16)
    for ref, value in ((a_ref, active), (dg_ref, d_gate), (du_ref, d_up)):
        ref[...] = value.reshape(slots, rows, -1)

    @pl.when(step == 0)
    def _():
        for total in sums:
            total[...] = jnp.zeros_like(total)

    wide = 512
    for first in range(0, model, wide):
        here = slice(first, first + wide)
        for total, left, right in zip(sums, (h_ref, h_ref, c_ref), (d_gate, d_up, active)):
            left = left[:, :, here].reshape(slots * rows, wide)
            total[here, :] += lax.dot_general(left, right, TN, preferred_element_type=f32)

    @pl.when(step == pl.num_programs(0) - 1)
    def _():
        for ref, total in zip((wg_ref, wu_ref, wd_ref), sums):
            ref[...] = total[...].astype(bf16)


def ffn(h, c, w_gate, w_up, w_down):
    team, rows, model = h.shape
    ff = w_gate.shape[1]
    bf16 = jnp.bfloat16
    tall = pl.BlockSpec((FFN_SLOTS, rows, model), lambda i: (i, 0, 0))
    weight = pl.BlockSpec((model, ff), lambda i: (0, 0))
    return pl.pallas_call(
        ffn_kernel,
        grid=(team // FFN_SLOTS,),
        in_specs=[tall, tall, weight, weight, weight],
        out_specs=[pl.BlockSpec((FFN_SLOTS, rows, ff), lambda i: (i, 0, 0))] * 3 + [weight] * 3,
        out_shape=[jax.ShapeDtypeStruct((team, rows, ff), bf16)] * 3 + [jax.ShapeDtypeStruct((model, ff), bf16)] * 3,
        scratch_shapes=[pltpu.VMEM((model, ff), jnp.float32)] * 3,
        cost_estimate=COST,
        compiler_params=pltpu.CompilerParams(vmem_limit_bytes=60 << 20),
    )(h, c, w_gate, w_up, w_down)


def rotation_tables(positions):
    half = HEAD_DIM // 2
    lane = jnp.arange(128, dtype=jnp.int32)
    freqs = rope_base ** (-(lane % half).astype(jnp.float32) * 2.0 / HEAD_DIM)
    angles = positions.astype(jnp.float32)[:, None] * freqs[None, :]
    sign = jnp.where(lane % HEAD_DIM < half, -SCALE, SCALE)
    return (jnp.cos(angles) * SCALE).reshape(TEAM, -1, 128), (jnp.sin(angles) * sign).reshape(TEAM, -1, 128)


def norm_back(grad, normed, scale):
    return scale * (grad - normed * jnp.mean(grad * normed, axis=-1, keepdims=True))


def after(x, *others):
    return lax.optimization_barrier((x,) + others)[0]


def local(
    layer_input, attn_gain, query_weight, key_matrix, value_matrix, output_weight, ffn_gain,
    gate_weight, up_weight, down_weight, block_ids, cotangent,
):
    f32, bf16 = jnp.float32, jnp.bfloat16
    seqs, tokens, model = layer_input.shape
    rows = seqs * tokens
    groups = lax.axis_size("dp")
    group = lax.axis_index("dp")
    devices = groups * TEAM
    share = query_weight.shape[0]
    span = TEAM * tokens
    heads = QUERY_HEADS // TEAM
    ff = gate_weight.shape[1] // TEAM
    twin = TEAM // KEY_HEADS
    cut = heads * HEAD_DIM

    gain_one = attn_gain.astype(f32)[:, None]
    gain_two = ffn_gain.astype(f32)[:, None]

    def scaled(weight, gain):
        return (weight.astype(f32) * gain).astype(bf16)

    def doubled(weight):
        split = weight.reshape(share, KEY_HEADS, 1, HEAD_DIM)
        return jnp.broadcast_to(split, (share, KEY_HEADS, twin, HEAD_DIM)).reshape(share, TEAM, HEAD_DIM)

    def deal(k):
        return [(j, ((j + k) % groups) * TEAM + j // groups) for j in range(devices)]

    def by_member(weight):
        return jnp.moveaxis(weight.reshape(share, TEAM, -1), 1, 0)

    def in_order(mine, far):
        mine = mine.reshape(TEAM * share, -1)
        far = far.reshape((-1,) + mine.shape)
        if groups == 1:
            return mine
        if groups == 2:
            first = group == 0
            return jnp.concatenate([jnp.where(first, mine, far[0]), jnp.where(first, far[0], mine)])
        blocks = jnp.concatenate([mine[None], far])
        return jnp.take(blocks, lax.rem(group - jnp.arange(groups) + groups, groups), axis=0).reshape(model, -1)

    pack_q = by_member(scaled(query_weight, gain_one))
    pack_kv = jnp.concatenate(
        [doubled(scaled(key_matrix, gain_one)), doubled(scaled(value_matrix, gain_one))], axis=-1
    )
    pack_kv = jnp.moveaxis(pack_kv, 1, 0)
    x = layer_input.reshape(rows, model).astype(f32)
    norm_one = lax.rsqrt(jnp.mean(x * x, axis=-1, keepdims=True) + epsilon)
    normed_one = x * norm_one
    c_own = cotangent.reshape(rows, model)
    _, (w_q, w_kv, (h_one,)) = call(
        [Swap(pack_q, ORDER_A, True), Swap(pack_kv, ORDER_B, True), Gather(normed_one.astype(bf16), Z_FIRST, 3)], 1
    )
    w_in = jnp.concatenate([in_order(*w_q), in_order(*w_kv)], axis=-1)

    late_weight = after(output_weight, h_one)
    dealt = jnp.stack([lax.ppermute(late_weight, ALL, deal(k)) for k in range(groups)])
    if groups > 1:
        dealt = jnp.take(dealt, lax.rem(group - jnp.arange(groups) + groups, groups), axis=0)
    w_out = dealt.reshape(-1, model)

    cos, sin = rotation_tables(group * span + jnp.arange(span, dtype=jnp.int32))
    all_ids = block_ids.astype(f32)[:, None, :]
    ids = lax.dynamic_slice_in_dim(all_ids, group * span, span, 2)
    packs = (by_member(scaled(gate_weight, gain_two)), by_member(scaled(up_weight, gain_two)), by_member(down_weight))
    (q, kv, o, lse), own = attend(
        groups, h_one, w_in, cos, sin, ids, all_ids, 2,
        [Swap(a, order, patience=2) for a, order in zip(packs, (ORDER_A, ORDER_B, ORDER_C))],
    )
    own_gate, own_up, own_down = [a[0].reshape(TEAM * share, ff) for a in own]

    _, ((far_gate,), (branch,)) = call([Errand(own_gate, False), Scatter([(o, w_out)], False, EVEN)], 3)
    middle = x + branch
    norm_two = lax.rsqrt(jnp.mean(middle * middle, axis=-1, keepdims=True) + epsilon)
    normed_two = middle * norm_two
    _, ((far_up,), (far_down,), (h_two,), (c_all,)) = call(
        [Errand(own_up, False), Errand(own_down, False), Gather(normed_two.astype(bf16), Z_FIRST), Gather(c_own, Z_FIRST)], 4
    )
    w_gate, w_up, w_down = in_order(own_gate, far_gate), in_order(own_up, far_up), in_order(own_down, far_down)
    active, d_gate, d_up, *g_ffn = ffn(h_two, c_all, w_gate, w_up, w_down)
    g_gate, g_up, g_down = [a.reshape(groups, TEAM * share, -1) for a in g_ffn]

    def outer(left, right):
        left, right = left.reshape(-1, left.shape[-1]), right.reshape(-1, right.shape[-1])
        left, right = lax.optimization_barrier((left, right))
        out = lax.dot_general(left, right, TN, preferred_element_type=f32)
        return out.astype(bf16).reshape(groups, TEAM * share, -1)

    def total(mine, far):
        out = lax.dynamic_index_in_dim(mine, group, 0, keepdims=False).astype(f32)
        for k in range(groups - 1):
            out = out + far[k].astype(f32)
        return out.astype(bf16).reshape(TEAM, share, -1)

    def home(piece):
        return jnp.moveaxis(piece[0].reshape(TEAM, share, -1).astype(f32), 0, 1)

    _, ((far_gate,), (dn_two,)) = call(
        [Errand(g_gate, True), Scatter([(d_gate, w_gate), (d_up, w_up)], True, EVEN)], 5
    )
    middle_grad = c_own.astype(f32) + norm_back(dn_two, normed_two, norm_two)
    _, ((far_up,), (middle_low,)) = call([Errand(g_up, True), Gather(middle_grad.astype(bf16), Z_FIRST)], 6)
    w_part, middle_low = lax.optimization_barrier((outer(o, middle_low), middle_low))
    w_part = w_part.reshape(groups, -1, model)
    pieces = []
    for k in range(groups):
        pick = lax.rem(group + groups - k, groups) if groups > 1 else 0
        mine = lax.dynamic_index_in_dim(w_part, pick, 0, keepdims=False)
        pieces.append(lax.ppermute(mine, ALL, [(b, a) for a, b in deal(k)]).astype(f32))
    grad_output = sum(pieces)
    (d_in,), ((far_down,), home_gate, home_up, (produced,)) = attend_back(
        groups, middle_low, w_out, q, kv, o, lse, cos, sin, all_ids, ids, 7,
        [
            Errand(g_down, True), Swap(total(g_gate, far_gate), ORDER_A, patience=2),
            Swap(total(g_up, far_up), ORDER_B, patience=2), Scatter([(active, w_down)], True, Z_LAST),
        ],
    )
    layer_output = (middle + produced).reshape(seqs, tokens, model)
    d_in, grad_output = lax.optimization_barrier((d_in, grad_output))
    attn = outer(h_one, d_in).reshape(groups, TEAM, share, -1)
    sum_down = total(g_down, far_down)
    thirds = (sum_down[..., : ff // 4], sum_down[..., ff // 4 : ff // 2], sum_down[..., ff // 2 :])
    _, ((dn_one,), home_a, home_b, home_c, home_q, home_kv) = call(
        [
            Scatter([(d_in, w_in)], True, EVEN), *[Swap(a, o) for a, o in zip(thirds, (ORDER_A, ORDER_B, ORDER_C))],
            Swap(attn[..., :cut], ORDER_A, reduce=6), Swap(attn[..., cut:], ORDER_B, reduce=6),
        ],
        8,
    )
    input_grad = (middle_grad + norm_back(dn_one, normed_one, norm_one)).reshape(seqs, tokens, model)

    grad_gate, grad_up = home(home_gate).reshape(share, -1), home(home_up).reshape(share, -1)
    grad_down = jnp.concatenate([home(a) for a in (home_a, home_b, home_c)], axis=-1).reshape(share, -1)
    grad_query = home(home_q).reshape(share, -1)
    pair = home_kv[0].reshape(KEY_HEADS, twin, share, 2 * HEAD_DIM).astype(f32).sum(axis=1)
    pair = jnp.moveaxis(pair, 0, 1)
    grad_key, grad_value = pair[..., :HEAD_DIM].reshape(share, -1), pair[..., HEAD_DIM:].reshape(share, -1)

    def gain_grad(*both):
        return sum(jnp.sum(weight.astype(f32) * grad, axis=-1) for weight, grad in both)

    grad_gain_one = gain_grad((query_weight, grad_query), (key_matrix, grad_key), (value_matrix, grad_value))
    grad_gain_two = gain_grad((gate_weight, grad_gate), (up_weight, grad_up))
    return (
        layer_output, input_grad, grad_gain_one, grad_query * gain_one, grad_key * gain_one, grad_value * gain_one,
        grad_output, grad_gain_two, grad_gate * gain_two, grad_up * gain_two, grad_down,
    )


def solution(mesh):
    fine = Mesh(mesh.devices.reshape(-1, 2, 2, 2, 2), ALL)
    token = P(None, ALL, None)
    row = P(ALL, None)
    vec = P(ALL)
    in_specs = (token, vec, row, row, row, row, vec, row, row, row, P(), token)
    out_specs = (token, token, vec, row, row, row, row, vec, row, row, row)
    return jax.shard_map(local, mesh=fine, in_specs=in_specs, out_specs=out_specs, check_vma=False)
```

time: 874 us -> 755 us (0.86)
  matrix products: 62.7 us -> 10.6 us
  other arithmetic: 68.7 us -> 42.7 us
  Pallas kernels: 686 us -> 661 us
  local copies, waits for them, and re-layouts: 32.9 us -> 22 us
    pallas_call x10 -> x8, Pallas kernels: 686 us -> 623 us  [call(): pl.pallas_call(kernel, out_shape=list(outputs) + [o for each in job_out f...]
    dot_general x7 -> x2, matrix products: 62.7 us -> 10.6 us  [outer(): out = lax.dot_general(left, right, TN, preferred_element_type=f32)]
    pallas_call x0 -> x1, Pallas kernels: none -> 37.5 us  [ffn(): pl.pallas_call(ffn_kernel, grid=(team // FFN_SLOTS,), in_specs=[tall, tal...]
    concatenate x2 -> x0, other arithmetic: 20.6 us -> none  [the longest x1 17.9 us: local(): w_gate_up = jnp.concatenate([w_gate, w_up], axis=-1)]
  transfers between devices with their start and end apart: 4 -> 4, of which waited for: 0 -> 0; matrix products, arithmetic and copies ran while one was open for 6% -> 3% of each run, Pallas kernels for 22% -> 26%
where the time goes in v3:
time: 755 us; the launch traced here: 745 us
  Pallas kernels  661 us (88%)
  other arithmetic  42.7 us (6%)
  local copies, waits for them, and re-layouts  22 us (3%)
  matrix products  10.6 us (1%)
    pallas_call x8, Pallas kernels, call(): pl.pallas_call(kernel, out_shape=list(outputs) + [o for each in job_out f...  623 us
    pallas_call x1, Pallas kernels, ffn(): pl.pallas_call(ffn_kernel, grid=(team // FFN_SLOTS,), in_specs=[tall, tal...  37.5 us
  transfers between devices with their start and end apart: 4, of which 0 were waited for; matrix products, arithmetic and copies ran while one was open for 3% of the time, Pallas kernels for 26%

profile of v3, /device:TPU:0, one launch (start us, length us, event | category | flops | bytes accessed | tf_op | source)
XLA Modules:
  0.0 744.7 jit_solution(18354357484294327503)
XLA Ops:
  0.7 0.7 convert_element_type.173
  1.4 1.0 fusion.17
  2.7 1.8 copy_bitcast_fusion.3
  4.4 1.2 fusion.11
  5.8 1.0 fusion.6.refs_2_
  6.8 0.9 pad_maximum_fusion.4
  7.7 58.1 %shard_map.203 = (bf16[2,2,2,2,64,128]{5,4,3,2,1,0:T(8,128)(2,1)}, bf16[1,2,2,2,2,64,128]{6,5,4,3,2,1,0:T(8,128)(2,1)}, bf16[2,2,2,2,64,128]{5,4,3,2,1,0:T(8,128...) custom-call(bf16[2,2,2,2,64,128]{5,4,3,2,1,0:T(8,128)(2,1)} %bitcast.211, ...), custom_call_target="tpu_custom_call" | custom-call | flops 30000001024 | bytes 1048576 | tf_op jit(solution)/shard_map/pallas_call | solution.py:418
  65.8 0.7 collective-permute-start
  66.5 3.1 collective-permute-start.1
  69.7 0.6 broadcast_in_dim.54.refs_5_.refs_8_
  70.3 0.6 dynamic_slice.20.refs_4_.refs_9_
  70.9 0.5 fusion.2
  71.5 1.1 copy.61
  72.6 1.1 copy.60
  73.7 1.1 copy.59
  74.8 3.0 fusion.15
  78.0 1.1 maximum_maximum_fusion.refs_1_
  79.1 77.3 %shard_map.204 = (bf16[2,16,128,128]{3,2,1,0:T(8,128)(2,1)}, bf16[2,16,128,128]{3,2,1,0:T(8,128)(2,1)}, bf16[16,128,128]{2,1,0:T(8,128)(2,1)}, f32[8,1,512]{2,1,...) custom-call(bf16[16,128,2048]{2,1,0:T(8,128)(2,1)} %get-tuple-elemen, ...), custom_call_target="tpu_custom_call" | custom-call | flops 30000001024 | bytes 1048576 | tf_op jit(solution)/shard_map/pallas_call | solution.py:418
  156.7 0.6 gather_fusion
  157.3 0.9 bitcast_select_fusion.6.refs_2_.refs_1_
  158.2 58.9 %shard_map.205 = (bf16[1,1024,512]{2,1,0:T(8,128)(2,1)}, f32[128,2048]{1,0:T(8,128)}) custom-call(bf16[1024,512]{1,0:T(8,128)(2,1)} %bitcast.184, bf16[16,128,128]{2,1,0:T(8,128)(2,1)} %get-tuple-element.65.refs_1_.refs_4_, bf16[128,2048]{1,0:T(8,128)(2,1)} %bitcast_select_fusion.6.refs_2_.refs_1_), custom_call_target="tpu_custom_call" | custom-call | flops 30000001024 | bytes 1048576 | tf_op jit(solution)/shard_map/pallas_call | solution.py:418
  217.1 1.5 multiply_reduce_fusion.1
  218.7 0.9 multiply_convert_fusion.refs_2_
  219.6 102.6 %shard_map.206 = (bf16[1,1024,512]{2,1,0:T(8,128)(2,1)}, bf16[1,1024,512]{2,1,0:T(8,128)(2,1)}, bf16[16,128,2048]{2,1,0:T(8,128)(2,1)}, bf16[16,128,2048]{2,1,0:T(8,128)(2,1)}) custom-call(bf16[1024,512]{1,0:T(8,128)(2,1)} %bitcast.185, bf16[1024,512]{1,0:T(8,128)(2,1)} %bitcast.186, bf16[128,2048]{1,0:T(8,128)(2,1)} %multiply_convert_fusion.refs_2_, ...), custom_call_target="tpu_custom_call" | custom-call | flops 30000001024 | bytes 1048576 | tf_op jit(solution)/shard_map/pallas_call | solution.py:418
  322.3 1.5 bitcast_select_fusion.1
  324.3 1.0 copy-done.11
  325.9 1.5 pad_maximum_fusion.2.d_ref.refs_14_
  327.3 1.5 pad_maximum_fusion.1.u_ref.refs_4_
  328.8 1.5 pad_maximum_fusion.g_ref.refs_2_
  330.2 37.5 %shard_map.207 = (bf16[16,128,512]{2,1,0:T(8,128)(2,1)}, bf16[16,128,512]{2,1,0:T(8,128)(2,1)}, bf16[16,128,512]{2,1,0:T(8,128)(2,1)}, bf16[2048,512]{1,0:T(8,12...) custom-call(bf16[16,128,2048]{2,1,0:T(8,128)(2,1)} %get-tuple-element.70.h_ref, ...), custom_call_target="tpu_custom_call" | custom-call | flops 30000001024 | bytes 1048576 | tf_op jit(solution)/shard_map/pallas_call | solution.py:718
  367.8 75.4 %shard_map.208 = (bf16[1,1024,512]{2,1,0:T(8,128)(2,1)}, f32[128,2048]{1,0:T(8,128)}) custom-call(bf16[2,1024,512]{2,1,0:T(8,128)(2,1)} %bitcast.200, bf16[16,128,512]{2,1,0:T(8,128)(2,1)} %get-tuple-element.77.refs_1_, bf16[2048,512]{1,0:T(8,128)(2,1)} %pad_maximum_fusion.g_ref.refs_2_, bf16[16,128,512]{2,1,0:T(8,128)(2,1)} %get-tuple-element.78.refs_3_, ...), custom_call_target="tpu_custom_call" | custom-call | flops 30000001024 | bytes 1048576 | tf_op jit(solution)/shard_map/pallas_call | solution.py:418
  443.2 1.6 multiply_reduce_fusion
  444.9 1.2 fusion.29.refs_1_
  446.0 54.4 %shard_map.209 = (bf16[1,1024,512]{2,1,0:T(8,128)(2,1)}, bf16[16,128,2048]{2,1,0:T(8,128)(2,1)}) custom-call(bf16[2,1024,512]{2,1,0:T(8,128)(2,1)} %bitcast.202, bf16[128,2048]{1,0:T(8,128)(2,1)} %fusion.29.refs_1_), custom_call_target="tpu_custom_call" | custom-call | flops 30000001024 | bytes 1048576 | tf_op jit(solution)/shard_map/pallas_call | solution.py:418
  500.4 4.7 convolution_convert_fusion.1
  505.1 1.0 reshape.355
  506.1 1.3 reshape.358
  507.5 0.8 collective-permute-start.2
  508.3 2.6 collective-permute-start.3
  510.9 2.8 add_convert_fusion.1
  513.7 1.3 add_convert_fusion.2
  515.0 120.0 %shard_map.210 = (bf16[16,128,256]{2,1,0:T(8,128)(2,1)}, bf16[1,1024,512]{2,1,0:T(8,128)(2,1)}, bf16[2,2,2,2,64,512]{5,4,3,2,1,0:T(8,128)(2,1)}, bf16[2,2,2,2,64,512]{5,4,3,2,1,0:T(8,128)(2,1)}, f32[128,2048]{1,0:T(8,128)}) custom-call(bf16[16,128,2048]{2,1,0:T(8,128)(2,1)} %get-tuple-element.83.refs_0_, ...), custom_call_target="tpu_custom_call" | custom-call | flops 30000001024 | bytes 1048576 | tf_op jit(solution)/shard_map/pallas_call | solution.py:418
  635.0 1.5 convert_bitcast_fusion.1
  636.8 1.0 copy-done.15
  637.7 0.3 convert_bitcast_fusion
  638.4 1.0 copy-done.5
  639.6 2.7 broadcast_multiply_fusion
  642.7 0.8 slice.32
  643.6 0.5 add.159
  644.1 1.0 fusion.31
  645.1 0.9 convert_add_fusion
  645.9 5.9 convolution_convert_fusion
  651.8 1.3 fusion.30
  653.1 76.4 %shard_map.211 = (f32[128,2048]{1,0:T(8,128)}, bf16[2,2,2,2,64,128]{5,4,3,2,1,0:T(8,128)(2,1)}, bf16[2,2,2,2,64,128]{5,4,3,2,1,0:T(8,128)(2,1)}, bf16[2,2,2,2,64...) custom-call(bf16[16,128,256]{2,1,0:T(8,128)(2,1)} %get-tuple-element.94.re, ...), custom_call_target="tpu_custom_call" | custom-call | flops 30000001024 | bytes 1048576 | tf_op jit(solution)/shard_map/pallas_call | solution.py:418
  729.5 1.4 convert_bitcast_fusion.2
  730.9 1.5 copy.52
  732.5 0.8 fusion.32
  733.6 1.9 copy.41
  735.5 1.7 reshape.370
  737.2 2.1 bitcast_multiply_fusion.1
  739.3 1.5 fusion.7
  740.9 0.9 broadcast_multiply_fusion.2
  741.8 2.0 fusion.10
  743.8 0.5 add_add_fusion
  (117 shorter events, 3.7 us)
Async XLA Ops:
  0.6 5.1 copy-start
  1.4 6.3 copy-start.33
  5.8 1.9 copy-start.35
  7.7 58.1 %copy-start.39 = (bf16[64,2048]{1,0:T(8,128)(2,1)S(1)}, bf16[64,2048]{1,0:T(8,128)(2,1)}, u32[]{:S(2)}) copy-start(bf16[64,2048]{1,0:T(8,128)(2,1)} %param.17) | copy-start | bytes 786436
  7.7 62.0 %copy-start.32 = (s32[2,2048]{1,0:T(2,128)S(1)}, s32[2,2048]{1,0:T(2,128)}, u32[]{:S(2)}) copy-start(s32[2,2048]{1,0:T(2,128)} %param.22) | copy-start | bytes 49156
  7.7 63.2 %copy-start.40 = (bf16[64]{0:T(256)(128)(2,1)S(1)}, bf16[64]{0:T(256)(128)(2,1)}, u32[]{:S(2)}) copy-start(bf16[64]{0:T(256)(128)(2,1)} %param.18) | copy-start | bytes 388
  7.7 63.2 %copy-start.4 = (bf16[64,8192]{1,0:T(8,128)(2,1)S(1)}, bf16[64,8192]{1,0:T(8,128)(2,1)}, u32[]{:S(2)}) copy-start(bf16[64,8192]{1,0:T(8,128)(2,1)} %param.20) | copy-start | bytes 3145732
  7.7 63.2 %copy-start.6 = (bf16[64,8192]{1,0:T(8,128)(2,1)S(1)}, bf16[64,8192]{1,0:T(8,128)(2,1)}, u32[]{:S(2)}) copy-start(bf16[64,8192]{1,0:T(8,128)(2,1)} %param.19) | copy-start | bytes 3145732
  65.8 90.8 %collective-permute-start = (bf16[64,2048]{1,0:T(8,128)(2,1)S(1)}, bf16[64,2048]{1,0:T(8,128)(2,1)S(1)}, u32[]{:S(2)}, u32[]{:S(2)}) collective-permute-start(bf16[64,2048]{1,0:T(8,128)(2,1)S(1)} %copy-done.39), channel_id=1, source_target_pairs={{0,0},{1,16},{2,1},{3,17},{4,2},{5,18},{6,3},{7,19},{8,4},{9,20},{... | collective-permute-start | bytes 786440 | tf_op jit(solution)/shard_map/ppermute | solution.py:806
  66.5 90.1 %collective-permute-start.1 = (bf16[64,2048]{1,0:T(8,128)(2,1)S(1)}, bf16[64,2048]{1,0:T(8,128)(2,1)S(1)}, u32[]{:S(2)}, u32[]{:S(2)}) collective-permute-start(bf16[64,2048]{1,0:T(8,128)(2,1)S(1)} %copy-done.39), channel_id=1, source_target_pairs={{0,16},{1,0},{2,17},{3,1},{4,18},{5,2},{6,19},{7,3},{8,20},{9,4},{... | collective-permute-start | bytes 786440 | tf_op jit(solution)/shard_map/ppermute | solution.py:806
  70.9 0.6 copy-start.37
  71.5 2.2 copy-start.18
  73.7 4.2 copy-start.25
  73.7 4.2 copy-start.26
  73.7 4.2 copy-start.27
  73.7 4.2 copy-start.28
  217.1 1.6 copy-start.1
  219.6 102.6 %copy-start.13 = (bf16[2,2,2,2,64,512]{5,4,3,2,1,0:T(8,128)(2,1)S(1)}, bf16[2,2,2,2,64,512]{5,4,3,2,1,0:T(8,128)(2,1)}, u32[]{:S(2)}) copy-start(bf16[2,2,2,2,64,512]{5,4,3,2,1,0:T(8,128)(2,1)} %get-tuple-element.69) | copy-start | bytes 3145732
  322.3 1.5 copy-start.12
  322.3 1.8 copy-start.16
  324.1 1.2 copy-start.11
  324.1 1.5 copy-start.14
  443.2 1.7 copy-start.2
  443.2 1.7 copy-start.8
  446.0 54.4 %copy-start.10 = (bf16[16,128,128]{2,1,0:T(8,128)(2,1)S(1)}, bf16[16,128,128]{2,1,0:T(8,128)(2,1)}, u32[]{:S(2)}) copy-start(bf16[16,128,128]{2,1,0:T(8,128)(2,1)} %get-tuple-element.65.refs_1_.refs_4_) | copy-start | bytes 1572868
  507.4 6.3 copy-start.19
  507.4 6.3 copy-start.23
  507.5 137.6 %collective-permute-start.2 = (bf16[64,2048]{1,0:T(8,128)(2,1)S(1)}, bf16[64,2048]{1,0:T(8,128)(2,1)S(1)}, u32[]{:S(2)}, u32[]{:S(2)}) collective-permute-start(bf16[64,2048]{1,0:T(8,128)(2,1)S(1)} %get-tuple-element.125), channel_id=1, source_target_pairs={{0,0},{16,1},{1,2},{17,3},{2,4},{18,5},{3,6},{19,7},{4,8},{20,9},{... | collective-permute-start | bytes 786440 | tf_op jit(solution)/shard_map/ppermute | solution.py:858
  508.3 136.8 %collective-permute-start.3 = (bf16[64,2048]{1,0:T(8,128)(2,1)S(1)}, bf16[64,2048]{1,0:T(8,128)(2,1)S(1)}, u32[]{:S(2)}, u32[]{:S(2)}) collective-permute-start(bf16[64,2048]{1,0:T(8,128)(2,1)S(1)} %get-tuple-element.126), channel_id=1, source_target_pairs={{16,0},{0,1},{17,2},{1,3},{18,4},{2,5},{19,6},{3,7},{20,8},{4,9},{... | collective-permute-start | bytes 786440 | tf_op jit(solution)/shard_map/ppermute | solution.py:858
  636.5 1.2 copy-start.15
  638.1 1.2 copy-start.5
  638.1 1.5 copy-start.7
  638.1 1.5 copy-start.38
  639.6 2.7 copy-start.20
  639.6 2.7 copy-start.22
  642.7 3.2 copy-start.41
  730.9 1.5 copy-start.29
  732.4 4.8 copy-start.17
  732.4 4.8 copy-start.34
  732.5 6.9 copy-start.36
  733.6 8.2 %copy-start.9 = (bf16[2,64,2048]{2,1,0:T(8,128)(2,1)S(1)}, bf16[2,64,2048]{2,1,0:T(8,128)(2,1)}, u32[]{:S(2)}) copy-start(bf16[2,64,2048]{2,1,0:T(8,128)(2,1)} %param.23) | copy-start | bytes 1572868
  737.2 3.7 copy-start.24
  737.2 3.7 copy-start.30
  737.2 3.7 copy-start.31
  737.2 4.6 copy-start.3
  737.2 4.6 copy-start.21

commit v4 on v3

--- a/solution.py
+++ b/solution.py
@@ -89,8 +89,8 @@
 
 
 class Errand:
-    def __init__(self, array, own_block):
-        self.inputs, self.own_block = [(array, anywhere)], own_block
+    def __init__(self, array, own_block, turn=0):
+        self.inputs, self.own_block, self.turn = [(array, anywhere)], own_block, turn
 
     def outputs(self, groups):
         a = self.inputs[0][0]
@@ -101,6 +101,8 @@
         return [dma_sems(groups - 1), dma_sems(groups - 1)]
 
     def run(self, groups, src, dst, scratch):
+        for _ in range(self.turn):
+            yield
         copies = to_groups(
             groups, lambda k, peer: (src[0].at[peer] if self.own_block else src[0], dst[0].at[k - 1]), *scratch
         )
@@ -183,8 +185,8 @@
 
 
 class Gather:
-    def __init__(self, x, plan, patience=1):
-        self.inputs, self.plan, self.patience = [(x, vmem)], plan, patience
+    def __init__(self, x, plan, patience=1, turn=0):
+        self.inputs, self.plan, self.patience, self.turn = [(x, vmem)], plan, patience, turn
 
     def outputs(self, groups):
         x = self.inputs[0][0]
@@ -195,6 +197,8 @@
 
     def run(self, groups, src, dst, scratch):
         (x_ref,), (g_ref,), (ssem, rsem, lsem) = src, dst, scratch
+        for _ in range(self.turn):
+            yield
         me = coords()
         rows = x_ref.shape[0]
         plan = self.plan
@@ -374,6 +378,38 @@
             cp.wait_send()
 
 
+class Relay:
+    def __init__(self, scatter, extras, change, send, plan):
+        self.scatter, self.change, self.send = scatter, change, send
+        self.inputs = scatter.inputs + [(a, vmem) for a in extras]
+        self.shape = (scatter.rows, scatter.cols)
+        self.gather = Gather(jax.ShapeDtypeStruct(self.shape, jnp.bfloat16), plan)
+
+    def outputs(self, groups):
+        return self.scatter.outputs(groups) + self.gather.outputs(groups)
+
+    def scratch(self, groups):
+        own = [pltpu.VMEM(self.shape, jnp.bfloat16)]
+        return self.scatter.scratch(groups) + self.gather.scratch(groups) + own
+
+    def run(self, groups, src, dst, scratch):
+        n = len(self.scatter.inputs)
+        m = len(self.scatter.scratch(groups))
+        kept, gathered = dst
+        low = scratch[-1]
+        yield from self.scatter.run(groups, src[:n], (kept,), scratch[:m])
+
+        def rows(i, _):
+            here = pl.ds(pl.multiple_of(i * 16, 16), 16)
+            value = self.change(kept[here, :], *[a[here, :] for a in src[n:]])
+            kept[here, :] = value
+            low[here, :] = self.send(value).astype(low.dtype)
+            return 0
+
+        lax.fori_loop(0, self.shape[0] // 16, rows, 0)
+        yield from self.gather.run(groups, (low,), (gathered,), scratch[m:-1])
+
+
 def call(jobs, cid, body=None, inputs=(), outputs=(), scratch=()):
     groups = lax.axis_size("dp")
     jobs = list(jobs)
@@ -435,6 +471,7 @@
 NEG = -1e30
 CHUNK = 256
 SLOTS = 4
+GATHER_PLAN = Z_FIRST
 FFN_SLOTS = 4
 ORDER_A = ("c", "x", "y", "z")
 ORDER_B = ("c", "y", "z", "x")
@@ -740,6 +777,10 @@
     return scale * (grad - normed * jnp.mean(grad * normed, axis=-1, keepdims=True))
 
 
+def rms(values):
+    return lax.rsqrt(jnp.mean(values * values, axis=-1, keepdims=True) + epsilon)
+
+
 def after(x, *others):
     return lax.optimization_barrier((x,) + others)[0]
 
@@ -794,7 +835,7 @@
     )
     pack_kv = jnp.moveaxis(pack_kv, 1, 0)
     x = layer_input.reshape(rows, model).astype(f32)
-    norm_one = lax.rsqrt(jnp.mean(x * x, axis=-1, keepdims=True) + epsilon)
+    norm_one = rms(x)
     normed_one = x * norm_one
     c_own = cotangent.reshape(rows, model)
     _, (w_q, w_kv, (h_one,)) = call(
@@ -818,12 +859,13 @@
     )
     own_gate, own_up, own_down = [a[0].reshape(TEAM * share, ff) for a in own]
 
-    _, ((far_gate,), (branch,)) = call([Errand(own_gate, False), Scatter([(o, w_out)], False, EVEN)], 3)
-    middle = x + branch
-    norm_two = lax.rsqrt(jnp.mean(middle * middle, axis=-1, keepdims=True) + epsilon)
-    normed_two = middle * norm_two
-    _, ((far_up,), (far_down,), (h_two,), (c_all,)) = call(
-        [Errand(own_up, False), Errand(own_down, False), Gather(normed_two.astype(bf16), Z_FIRST), Gather(c_own, Z_FIRST)], 4
+    _, ((far_gate,), (far_up,), (far_down,), (middle, h_two), (c_all,)) = call(
+        [
+            Errand(own_gate, False), Errand(own_up, False, 10), Errand(own_down, False, 16),
+            Relay(Scatter([(o, w_out)], False, EVEN), [x], lambda total, x: x + total, lambda mid: mid * rms(mid), GATHER_PLAN),
+            Gather(c_own, GATHER_PLAN, 1, 12),
+        ],
+        3,
     )
     w_gate, w_up, w_down = in_order(own_gate, far_gate), in_order(own_up, far_up), in_order(own_down, far_down)
     active, d_gate, d_up, *g_ffn = ffn(h_two, c_all, w_gate, w_up, w_down)
@@ -844,11 +886,19 @@
     def home(piece):
         return jnp.moveaxis(piece[0].reshape(TEAM, share, -1).astype(f32), 0, 1)
 
-    _, ((far_gate,), (dn_two,)) = call(
-        [Errand(g_gate, True), Scatter([(d_gate, w_gate), (d_up, w_up)], True, EVEN)], 5
+    def back(total, c, mid):
+        scale = rms(mid)
+        return c.astype(f32) + norm_back(total, mid * scale, scale)
+
+    _, ((far_gate,), (far_up,), (middle_grad, middle_low)) = call(
+        [
+            Errand(g_gate, True), Errand(g_up, True, 10),
+            Relay(
+                Scatter([(d_gate, w_gate), (d_up, w_up)], True, EVEN), [c_own, middle], back, lambda grad: grad, GATHER_PLAN
+            ),
+        ],
+        5,
     )
-    middle_grad = c_own.astype(f32) + norm_back(dn_two, normed_two, norm_two)
-    _, ((far_up,), (middle_low,)) = call([Errand(g_up, True), Gather(middle_grad.astype(bf16), Z_FIRST)], 6)
     w_part, middle_low = lax.optimization_barrier((outer(o, middle_low), middle_low))
     w_part = w_part.reshape(groups, -1, model)
     pieces = []

time: 755 us -> 720 us (0.954)
  Pallas kernels: 661 us -> 638 us
    pallas_call x8 -> x6, Pallas kernels: 623 us -> 600 us  [call(): pl.pallas_call(kernel, out_shape=list(outputs) + [o for each in job_out f...]
  transfers between devices with their start and end apart: 4 -> 4, of which waited for: 0 -> 0; matrix products, arithmetic and copies ran while one was open for 3% -> 3% of each run, Pallas kernels for 26% -> 27%
where the time goes in v4:
time: 720 us; the launch traced here: 710 us
  Pallas kernels  638 us (89%)
  other arithmetic  37.6 us (5%)
  local copies, waits for them, and re-layouts  18 us (2%)
  matrix products  10.6 us (1%)
    pallas_call x6, Pallas kernels, call(): pl.pallas_call(kernel, out_shape=list(outputs) + [o for each in job_out f...  600 us
    pallas_call x1, Pallas kernels, ffn(): pl.pallas_call(ffn_kernel, grid=(team // FFN_SLOTS,), in_specs=[tall, tal...  37.6 us
  transfers between devices with their start and end apart: 4, of which 0 were waited for; matrix products, arithmetic and copies ran while one was open for 3% of the time, Pallas kernels for 27%

profile of v4, /device:TPU:0, one launch (start us, length us, event | category | flops | bytes accessed | tf_op | source)
XLA Modules:
  0.0 710.2 jit_solution(10406158917574578252)
XLA Ops:
  0.7 0.7 convert_element_type.160
  1.4 1.8 copy_bitcast_fusion.3
  3.2 1.0 fusion.9
  4.5 1.2 multiply_reduce_fusion.1
  5.8 1.0 multiply_convert_fusion.refs_2_
  6.8 0.9 pad_maximum_fusion.4
  7.7 58.0 %shard_map.203 = (bf16[2,2,2,2,64,128]{5,4,3,2,1,0:T(8,128)(2,1)}, bf16[1,2,2,2,2,64,128]{6,5,4,3,2,1,0:T(8,128)(2,1)}, bf16[2,2,2,2,64,128]{5,4,3,2,1,0:T(8,128...) custom-call(bf16[2,2,2,2,64,128]{5,4,3,2,1,0:T(8,128)(2,1)} %bitcast.180, ...), custom_call_target="tpu_custom_call" | custom-call | flops 30000001024 | bytes 1048576 | tf_op jit(solution)/shard_map/pallas_call | solution.py:454
  65.8 1.6 collective-permute-start.1
  67.4 0.7 collective-permute-start
  68.1 1.1 bitcast_convert_fusion.refs_5_
  69.2 0.6 broadcast_in_dim.52.refs_5_.refs_8_
  69.8 0.6 dynamic_slice.20.refs_4_.refs_9_
  70.5 0.5 fusion.2
  71.0 1.1 copy.61
  72.1 1.1 copy.60
  73.2 1.1 copy.59
  74.3 3.0 fusion.7
  77.5 1.1 maximum_maximum_fusion.refs_1_
  78.6 77.0 %shard_map.204 = (bf16[2,16,128,128]{3,2,1,0:T(8,128)(2,1)}, bf16[2,16,128,128]{3,2,1,0:T(8,128)(2,1)}, bf16[16,128,128]{2,1,0:T(8,128)(2,1)}, f32[8,1,512]{2,1,...) custom-call(bf16[16,128,2048]{2,1,0:T(8,128)(2,1)} %get-tuple-elemen, ...), custom_call_target="tpu_custom_call" | custom-call | flops 30000001024 | bytes 1048576 | tf_op jit(solution)/shard_map/pallas_call | solution.py:454
  155.8 0.6 gather_fusion
  156.4 0.9 bitcast_select_fusion.6.refs_4_.refs_1_
  157.4 160.6 %shard_map.205 = (bf16[1,1024,512]{2,1,0:T(8,128)(2,1)}, bf16[1,1024,512]{2,1,0:T(8,128)(2,1)}, bf16[1,1024,512]{2,1,0:T(8,128)(2,1)}, f32[128,2048]{1,0:T(8,128...) custom-call(bf16[1024,512]{1,0:T(8,128)(2,1)} %bitcast.156, bf16[1024,512]{1,0:T(8,128)(2,1)} %bitcast.155, ...), custom_call_target="tpu_custom_call" | custom-call | flops 30000001024 | bytes 1048576 | tf_op jit(solution)/shard_map/pallas_call | solution.py:454
  318.0 1.5 bitcast_select_fusion.5
  319.5 0.3 copy-done.15
  320.1 1.0 copy-done.9
  321.1 0.3 copy-done.14
  321.6 1.5 pad_maximum_fusion.g_ref.refs_3_
  323.1 1.5 pad_maximum_fusion.1.u_ref.refs_5_
  324.5 1.5 pad_maximum_fusion.2.d_ref.refs_14_
  326.0 37.6 %shard_map.206 = (bf16[16,128,512]{2,1,0:T(8,128)(2,1)}, bf16[16,128,512]{2,1,0:T(8,128)(2,1)}, bf16[16,128,512]{2,1,0:T(8,128)(2,1)}, bf16[2048,512]{1,0:T(8,12...) custom-call(bf16[16,128,2048]{2,1,0:T(8,128)(2,1)} %get-tuple-element.70.h_ref, ...), custom_call_target="tpu_custom_call" | custom-call | flops 30000001024 | bytes 1048576 | tf_op jit(solution)/shard_map/pallas_call | solution.py:755
  363.5 114.4 %shard_map.207 = (bf16[1,1024,512]{2,1,0:T(8,128)(2,1)}, bf16[1,1024,512]{2,1,0:T(8,128)(2,1)}, f32[128,2048]{1,0:T(8,128)}, bf16[16,128,2048]{2,1,0:T(8,128)(2,1)}) custom-call(bf16[2,1024,512]{2,1,0:T(8,128)(2,1)} %bitcast.171, bf16[2,1024,512]{2,1,0:T(8,128)(2,1)} %bitcast.169, bf16[16,128,512]{2,1,0:T(8,128)(2,1)} %get-tuple-element.77.refs_2_, ...), custom_call_target="tpu_custom_call" | custom-call | flops 30000001024 | bytes 1048576 | tf_op jit(solution)/shard_map/pallas_call | solution.py:454
  477.9 4.7 convolution_convert_fusion.1
  482.7 0.2 reshape.343
  483.0 2.6 add_convert_fusion.2
  485.6 1.3 add_convert_fusion.1
  486.9 0.2 reshape.346
  487.2 1.6 collective-permute-start.3
  488.8 0.7 collective-permute-start.2
  489.5 113.4 %shard_map.208 = (bf16[16,128,256]{2,1,0:T(8,128)(2,1)}, bf16[1,1024,512]{2,1,0:T(8,128)(2,1)}, bf16[2,2,2,2,64,512]{5,4,3,2,1,0:T(8,128)(2,1)}, bf16[2,2,2,2,64,512]{5,4,3,2,1,0:T(8,128)(2,1)}, f32[128,2048]{1,0:T(8,128)}) custom-call(bf16[16,128,2048]{2,1,0:T(8,128)(2,1)} %get-tuple-element.82.refs_0_, ...), custom_call_target="tpu_custom_call" | custom-call | flops 30000001024 | bytes 1048576 | tf_op jit(solution)/shard_map/pallas_call | solution.py:454
  602.9 1.5 convert_bitcast_fusion
  604.6 1.0 copy-done.13
  605.6 0.3 convert_bitcast_fusion.1
  606.2 1.0 copy-done.4
  607.2 0.3 copy-done.6
  607.5 2.9 broadcast_multiply_fusion
  610.4 0.3 add_convert_fusion
  610.7 0.9 copy-done.8
  611.6 0.3 copy-done.12
  612.0 1.1 add.138
  613.0 0.8 slice.32
  613.9 0.5 add.146
  614.4 1.0 fusion.21
  615.4 0.9 convert_add_fusion
  616.2 5.9 convolution_convert_fusion
  622.1 1.3 fusion.20
  623.4 76.7 %shard_map.209 = (f32[128,2048]{1,0:T(8,128)}, bf16[2,2,2,2,64,128]{5,4,3,2,1,0:T(8,128)(2,1)}, bf16[2,2,2,2,64,128]{5,4,3,2,1,0:T(8,128)(2,1)}, bf16[2,2,2,2,64...) custom-call(bf16[16,128,256]{2,1,0:T(8,128)(2,1)} %get-tuple-element.94.re, ...), custom_call_target="tpu_custom_call" | custom-call | flops 30000001024 | bytes 1048576 | tf_op jit(solution)/shard_map/pallas_call | solution.py:454
  700.1 1.5 multiply_reduce_fusion
  701.6 1.1 convert_reduce_fusion
  703.5 1.0 bitcast_multiply_fusion
  704.8 1.5 copy.52
  706.3 0.7 copy-done.21
  707.0 1.3 multiply_add_fusion
  708.4 0.9 broadcast_multiply_fusion.2
  709.3 0.5 add_add_fusion
  (115 shorter events, 2.8 us)
Async XLA Ops:
  0.6 5.1 copy-start
  1.4 2.8 copy-start.35
  5.8 1.9 copy-start.37
  7.7 58.1 %copy-start.41 = (bf16[64,2048]{1,0:T(8,128)(2,1)S(1)}, bf16[64,2048]{1,0:T(8,128)(2,1)}, u32[]{:S(2)}) copy-start(bf16[64,2048]{1,0:T(8,128)(2,1)} %param.17) | copy-start | bytes 786436
  7.7 61.5 %copy-start.34 = (s32[2,2048]{1,0:T(2,128)S(1)}, s32[2,2048]{1,0:T(2,128)}, u32[]{:S(2)}) copy-start(s32[2,2048]{1,0:T(2,128)} %param.22) | copy-start | bytes 49156
  7.7 62.7 %copy-start.42 = (bf16[64]{0:T(256)(128)(2,1)S(1)}, bf16[64]{0:T(256)(128)(2,1)}, u32[]{:S(2)}) copy-start(bf16[64]{0:T(256)(128)(2,1)} %param.18) | copy-start | bytes 388
  7.7 62.7 %copy-start.5 = (bf16[64,8192]{1,0:T(8,128)(2,1)S(1)}, bf16[64,8192]{1,0:T(8,128)(2,1)}, u32[]{:S(2)}) copy-start(bf16[64,8192]{1,0:T(8,128)(2,1)} %param.19) | copy-start | bytes 3145732
  65.8 4.7 copy-start.3
  65.8 90.0 %collective-permute-start.1 = (bf16[64,2048]{1,0:T(8,128)(2,1)S(1)}, bf16[64,2048]{1,0:T(8,128)(2,1)S(1)}, u32[]{:S(2)}, u32[]{:S(2)}) collective-permute-start(bf16[64,2048]{1,0:T(8,128)(2,1)S(1)} %copy-done.41), channel_id=1, source_target_pairs={{0,16},{1,0},{2,17},{3,1},{4,18},{5,2},{6,19},{7,3},{8,20},{9,4},{... | collective-permute-start | bytes 786440 | tf_op jit(solution)/shard_map/ppermute | solution.py:847
  67.4 88.4 %collective-permute-start = (bf16[64,2048]{1,0:T(8,128)(2,1)S(1)}, bf16[64,2048]{1,0:T(8,128)(2,1)S(1)}, u32[]{:S(2)}, u32[]{:S(2)}) collective-permute-start(bf16[64,2048]{1,0:T(8,128)(2,1)S(1)} %copy-done.41), channel_id=1, source_target_pairs={{0,0},{1,16},{2,1},{3,17},{4,2},{5,18},{6,3},{7,19},{8,4},{9,20},{... | collective-permute-start | bytes 786440 | tf_op jit(solution)/shard_map/ppermute | solution.py:847
  70.5 0.5 copy-start.39
  71.0 2.2 copy-start.17
  73.2 4.2 copy-start.25
  73.2 4.2 copy-start.26
  73.2 4.2 copy-start.27
  73.2 4.2 copy-start.28
  157.4 160.6 %copy-start.11 = (bf16[2,2,2,2,64,512]{5,4,3,2,1,0:T(8,128)(2,1)S(1)}, bf16[2,2,2,2,64,512]{5,4,3,2,1,0:T(8,128)(2,1)}, u32[]{:S(2)}) copy-start(bf16[2,2,2,2,64,512]{5,4,3,2,1,0:T(8,128)(2,1)} %get-tuple-element.64) | copy-start | bytes 3145732
  318.0 1.5 copy-start.10
  318.0 1.8 copy-start.15
  319.9 1.2 copy-start.9
  319.9 1.5 copy-start.14
  363.5 114.4 %copy-start.7 = (bf16[16,128,128]{2,1,0:T(8,128)(2,1)S(1)}, bf16[16,128,128]{2,1,0:T(8,128)(2,1)}, u32[]{:S(2)}) copy-start(bf16[16,128,128]{2,1,0:T(8,128)(2,1)} %get-tuple-element.67.refs_3_.refs_4_) | copy-start | bytes 1572868
  477.9 5.0 copy-start.20
  482.7 2.9 copy-start.19
  483.0 2.7 copy-start.23
  487.2 128.2 %collective-permute-start.3 = (bf16[64,2048]{1,0:T(8,128)(2,1)S(1)}, bf16[64,2048]{1,0:T(8,128)(2,1)S(1)}, u32[]{:S(2)}, u32[]{:S(2)}) collective-permute-start(bf16[64,2048]{1,0:T(8,128)(2,1)S(1)} %get-tuple-element.124), channel_id=1, source_target_pairs={{16,0},{0,1},{17,2},{1,3},{18,4},{2,5},{19,6},{3,7},{20,8},{4,9},{... | collective-permute-start | bytes 786440 | tf_op jit(solution)/shard_map/ppermute | solution.py:908
  488.8 126.6 %collective-permute-start.2 = (bf16[64,2048]{1,0:T(8,128)(2,1)S(1)}, bf16[64,2048]{1,0:T(8,128)(2,1)S(1)}, u32[]{:S(2)}, u32[]{:S(2)}) collective-permute-start(bf16[64,2048]{1,0:T(8,128)(2,1)S(1)} %get-tuple-element.123), channel_id=1, source_target_pairs={{0,0},{16,1},{1,2},{17,3},{2,4},{18,5},{3,6},{19,7},{4,8},{20,9},{... | collective-permute-start | bytes 786440 | tf_op jit(solution)/shard_map/ppermute | solution.py:908
  604.4 1.2 copy-start.13
  606.0 1.2 copy-start.4
  606.0 1.5 copy-start.6
  606.0 1.5 copy-start.40
  607.5 2.9 copy-start.18
  607.5 2.9 copy-start.22
  610.4 1.2 copy-start.8
  610.4 1.5 copy-start.12
  613.0 3.2 copy-start.43
  623.4 76.7 %copy-start.1 = (bf16[2,64,2048]{2,1,0:T(8,128)(2,1)S(1)}, bf16[2,64,2048]{2,1,0:T(8,128)(2,1)}, u32[]{:S(2)}) copy-start(bf16[2,64,2048]{2,1,0:T(8,128)(2,1)} %param.12) | copy-start | bytes 1572868
  623.4 76.7 %copy-start.38 = (f32[128]{0:T(128)S(1)}, f32[128]{0:T(128)}, u32[]{:S(2)}) copy-start(f32[128]{0:T(128)} %copy-done.37) | copy-start | bytes 1540
  701.6 1.8 copy-start.16
  701.6 1.8 copy-start.31
  701.6 1.8 copy-start.36
  702.7 1.8 copy-start.24
  702.7 1.8 copy-start.29
  702.7 1.8 copy-start.30
  704.7 1.6 copy-start.2
  704.8 2.3 copy-start.21
  706.3 2.1 copy-start.32
  706.3 2.1 copy-start.33

commit v5 on v4

--- a/solution.py
+++ b/solution.py
@@ -527,47 +527,72 @@
             )
         )
         copies[-1].start()
-    for k in range(groups):
-        p = lax.rem(me + groups - k, groups)
-        if k > 0:
-            copies[k - 1].wait_recv()
+
+    def block(s, i, kv, kid, begin):
+        at = s * steps + i
+        q = q_ref[:, pl.ds(i * SLOTS, SLOTS), s * tokens : (s + 1) * tokens, :].reshape(heads * CHUNK, 128)
+        scores = lax.dot_general(q, kv, NT, preferred_element_type=jnp.float32)
+        if kid is not None:
+            qid = as_column(own_ref[s, :, pl.ds(i * CHUNK, CHUNK)])
+            scores = jnp.where(kid <= jnp.concatenate([qid] * heads, axis=0), scores, NEG)
+        peak = jnp.max(scores, axis=-1, keepdims=True)
+        if not begin:
+            old = top[at]
+            peak = jnp.maximum(old, peak)
+        weight = jnp.exp(scores - peak)
+        summed = jnp.sum(weight, axis=-1, keepdims=True)
+        mixed = jnp.dot(weight.astype(jnp.bfloat16), kv, preferred_element_type=jnp.float32)
+        if not begin:
+            factor = jnp.exp(old - peak)
+            summed = summed + total[at] * factor
+            mixed = mixed + acc[at] * factor
+        top[at] = peak
+        total[at] = summed
+        acc[at] = mixed
+
+    for s in range(2):
+        for i in range(steps):
+            n = min((i + 2) * CHUNK, span)
+            kv = kv_ref[me, : n // tokens, s * tokens : (s + 1) * tokens, :].reshape(n, 128)
+            block(s, i, kv, idr_ref[s, :, pl.ds(pl.multiple_of(me * span, 128), n)], True)
+            if i % 2 == 1:
+                tick()
+    for k in range(1, groups):
+        copies[k - 1].wait_recv()
         for s in range(2):
-            kv = kv_ref[p, :, s * tokens : (s + 1) * tokens, :].reshape(span, 128)
-            kid = idr_ref[s, :, pl.ds(pl.multiple_of(p * span, 128), span)]
-
-            def block(i, _, s=s, kv=kv, kid=kid, k=k):
-                at = s * steps + i
-                q = q_ref[:, pl.ds(i * SLOTS, SLOTS), s * tokens : (s + 1) * tokens, :].reshape(heads * CHUNK, 128)
-                qid = as_column(own_ref[s, :, pl.ds(pl.multiple_of(i * CHUNK, CHUNK), CHUNK)])
-                qid = jnp.concatenate([qid] * heads, axis=0)
-                scores = lax.dot_general(q, kv, NT, preferred_element_type=jnp.float32)
-                scores = jnp.where(kid <= qid, scores, NEG)
-                peak = jnp.max(scores, axis=-1, keepdims=True)
-                if k > 0:
-                    old = top[at]
-                    peak = jnp.maximum(old, peak)
-                weight = jnp.exp(scores - peak)
-                summed = jnp.sum(weight, axis=-1, keepdims=True)
-                mixed = jnp.dot(weight.astype(jnp.bfloat16), kv, preferred_element_type=jnp.float32)
-                if k > 0:
-                    factor = jnp.exp(old - peak)
-                    summed = summed + total[at] * factor
-                    mixed = mixed + acc[at] * factor
-                if k < groups - 1:
-                    top[at] = peak
-                    total[at] = summed
-                    acc[at] = mixed
-                else:
-                    mixed = mixed / summed
-                    first, second = mixed[:CHUNK], mixed[CHUNK:]
-                    out = jnp.where(low_lanes(first.shape), pltpu.roll(first, HEAD_DIM, 1), second)
-                    o_ref[pl.ds(i * SLOTS, SLOTS), s * tokens : (s + 1) * tokens, :] = out.astype(jnp.bfloat16).reshape(SLOTS, tokens, 128)
-                    lse_ref[at] = as_row(peak + jnp.log(summed))
-                return 0
-
             for first in range(0, steps, 2):
-                lax.fori_loop(first, first + 2, block, 0)
+
+                @pl.when(me >= k)
+                def _(s=s, first=first, k=k):
+                    kv = kv_ref[me - k, :, s * tokens : (s + 1) * tokens, :].reshape(span, 128)
+
+                    def earlier(i, _):
+                        block(s, i, kv, None, False)
+                        return 0
+
+                    lax.fori_loop(first, first + 2, earlier, 0)
+
                 tick()
+            if k == groups - 1:
+
+                @pl.when(me < k)
+                def _(s=s):
+                    kv = kv_ref[me + 1, : CHUNK // tokens, s * tokens : (s + 1) * tokens, :].reshape(CHUNK, 128)
+                    kid = idr_ref[s, :, pl.ds(pl.multiple_of((me + 1) * span, 128), CHUNK)]
+                    block(s, steps - 1, kv, kid, False)
+
+    for s in range(2):
+
+        def finish(i, _, s=s):
+            at = s * steps + i
+            mixed = acc[at] / total[at]
+            first, second = mixed[:CHUNK], mixed[CHUNK:]
+            out = jnp.where(low_lanes(first.shape), pltpu.roll(first, HEAD_DIM, 1), second)
+            o_ref[pl.ds(i * SLOTS, SLOTS), s * tokens : (s + 1) * tokens, :] = out.astype(jnp.bfloat16).reshape(SLOTS, tokens, 128)
+            lse_ref[at] = as_row(top[at] + jnp.log(total[at]))
+            return 0
+
+        lax.fori_loop(0, steps, finish, 0)
     for cp in copies:
         cp.wait_send()
 
@@ -622,49 +647,66 @@
             return 0
 
         lax.fori_loop(0, steps, deltas, 0)
+    dq[...] = jnp.zeros_like(dq)
     copies = []
-    order = list(range(1, groups)) + [0]
-    for turn, k in enumerate(order):
-        p = lax.rem(me + k, groups)
+
+    def block(s, i, n, kv, kid):
+        at = s * steps + i
+        here = (slice(None), pl.ds(i * SLOTS, SLOTS), slice(s * tokens, (s + 1) * tokens), slice(None))
+        q = q_ref[here].reshape(2 * CHUNK, 128)
+        g = gz[here].reshape(2 * CHUNK, 128)
+        scores = lax.dot_general(kv, q, NT, preferred_element_type=f32)
+        prob = jnp.exp(scores - lse_ref[at])
+        if kid is not None:
+            qid = own_ref[s, :, pl.ds(i * CHUNK, CHUNK)]
+            prob = jnp.where(kid <= jnp.concatenate([qid] * 2, axis=1), prob, 0.0)
+        dp = lax.dot_general(kv, g, NT, preferred_element_type=f32)
+        ds = (prob * (dp - delta[at])).astype(bf16)
+        part = jnp.dot(ds, q, preferred_element_type=f32)
+        part = part + jnp.dot(prob.astype(bf16), g, preferred_element_type=f32)
+        dkv[s, :n, :] = dkv[s, :n, :] + part
+        dq[at] = dq[at] + lax.dot_general(ds, kv, TN, preferred_element_type=f32)
+
+    for k in range(1, groups):
         for s in range(2):
-            kv = kv_ref[p, :, s * tokens : (s + 1) * tokens, :].reshape(span, 128)
-            kid = as_column(all_ref[s, :, pl.ds(pl.multiple_of(p * span, span), span)])
-
-            def block(i, _, s=s, kv=kv, kid=kid, turn=turn):
-                at = s * steps + i
-                here = (slice(None), pl.ds(i * SLOTS, SLOTS), slice(s * tokens, (s + 1) * tokens), slice(None))
-                q = q_ref[here].reshape(2 * CHUNK, 128)
-                g = gz[here].reshape(2 * CHUNK, 128)
-                qid = own_ref[s, :, pl.ds(pl.multiple_of(i * CHUNK, CHUNK), CHUNK)]
-                qid = jnp.concatenate([qid] * 2, axis=1)
-                scores = lax.dot_general(kv, q, NT, preferred_element_type=f32)
-                prob = jnp.where(kid <= qid, jnp.exp(scores - lse_ref[at]), 0.0)
-                dp = lax.dot_general(kv, g, NT, preferred_element_type=f32)
-                ds = (prob * (dp - delta[at])).astype(bf16)
-                part = jnp.dot(ds, q, preferred_element_type=f32)
-                part = part + jnp.dot(prob.astype(bf16), g, preferred_element_type=f32)
-                dkv[s] = dkv[s] + part
-                mine = lax.dot_general(ds, kv, TN, preferred_element_type=f32)
-                if turn == 0:
-                    dq[at] = mine
-                else:
-                    dq[at] = dq[at] + mine
-                return 0
-
             dkv[s] = jnp.zeros((span, 128), f32)
             for first in range(0, steps, 2):
-                lax.fori_loop(first, first + 2, block, 0)
+
+                @pl.when(me + k >= groups)
+                def _(s=s, first=first, k=k):
+                    kv = kv_ref[me + k - groups, :, s * tokens : (s + 1) * tokens, :].reshape(span, 128)
+
+                    def earlier(i, _):
+                        block(s, i, span, kv, None)
+                        return 0
+
+                    lax.fori_loop(first, first + 2, earlier, 0)
+
                 tick()
-            if k > 0:
-                out_buf[k - 1, :, s * tokens : (s + 1) * tokens, :] = dkv[s].astype(bf16).reshape(TEAM, tokens, 128)
-        if k > 0:
-            copies.append(
-                pltpu.make_async_remote_copy(
-                    src_ref=out_buf.at[k - 1], dst_ref=in_buf.at[k - 1], send_sem=ssem.at[k - 1], recv_sem=rsem.at[k - 1],
-                    device_id={"dp": p}, device_id_type=MESH,
-                )
+            if k == 1:
+
+                @pl.when(me + 1 < groups)
+                def _(s=s):
+                    kv = kv_ref[me + 1, : CHUNK // tokens, s * tokens : (s + 1) * tokens, :].reshape(CHUNK, 128)
+                    kid = as_column(all_ref[s, :, pl.ds(pl.multiple_of((me + 1) * span, 128), CHUNK)])
+                    block(s, steps - 1, CHUNK, kv, kid)
+
+            out_buf[k - 1, :, s * tokens : (s + 1) * tokens, :] = dkv[s].astype(bf16).reshape(TEAM, tokens, 128)
+        copies.append(
+            pltpu.make_async_remote_copy(
+                src_ref=out_buf.at[k - 1], dst_ref=in_buf.at[k - 1], send_sem=ssem.at[k - 1], recv_sem=rsem.at[k - 1],
+                device_id={"dp": lax.rem(me + k, groups)}, device_id_type=MESH,
             )
-            copies[-1].start()
+        )
+        copies[-1].start()
+    for s in range(2):
+        dkv[s] = jnp.zeros((span, 128), f32)
+        kid = as_column(all_ref[s, :, pl.ds(pl.multiple_of(me * span, 128), span)])
+        for i in range(steps):
+            n = min((i + 2) * CHUNK, span)
+            block(s, i, n, kv_ref[me, : n // tokens, s * tokens : (s + 1) * tokens, :].reshape(n, 128), kid[:n])
+            if i % 2 == 1:
+                tick()
     for cp in copies:
         cp.wait_recv()
     for s in range(2):
@@ -855,7 +897,7 @@
     packs = (by_member(scaled(gate_weight, gain_two)), by_member(scaled(up_weight, gain_two)), by_member(down_weight))
     (q, kv, o, lse), own = attend(
         groups, h_one, w_in, cos, sin, ids, all_ids, 2,
-        [Swap(a, order, patience=2) for a, order in zip(packs, (ORDER_A, ORDER_B, ORDER_C))],
+        [Swap(a, order, patience=3) for a, order in zip(packs, (ORDER_A, ORDER_B, ORDER_C))],
     )
     own_gate, own_up, own_down = [a[0].reshape(TEAM * share, ff) for a in own]
 
@@ -910,8 +952,8 @@
     (d_in,), ((far_down,), home_gate, home_up, (produced,)) = attend_back(
         groups, middle_low, w_out, q, kv, o, lse, cos, sin, all_ids, ids, 7,
         [
-            Errand(g_down, True), Swap(total(g_gate, far_gate), ORDER_A, patience=2),
-            Swap(total(g_up, far_up), ORDER_B, patience=2), Scatter([(active, w_down)], True, Z_LAST),
+            Errand(g_down, True), Swap(total(g_gate, far_gate), ORDER_A, patience=3),
+            Swap(total(g_up, far_up), ORDER_B, patience=3), Scatter([(active, w_down)], True, Z_LAST),
         ],
     )
     layer_output = (middle + produced).reshape(seqs, tokens, model)
@@ -919,10 +961,10 @@
     attn = outer(h_one, d_in).reshape(groups, TEAM, share, -1)
     sum_down = total(g_down, far_down)
     thirds = (sum_down[..., : ff // 4], sum_down[..., ff // 4 : ff // 2], sum_down[..., ff // 2 :])
-    _, ((dn_one,), home_a, home_b, home_c, home_q, home_kv) = call(
+    _, (home_q, home_kv, (dn_one,), home_a, home_b, home_c) = call(
         [
-            Scatter([(d_in, w_in)], True, EVEN), *[Swap(a, o) for a, o in zip(thirds, (ORDER_A, ORDER_B, ORDER_C))],
-            Swap(attn[..., :cut], ORDER_A, reduce=6), Swap(attn[..., cut:], ORDER_B, reduce=6),
+            Swap(attn[..., :cut], ORDER_A, reduce=6), Swap(attn[..., cut:], ORDER_B, reduce=6), Scatter([(d_in, w_in)], True, EVEN),
+            *[Swap(a, o, patience=3) for a, o in zip(thirds, (ORDER_A, ORDER_B, ORDER_C))],
         ],
         8,
     )

time: 720 us -> 693 us (0.963)
  Pallas kernels: 638 us -> 612 us
    pallas_call x6, Pallas kernels: 600 us -> 575 us  [call(): pl.pallas_call(kernel, out_shape=list(outputs) + [o for each in job_out f...]
  transfers between devices with their start and end apart: 4 -> 4, of which waited for: 0 -> 0; matrix products, arithmetic and copies ran while one was open for 3% -> 3% of each run, Pallas kernels for 27% -> 26%
where the time goes in v5:
time: 693 us; the launch traced here: 684 us
  Pallas kernels  612 us (88%)
  other arithmetic  37.6 us (5%)
  local copies, waits for them, and re-layouts  18 us (3%)
  matrix products  10.6 us (2%)
    pallas_call x6, Pallas kernels, call(): pl.pallas_call(kernel, out_shape=list(outputs) + [o for each in job_out f...  575 us
    pallas_call x1, Pallas kernels, ffn(): pl.pallas_call(ffn_kernel, grid=(team // FFN_SLOTS,), in_specs=[tall, tal...  37.1 us
  transfers between devices with their start and end apart: 4, of which 0 were waited for; matrix products, arithmetic and copies ran while one was open for 3% of the time, Pallas kernels for 26%

profile of v5, /device:TPU:0, one launch (start us, length us, event | category | flops | bytes accessed | tf_op | source)
XLA Modules:
  0.0 684.5 jit_solution(13774139609649140410)
XLA Ops:
  0.7 0.7 convert_element_type.160
  1.4 1.8 copy_bitcast_fusion.3
  3.2 1.0 fusion.9
  4.5 1.2 multiply_reduce_fusion.1
  5.8 1.0 multiply_convert_fusion.refs_2_
  6.8 0.9 pad_maximum_fusion.4
  7.7 58.0 %shard_map.203 = (bf16[2,2,2,2,64,128]{5,4,3,2,1,0:T(8,128)(2,1)}, bf16[1,2,2,2,2,64,128]{6,5,4,3,2,1,0:T(8,128)(2,1)}, bf16[2,2,2,2,64,128]{5,4,3,2,1,0:T(8,128...) custom-call(bf16[2,2,2,2,64,128]{5,4,3,2,1,0:T(8,128)(2,1)} %bitcast.180, ...), custom_call_target="tpu_custom_call" | custom-call | flops 30000001024 | bytes 1048576 | tf_op jit(solution)/shard_map/pallas_call | solution.py:454
  65.8 1.6 collective-permute-start.1
  67.4 0.7 collective-permute-start
  68.1 1.1 bitcast_convert_fusion.refs_5_
  69.2 0.6 broadcast_in_dim.52.refs_5_.refs_8_
  69.8 0.6 dynamic_slice.20.refs_4_.refs_9_
  70.5 0.5 fusion.2
  71.0 1.1 copy.61
  72.1 1.1 copy.60
  73.2 1.1 copy.59
  74.3 3.0 fusion.7
  77.5 1.1 maximum_maximum_fusion.refs_1_.refs_3_
  78.6 67.8 %shard_map.204 = (bf16[2,16,128,128]{3,2,1,0:T(8,128)(2,1)}, bf16[2,16,128,128]{3,2,1,0:T(8,128)(2,1)}, bf16[16,128,128]{2,1,0:T(8,128)(2,1)}, f32[8,1,512]{2,1,...) custom-call(bf16[16,128,2048]{2,1,0:T(8,128)(2,1)} %get-tuple-elemen, ...), custom_call_target="tpu_custom_call" | custom-call | flops 30000001024 | bytes 1048576 | tf_op jit(solution)/shard_map/pallas_call | solution.py:454
  146.7 0.6 gather_fusion
  147.3 0.9 bitcast_select_fusion.6.refs_4_.refs_1_
  148.2 160.6 %shard_map.205 = (bf16[1,1024,512]{2,1,0:T(8,128)(2,1)}, bf16[1,1024,512]{2,1,0:T(8,128)(2,1)}, bf16[1,1024,512]{2,1,0:T(8,128)(2,1)}, f32[128,2048]{1,0:T(8,128...) custom-call(bf16[1024,512]{1,0:T(8,128)(2,1)} %bitcast.156, bf16[1024,512]{1,0:T(8,128)(2,1)} %bitcast.155, ...), custom_call_target="tpu_custom_call" | custom-call | flops 30000001024 | bytes 1048576 | tf_op jit(solution)/shard_map/pallas_call | solution.py:454
  308.9 1.5 bitcast_select_fusion.5
  310.4 0.3 copy-done.15
  310.9 1.0 copy-done.9
  312.0 0.3 copy-done.14
  312.5 1.5 pad_maximum_fusion.g_ref.refs_3_
  313.9 1.5 pad_maximum_fusion.1.u_ref.refs_5_
  315.4 1.5 pad_maximum_fusion.2.d_ref.refs_14_
  316.8 37.1 %shard_map.206 = (bf16[16,128,512]{2,1,0:T(8,128)(2,1)}, bf16[16,128,512]{2,1,0:T(8,128)(2,1)}, bf16[16,128,512]{2,1,0:T(8,128)(2,1)}, bf16[2048,512]{1,0:T(8,12...) custom-call(bf16[16,128,2048]{2,1,0:T(8,128)(2,1)} %get-tuple-element.70.h_ref, ...), custom_call_target="tpu_custom_call" | custom-call | flops 30000001024 | bytes 1048576 | tf_op jit(solution)/shard_map/pallas_call | solution.py:797
  354.0 114.6 %shard_map.207 = (bf16[1,1024,512]{2,1,0:T(8,128)(2,1)}, bf16[1,1024,512]{2,1,0:T(8,128)(2,1)}, f32[128,2048]{1,0:T(8,128)}, bf16[16,128,2048]{2,1,0:T(8,128)(2,1)}) custom-call(bf16[2,1024,512]{2,1,0:T(8,128)(2,1)} %bitcast.171, bf16[2,1024,512]{2,1,0:T(8,128)(2,1)} %bitcast.169, bf16[16,128,512]{2,1,0:T(8,128)(2,1)} %get-tuple-element.77.refs_2_, ...), custom_call_target="tpu_custom_call" | custom-call | flops 30000001024 | bytes 1048576 | tf_op jit(solution)/shard_map/pallas_call | solution.py:454
  468.6 4.7 convolution_convert_fusion.1
  473.4 0.2 reshape.343
  473.7 2.6 add_convert_fusion.2
  476.3 1.3 add_convert_fusion.1
  477.6 0.2 reshape.347
  477.9 1.4 collective-permute-start.3
  479.2 0.7 collective-permute-start.2
  479.9 108.5 %shard_map.208 = (bf16[16,128,256]{2,1,0:T(8,128)(2,1)}, bf16[1,1024,512]{2,1,0:T(8,128)(2,1)}, bf16[2,2,2,2,64,512]{5,4,3,2,1,0:T(8,128)(2,1)}, bf16[2,2,2,2,64,512]{5,4,3,2,1,0:T(8,128)(2,1)}, f32[128,2048]{1,0:T(8,128)}) custom-call(bf16[16,128,2048]{2,1,0:T(8,128)(2,1)} %get-tuple-element.82.refs_0_, ...), custom_call_target="tpu_custom_call" | custom-call | flops 30000001024 | bytes 1048576 | tf_op jit(solution)/shard_map/pallas_call | solution.py:454
  588.4 1.5 convert_bitcast_fusion
  590.1 1.0 copy-done.13
  591.1 0.3 convert_bitcast_fusion.1
  591.7 1.0 copy-done.4
  592.7 0.3 copy-done.6
  593.0 2.9 broadcast_multiply_fusion
  595.9 0.3 add_convert_fusion
  596.2 0.9 copy-done.8
  597.1 0.3 copy-done.12
  597.5 1.1 add.138
  598.5 0.9 slice.34
  599.4 0.5 add.146
  599.9 0.9 fusion.20
  600.9 0.9 convert_add_fusion
  601.7 5.9 convolution_convert_fusion
  607.6 1.3 fusion.21
  608.9 65.6 %shard_map.209 = (bf16[2,2,2,2,64,128]{5,4,3,2,1,0:T(8,128)(2,1)}, bf16[2,2,2,2,64,128]{5,4,3,2,1,0:T(8,128)(2,1)}, f32[128,2048]{1,0:T(8,128)}, bf16[2,2,2,2,64...) custom-call(bf16[2,2,2,2,2,64,128]{6,5,4,3,2,1,0:T(8,128)(2,1)} %bitcast.1, ...), custom_call_target="tpu_custom_call" | custom-call | flops 30000001024 | bytes 1048576 | tf_op jit(solution)/shard_map/pallas_call | solution.py:454
  674.6 1.5 multiply_reduce_fusion
  676.1 1.1 convert_reduce_fusion
  677.9 1.0 bitcast_multiply_fusion
  679.2 1.5 copy.52
  680.8 0.7 copy-done.21
  681.5 1.3 multiply_add_fusion
  682.8 0.9 broadcast_multiply_fusion.2
  683.7 0.5 add_add_fusion
  (115 shorter events, 2.8 us)
Async XLA Ops:
  0.6 5.1 copy-start
  1.4 2.8 copy-start.35
  5.8 1.9 copy-start.37
  7.7 58.1 %copy-start.41 = (bf16[64,2048]{1,0:T(8,128)(2,1)S(1)}, bf16[64,2048]{1,0:T(8,128)(2,1)}, u32[]{:S(2)}) copy-start(bf16[64,2048]{1,0:T(8,128)(2,1)} %param.17) | copy-start | bytes 786436
  7.7 61.5 %copy-start.34 = (s32[2,2048]{1,0:T(2,128)S(1)}, s32[2,2048]{1,0:T(2,128)}, u32[]{:S(2)}) copy-start(s32[2,2048]{1,0:T(2,128)} %param.22) | copy-start | bytes 49156
  7.7 62.7 %copy-start.42 = (bf16[64]{0:T(256)(128)(2,1)S(1)}, bf16[64]{0:T(256)(128)(2,1)}, u32[]{:S(2)}) copy-start(bf16[64]{0:T(256)(128)(2,1)} %param.18) | copy-start | bytes 388
  7.7 62.7 %copy-start.5 = (bf16[64,8192]{1,0:T(8,128)(2,1)S(1)}, bf16[64,8192]{1,0:T(8,128)(2,1)}, u32[]{:S(2)}) copy-start(bf16[64,8192]{1,0:T(8,128)(2,1)} %param.19) | copy-start | bytes 3145732
  65.8 4.7 copy-start.3
  65.8 80.8 %collective-permute-start.1 = (bf16[64,2048]{1,0:T(8,128)(2,1)S(1)}, bf16[64,2048]{1,0:T(8,128)(2,1)S(1)}, u32[]{:S(2)}, u32[]{:S(2)}) collective-permute-start(bf16[64,2048]{1,0:T(8,128)(2,1)S(1)} %copy-done.41), channel_id=1, source_target_pairs={{0,16},{1,0},{2,17},{3,1},{4,18},{5,2},{6,19},{7,3},{8,20},{9,4},{... | collective-permute-start | bytes 786440 | tf_op jit(solution)/shard_map/ppermute | solution.py:889
  67.4 79.2 %collective-permute-start = (bf16[64,2048]{1,0:T(8,128)(2,1)S(1)}, bf16[64,2048]{1,0:T(8,128)(2,1)S(1)}, u32[]{:S(2)}, u32[]{:S(2)}) collective-permute-start(bf16[64,2048]{1,0:T(8,128)(2,1)S(1)} %copy-done.41), channel_id=1, source_target_pairs={{0,0},{1,16},{2,1},{3,17},{4,2},{5,18},{6,3},{7,19},{8,4},{9,20},{... | collective-permute-start | bytes 786440 | tf_op jit(solution)/shard_map/ppermute | solution.py:889
  70.5 0.5 copy-start.39
  71.0 2.2 copy-start.17
  73.2 4.2 copy-start.25
  73.2 4.2 copy-start.26
  73.2 4.2 copy-start.27
  73.2 4.2 copy-start.28
  148.2 160.6 %copy-start.11 = (bf16[2,2,2,2,64,512]{5,4,3,2,1,0:T(8,128)(2,1)S(1)}, bf16[2,2,2,2,64,512]{5,4,3,2,1,0:T(8,128)(2,1)}, u32[]{:S(2)}) copy-start(bf16[2,2,2,2,64,512]{5,4,3,2,1,0:T(8,128)(2,1)} %get-tuple-element.64) | copy-start | bytes 3145732
  308.9 1.5 copy-start.10
  308.9 1.8 copy-start.15
  310.7 1.2 copy-start.9
  310.7 1.5 copy-start.14
  354.0 114.6 %copy-start.7 = (bf16[16,128,128]{2,1,0:T(8,128)(2,1)S(1)}, bf16[16,128,128]{2,1,0:T(8,128)(2,1)}, u32[]{:S(2)}) copy-start(bf16[16,128,128]{2,1,0:T(8,128)(2,1)} %get-tuple-element.67.refs_3_.refs_4_) | copy-start | bytes 1572868
  468.6 5.0 copy-start.20
  473.4 2.9 copy-start.19
  473.7 2.7 copy-start.23
  477.9 123.0 %collective-permute-start.3 = (bf16[64,2048]{1,0:T(8,128)(2,1)S(1)}, bf16[64,2048]{1,0:T(8,128)(2,1)S(1)}, u32[]{:S(2)}, u32[]{:S(2)}) collective-permute-start(bf16[64,2048]{1,0:T(8,128)(2,1)S(1)} %get-tuple-element.124), channel_id=1, source_target_pairs={{16,0},{0,1},{17,2},{1,3},{18,4},{2,5},{19,6},{3,7},{20,8},{4,9},{... | collective-permute-start | bytes 786440 | tf_op jit(solution)/shard_map/ppermute | solution.py:950
  479.2 121.6 %collective-permute-start.2 = (bf16[64,2048]{1,0:T(8,128)(2,1)S(1)}, bf16[64,2048]{1,0:T(8,128)(2,1)S(1)}, u32[]{:S(2)}, u32[]{:S(2)}) collective-permute-start(bf16[64,2048]{1,0:T(8,128)(2,1)S(1)} %get-tuple-element.123), channel_id=1, source_target_pairs={{0,0},{16,1},{1,2},{17,3},{2,4},{18,5},{3,6},{19,7},{4,8},{20,9},{... | collective-permute-start | bytes 786440 | tf_op jit(solution)/shard_map/ppermute | solution.py:950
  589.9 1.2 copy-start.13
  591.5 1.2 copy-start.4
  591.5 1.5 copy-start.6
  591.5 1.5 copy-start.40
  593.0 2.9 copy-start.18
  593.0 2.9 copy-start.22
  595.9 1.2 copy-start.8
  595.9 1.5 copy-start.12
  598.5 3.2 copy-start.43
  608.9 65.7 %copy-start.1 = (bf16[2,64,2048]{2,1,0:T(8,128)(2,1)S(1)}, bf16[2,64,2048]{2,1,0:T(8,128)(2,1)}, u32[]{:S(2)}) copy-start(bf16[2,64,2048]{2,1,0:T(8,128)(2,1)} %param.12) | copy-start | bytes 1572868
  608.9 65.7 %copy-start.38 = (f32[128]{0:T(128)S(1)}, f32[128]{0:T(128)}, u32[]{:S(2)}) copy-start(f32[128]{0:T(128)} %copy-done.37) | copy-start | bytes 1540
  676.1 1.8 copy-start.16
  676.1 1.8 copy-start.31
  676.1 1.8 copy-start.36
  677.2 1.8 copy-start.24
  677.2 1.8 copy-start.29
  677.2 1.8 copy-start.30
  679.2 1.6 copy-start.2
  679.2 2.3 copy-start.21
  680.7 2.1 copy-start.32
  680.7 2.1 copy-start.33

commit v6 on v5

--- a/solution.py
+++ b/solution.py
@@ -953,11 +953,10 @@
         groups, middle_low, w_out, q, kv, o, lse, cos, sin, all_ids, ids, 7,
         [
             Errand(g_down, True), Swap(total(g_gate, far_gate), ORDER_A, patience=3),
-            Swap(total(g_up, far_up), ORDER_B, patience=3), Scatter([(active, w_down)], True, Z_LAST),
+            Swap(total(g_up, far_up), ORDER_B, patience=3), Scatter([(active, w_down)], True, Z_LAST, 2),
         ],
     )
     layer_output = (middle + produced).reshape(seqs, tokens, model)
-    d_in, grad_output = lax.optimization_barrier((d_in, grad_output))
     attn = outer(h_one, d_in).reshape(groups, TEAM, share, -1)
     sum_down = total(g_down, far_down)
     thirds = (sum_down[..., : ff // 4], sum_down[..., ff // 4 : ff // 2], sum_down[..., ff // 2 :])

time: 693 us -> 689 us (level)
  transfers between devices with their start and end apart: 4 -> 4, of which waited for: 0 -> 0; matrix products, arithmetic and copies ran while one was open for 3% -> 3% of each run, Pallas kernels for 26% -> 10%
where the time goes in v6:
time: 689 us; the launch traced here: 678 us
  Pallas kernels  607 us (88%)
  other arithmetic  37.6 us (5%)
  local copies, waits for them, and re-layouts  17.3 us (3%)
  matrix products  10.7 us (2%)
    pallas_call x6, Pallas kernels, call(): pl.pallas_call(kernel, out_shape=list(outputs) + [o for each in job_out f...  570 us
    pallas_call x1, Pallas kernels, ffn(): pl.pallas_call(ffn_kernel, grid=(team // FFN_SLOTS,), in_specs=[tall, tal...  37.2 us
  transfers between devices with their start and end apart: 4, of which 0 were waited for; matrix products, arithmetic and copies ran while one was open for 3% of the time, Pallas kernels for 10%

profile of v6, /device:TPU:0, one launch (start us, length us, event | category | flops | bytes accessed | tf_op | source)
XLA Modules:
  0.0 677.9 jit_solution(16367618651393348017)
XLA Ops:
  0.7 0.7 convert_element_type.160
  1.4 1.8 copy_bitcast_fusion.3
  3.2 1.0 fusion.9
  4.5 1.2 multiply_reduce_fusion.1
  5.8 1.0 multiply_convert_fusion.refs_2_
  6.8 0.9 pad_maximum_fusion.4
  7.7 58.0 %shard_map.203 = (bf16[2,2,2,2,64,128]{5,4,3,2,1,0:T(8,128)(2,1)}, bf16[1,2,2,2,2,64,128]{6,5,4,3,2,1,0:T(8,128)(2,1)}, bf16[2,2,2,2,64,128]{5,4,3,2,1,0:T(8,128...) custom-call(bf16[2,2,2,2,64,128]{5,4,3,2,1,0:T(8,128)(2,1)} %bitcast.180, ...), custom_call_target="tpu_custom_call" | custom-call | flops 30000001024 | bytes 1048576 | tf_op jit(solution)/shard_map/pallas_call | solution.py:454
  65.8 1.6 collective-permute-start.1
  67.4 0.7 collective-permute-start
  68.1 1.1 bitcast_convert_fusion.refs_5_
  69.2 0.6 broadcast_in_dim.52.refs_5_.refs_8_
  69.8 0.6 dynamic_slice.20.refs_4_.refs_9_
  70.5 0.5 fusion.2
  71.0 1.1 copy.61
  72.1 1.1 copy.60
  73.2 1.1 copy.59
  74.3 3.0 fusion.7
  77.5 1.1 maximum_maximum_fusion.refs_1_.refs_3_
  78.6 67.8 %shard_map.204 = (bf16[2,16,128,128]{3,2,1,0:T(8,128)(2,1)}, bf16[2,16,128,128]{3,2,1,0:T(8,128)(2,1)}, bf16[16,128,128]{2,1,0:T(8,128)(2,1)}, f32[8,1,512]{2,1,...) custom-call(bf16[16,128,2048]{2,1,0:T(8,128)(2,1)} %get-tuple-elemen, ...), custom_call_target="tpu_custom_call" | custom-call | flops 30000001024 | bytes 1048576 | tf_op jit(solution)/shard_map/pallas_call | solution.py:454
  146.7 0.6 gather_fusion
  147.3 0.9 bitcast_select_fusion.6.refs_4_.refs_1_
  148.2 160.6 %shard_map.205 = (bf16[1,1024,512]{2,1,0:T(8,128)(2,1)}, bf16[1,1024,512]{2,1,0:T(8,128)(2,1)}, bf16[1,1024,512]{2,1,0:T(8,128)(2,1)}, f32[128,2048]{1,0:T(8,128...) custom-call(bf16[1024,512]{1,0:T(8,128)(2,1)} %bitcast.155, bf16[1024,512]{1,0:T(8,128)(2,1)} %bitcast.154, ...), custom_call_target="tpu_custom_call" | custom-call | flops 30000001024 | bytes 1048576 | tf_op jit(solution)/shard_map/pallas_call | solution.py:454
  308.9 1.5 bitcast_select_fusion.5
  310.4 0.3 copy-done.16
  310.9 1.0 copy-done.10
  311.9 0.3 copy-done.15
  312.5 1.5 pad_maximum_fusion.g_ref.refs_3_
  313.9 1.5 pad_maximum_fusion.1.u_ref.refs_5_
  315.4 1.5 pad_maximum_fusion.2.d_ref.refs_14_
  316.8 37.2 %shard_map.206 = (bf16[16,128,512]{2,1,0:T(8,128)(2,1)}, bf16[16,128,512]{2,1,0:T(8,128)(2,1)}, bf16[16,128,512]{2,1,0:T(8,128)(2,1)}, bf16[2048,512]{1,0:T(8,12...) custom-call(bf16[16,128,2048]{2,1,0:T(8,128)(2,1)} %get-tuple-element.68.h_ref, ...), custom_call_target="tpu_custom_call" | custom-call | flops 30000001024 | bytes 1048576 | tf_op jit(solution)/shard_map/pallas_call | solution.py:797
  354.0 114.6 %shard_map.207 = (bf16[1,1024,512]{2,1,0:T(8,128)(2,1)}, bf16[1,1024,512]{2,1,0:T(8,128)(2,1)}, f32[128,2048]{1,0:T(8,128)}, bf16[16,128,2048]{2,1,0:T(8,128)(2,1)}) custom-call(bf16[2,1024,512]{2,1,0:T(8,128)(2,1)} %bitcast.171, bf16[2,1024,512]{2,1,0:T(8,128)(2,1)} %bitcast.169, bf16[16,128,512]{2,1,0:T(8,128)(2,1)} %get-tuple-element.75.refs_2_, ...), custom_call_target="tpu_custom_call" | custom-call | flops 30000001024 | bytes 1048576 | tf_op jit(solution)/shard_map/pallas_call | solution.py:454
  468.6 4.7 convolution_convert_fusion.1
  473.4 0.2 reshape.343
  473.7 2.6 add_convert_fusion.2
  476.3 1.3 add_convert_fusion.1
  477.6 101.8 %shard_map.208 = (bf16[16,128,256]{2,1,0:T(8,128)(2,1)}, bf16[1,1024,512]{2,1,0:T(8,128)(2,1)}, bf16[2,2,2,2,64,512]{5,4,3,2,1,0:T(8,128)(2,1)}, bf16[2,2,2,2,64,512]{5,4,3,2,1,0:T(8,128)(2,1)}, f32[128,2048]{1,0:T(8,128)}) custom-call(bf16[16,128,2048]{2,1,0:T(8,128)(2,1)} %get-tuple-element.80.refs_0_, ...), custom_call_target="tpu_custom_call" | custom-call | flops 30000001024 | bytes 1048576 | tf_op jit(solution)/shard_map/pallas_call | solution.py:454
  579.4 1.6 add_convert_fusion
  581.0 0.9 fusion.20
  581.9 0.8 slice.34
  582.8 5.9 convolution_convert_fusion
  588.7 1.3 fusion.21
  589.9 67.1 %shard_map.209 = (bf16[2,2,2,2,64,128]{5,4,3,2,1,0:T(8,128)(2,1)}, bf16[2,2,2,2,64,128]{5,4,3,2,1,0:T(8,128)(2,1)}, f32[128,2048]{1,0:T(8,128)}, bf16[2,2,2,2,64...) custom-call(bf16[2,2,2,2,2,64,128]{6,5,4,3,2,1,0:T(8,128)(2,1)} %bitcast.1, ...), custom_call_target="tpu_custom_call" | custom-call | flops 30000001024 | bytes 1048576 | tf_op jit(solution)/shard_map/pallas_call | solution.py:454
  657.1 1.5 multiply_reduce_fusion
  658.6 1.1 convert_reduce_fusion
  660.4 1.0 bitcast_multiply_fusion
  661.7 0.7 collective-permute-start.3
  662.4 0.7 collective-permute-start.2
  663.1 0.3 convert_bitcast_fusion
  663.4 0.2 copy.51
  663.7 1.0 copy-done.12
  664.6 0.3 convert_bitcast_fusion.1
  665.0 0.2 copy.50
  665.3 0.9 copy-done.2
  666.2 0.3 copy-done.21
  666.5 1.3 multiply_add_fusion
  667.9 0.9 broadcast_multiply_fusion.2
  668.9 2.7 broadcast_multiply_fusion
  671.9 1.0 copy-done.8
  672.8 0.3 copy-done.9
  673.1 1.1 add.138
  674.2 1.5 copy.52
  675.8 0.5 add.146
  676.3 0.5 add_add_fusion
  676.8 0.9 convert_add_fusion
  (115 shorter events, 2.7 us)
Async XLA Ops:
  0.6 5.1 copy-start
  1.4 2.8 copy-start.35
  5.8 1.9 copy-start.37
  7.7 58.1 %copy-start.41 = (bf16[64,2048]{1,0:T(8,128)(2,1)S(1)}, bf16[64,2048]{1,0:T(8,128)(2,1)}, u32[]{:S(2)}) copy-start(bf16[64,2048]{1,0:T(8,128)(2,1)} %param.17) | copy-start | bytes 786436
  7.7 61.5 %copy-start.34 = (s32[2,2048]{1,0:T(2,128)S(1)}, s32[2,2048]{1,0:T(2,128)}, u32[]{:S(2)}) copy-start(s32[2,2048]{1,0:T(2,128)} %param.22) | copy-start | bytes 49156
  7.7 62.7 %copy-start.42 = (bf16[64]{0:T(256)(128)(2,1)S(1)}, bf16[64]{0:T(256)(128)(2,1)}, u32[]{:S(2)}) copy-start(bf16[64]{0:T(256)(128)(2,1)} %param.18) | copy-start | bytes 388
  7.7 62.7 %copy-start.5 = (bf16[64,8192]{1,0:T(8,128)(2,1)S(1)}, bf16[64,8192]{1,0:T(8,128)(2,1)}, u32[]{:S(2)}) copy-start(bf16[64,8192]{1,0:T(8,128)(2,1)} %param.19) | copy-start | bytes 3145732
  65.8 4.7 copy-start.3
  65.8 80.9 %collective-permute-start.1 = (bf16[64,2048]{1,0:T(8,128)(2,1)S(1)}, bf16[64,2048]{1,0:T(8,128)(2,1)S(1)}, u32[]{:S(2)}, u32[]{:S(2)}) collective-permute-start(bf16[64,2048]{1,0:T(8,128)(2,1)S(1)} %copy-done.41), channel_id=1, source_target_pairs={{0,16},{1,0},{2,17},{3,1},{4,18},{5,2},{6,19},{7,3},{8,20},{9,4},{... | collective-permute-start | bytes 786440 | tf_op jit(solution)/shard_map/ppermute | solution.py:889
  67.4 79.2 %collective-permute-start = (bf16[64,2048]{1,0:T(8,128)(2,1)S(1)}, bf16[64,2048]{1,0:T(8,128)(2,1)S(1)}, u32[]{:S(2)}, u32[]{:S(2)}) collective-permute-start(bf16[64,2048]{1,0:T(8,128)(2,1)S(1)} %copy-done.41), channel_id=1, source_target_pairs={{0,0},{1,16},{2,1},{3,17},{4,2},{5,18},{6,3},{7,19},{8,4},{9,20},{... | collective-permute-start | bytes 786440 | tf_op jit(solution)/shard_map/ppermute | solution.py:889
  70.5 0.5 copy-start.39
  71.0 2.2 copy-start.18
  73.2 4.2 copy-start.27
  73.2 4.2 copy-start.28
  73.2 4.2 copy-start.29
  73.2 4.2 copy-start.30
  148.2 160.6 %copy-start.13 = (bf16[2,2,2,2,64,512]{5,4,3,2,1,0:T(8,128)(2,1)S(1)}, bf16[2,2,2,2,64,512]{5,4,3,2,1,0:T(8,128)(2,1)}, u32[]{:S(2)}) copy-start(bf16[2,2,2,2,64,512]{5,4,3,2,1,0:T(8,128)(2,1)} %get-tuple-element.62) | copy-start | bytes 3145732
  308.9 1.5 copy-start.11
  308.9 1.8 copy-start.16
  310.7 1.2 copy-start.10
  310.7 1.5 copy-start.15
  354.0 114.6 %copy-start.7 = (bf16[16,128,128]{2,1,0:T(8,128)(2,1)S(1)}, bf16[16,128,128]{2,1,0:T(8,128)(2,1)}, u32[]{:S(2)}) copy-start(bf16[16,128,128]{2,1,0:T(8,128)(2,1)} %get-tuple-element.65.refs_3_.refs_4_) | copy-start | bytes 1572868
  468.6 5.0 copy-start.20
  473.4 2.9 copy-start.19
  473.6 2.7 copy-start.23
  477.6 101.8 %copy-start.22 = (bf16[2048,512]{1,0:T(8,128)(2,1)S(1)}, bf16[2048,512]{1,0:T(8,128)(2,1)}, u32[]{:S(2)}) copy-start(bf16[2048,512]{1,0:T(8,128)(2,1)} %get-tuple-element.84) | copy-start | bytes 6291460
  579.4 3.4 copy-start.43
  589.9 67.1 %copy-start.1 = (bf16[2,64,2048]{2,1,0:T(8,128)(2,1)S(1)}, bf16[2,64,2048]{2,1,0:T(8,128)(2,1)}, u32[]{:S(2)}) copy-start(bf16[2,64,2048]{2,1,0:T(8,128)(2,1)} %param.12) | copy-start | bytes 1572868
  589.9 67.1 %copy-start.38 = (f32[128]{0:T(128)S(1)}, f32[128]{0:T(128)}, u32[]{:S(2)}) copy-start(f32[128]{0:T(128)} %copy-done.37) | copy-start | bytes 1540
  658.6 1.8 copy-start.17
  658.6 1.8 copy-start.31
  658.6 1.8 copy-start.36
  660.1 3.0 copy-start.14
  661.7 15.1 %collective-permute-start.3 = (bf16[64,2048]{1,0:T(8,128)(2,1)S(1)}, bf16[64,2048]{1,0:T(8,128)(2,1)S(1)}, u32[]{:S(2)}, u32[]{:S(2)}) collective-permute-start(bf16[64,2048]{1,0:T(8,128)(2,1)S(1)} %get-tuple-element.118), channel_id=1, source_target_pairs={{16,0},{0,1},{17,2},{1,3},{18,4},{2,5},{19,6},{3,7},{20,8},{4,9},{... | collective-permute-start | bytes 786440 | tf_op jit(solution)/shard_map/ppermute | solution.py:950
  662.4 14.4 %collective-permute-start.2 = (bf16[64,2048]{1,0:T(8,128)(2,1)S(1)}, bf16[64,2048]{1,0:T(8,128)(2,1)S(1)}, u32[]{:S(2)}, u32[]{:S(2)}) collective-permute-start(bf16[64,2048]{1,0:T(8,128)(2,1)S(1)} %get-tuple-element.117), channel_id=1, source_target_pairs={{0,0},{16,1},{1,2},{17,3},{2,4},{18,5},{3,6},{19,7},{4,8},{20,9},{... | collective-permute-start | bytes 786440 | tf_op jit(solution)/shard_map/ppermute | solution.py:950
  663.4 1.2 copy-start.12
  665.0 1.2 copy-start.2
  665.0 1.5 copy-start.21
  665.3 2.6 copy-start.32
  665.3 2.6 copy-start.33
  666.5 2.3 copy-start.4
  666.5 2.3 copy-start.6
  666.5 2.3 copy-start.40
  668.8 2.8 copy-start.24
  668.8 2.8 copy-start.25
  668.8 2.8 copy-start.26
  671.6 1.2 copy-start.8
  671.6 1.5 copy-start.9
